TPU v7x, 32 devices: a whole 2x2x4 slice. The times are simulated.
32 devices in a mesh: latent: 4 (over z), row: 2 (over x), col: 4 (over y, core).
Axes of the slice: x: 2, y: 2, z: 4, core: 2. Of those that a mesh axis runs over, the one named last changes fastest.
Arguments:
- observations: bfloat16 [128, 64, 2048], P('col', 'latent', 'row'), may hold values from -6 to 6
- rotation: float32 [64, 4], replicated, may hold values from -0.75 to 0.75
- ordering: int32 [2048], P('row'), may hold values from 0 to 2047, as said below
- working: bfloat16 [4, 2048, 2048], P('latent', 'row', 'col'), as said below
- factor_inverse: bfloat16 [4, 2, 512, 512], P('latent'), as said below
- panel_index: int32 [2], replicated, may hold values from 0 to 3
Outputs:
- trailing: float32 [4, 2048, 2048], P('latent', 'row', 'col')
- panels: bfloat16 [4, 2, 2048, 512], P('latent', None, 'row', 'col')
- whitened: float32 [4, 128, 2048], P('latent', 'col', 'row')
Inputs may be any that keep to these rules, and one draw needn't show every extreme that they name: `ordering`: a permutation of the stations that maps each block of 1024 consecutive positions onto the same block. `working`: symmetric in its last two dimensions. `factor_inverse`: lower triangular in its last two dimensions, with a positive diagonal.
All inputs are finite; a program needn't handle non-finite values.
Results may differ from a plain program's by a relative error of at most 0.0047.
Values may be sent and summed in bfloat16 or wider, within the bound.
No kernel may reach another device: no remote copies, remote signals or barrier semaphores. Data moves between devices by JAX's collectives and lax.ppermute only.
A program may use at most 64 MiB of HBM per device.

v0:
```python
import jax
import jax.numpy as jnp
from jax import lax
from jax.sharding import PartitionSpec as P

PANELS = 2


def spread(value, axis, source):
    kept = jnp.where(lax.axis_index(axis) == source, value, 0).astype(value.dtype)
    return lax.psum(kept, axis)


def local(observations, rotation, ordering, working, factor_inverse, panel_index):
    row_tile = working.shape[1]
    col_tile = working.shape[2]
    width = factor_inverse.shape[2]
    col_count = lax.axis_size("col")
    share = width // col_count
    row_place = lax.axis_index("row")
    col_place = lax.axis_index("col")
    var_count = observations.shape[1]
    own_rows = lax.dynamic_slice_in_dim(
        rotation, lax.axis_index("latent") * var_count, var_count, 0
    )
    terms = jnp.einsum(
        "tvs,vl->lts", observations.astype(jnp.float32), own_rows, precision=lax.Precision.HIGHEST
    )
    latent_field = lax.psum_scatter(terms, "latent", scatter_dimension=0, tiled=True)[0]
    local_order = ordering - row_place * row_tile
    latent_field = jnp.take(latent_field, local_order, axis=1)
    matrix = working[0].astype(jnp.float32)
    shares = []
    for panel in range(PANELS):
        inverse = factor_inverse[0, panel]
        start = panel_index[panel] * width
        owner_col = start // col_tile
        owner_row = start // row_tile
        column_block = matrix.astype(jnp.bfloat16)
        local_rows = jnp.dot(column_block, inverse.T, preferred_element_type=jnp.float32).astype(
            jnp.bfloat16
        )
        row_panel = spread(local_rows, "col", owner_col)
        rhs_part = lax.dynamic_slice_in_dim(latent_field, start - owner_row * row_tile, width, 1)
        rhs_local = jnp.dot(
            rhs_part, inverse.astype(jnp.float32).T, precision=lax.Precision.HIGHEST
        ).astype(jnp.bfloat16)
        row_block = lax.dynamic_slice_in_dim(matrix, start - owner_row * row_tile, width, 0).astype(
            jnp.bfloat16
        )
        local_cols = lax.dot_general(
            row_block, inverse, (((0,), (1,)), ((), ())), preferred_element_type=jnp.float32
        ).astype(jnp.bfloat16)
        col_panel, rhs_block = (
            spread(local_cols, "row", owner_row),
            spread(rhs_local, "row", owner_row),
        )
        matrix = matrix - lax.dot_general(
            row_panel, col_panel, (((1,), (1,)), ((), ())), preferred_element_type=jnp.float32
        )
        latent_field = latent_field - lax.dot_general(
            rhs_block, row_panel, (((1,), (1,)), ((), ())), preferred_element_type=jnp.float32
        )
        shares.append(lax.dynamic_slice_in_dim(row_panel, col_place * share, share, 1))
    return (matrix[None], jnp.stack(shares)[None], latent_field[None])


def solution(mesh):
    return jax.shard_map(
        local,
        mesh=mesh,
        in_specs=(
            P("col", "latent", "row"),
            P(),
            P("row"),
            P("latent", "row", "col"),
            P("latent", None, None, None),
            P(),
        ),
        out_specs=(
            P("latent", "row", "col"),
            P("latent", None, "row", "col"),
            P("latent", "col", "row"),
        ),
        check_vma=False,
    )
```

profile of v0, /device:TPU:0, one launch (start us, length us, event | category | flops | bytes accessed | tf_op | source)
XLA Modules:
  0.0 168.1 jit_solution(5816712815958730422)
XLA Ops:
  8.0 0.0 copy-start
  8.0 0.0 copy-start.2
  8.0 0.0 copy-start.3
  8.0 0.0 all-reduce.7.cloned.1.call-start
  8.1 1.4 fusion.32
  10.2 2.5 %fusion.2 = bf16[512,512]{1,0:T(8,128)(2,1)} fusion(bf16[1024,512]{1,0:T(8,128)(2,1)} %bitcast.49, s32[]{:T(128)S(6)} %select_n.85, pred[]{:T(512)S(6)} %eq.15, bf16[1,2,512,512]{3,2,1,0:T(8,128)(2,1)} %param.10), kind=kOutput, calls=%fused_computation.9 | convolution fusion | flops 268959744 | bytes 1572869 | tf_op jit(solution)/shard_map/dot_general | solution.py:51
  12.7 0.0 all-reduce.7.cloned.1.call-update
  12.7 0.0 all-reduce.5.cloned.1.call-start
  12.8 0.0 copy-done.2
  12.8 0.0 copy-done.3
  12.8 0.0 copy-start.7
  12.8 1.7 %fusion = bf16[1024,512]{1,0:T(8,128)(2,1)} fusion(bf16[1,1024,512]{2,1,0:T(8,128)(2,1)S(1)} %copy-done.3, pred[]{:T(512)S(6)} %eq.14, bf16[1,2,512,512]{3,2,1,0:T(8,128)(2,1)S(1)} %copy-done.2), kind=kOutput, calls=%fused_computation.5 | convolution fusion | flops 537919488 | bytes 2621441 | tf_op jit(solution)/shard_map/dot_general | solution.py:40
  14.5 0.0 all-reduce.5.cloned.1.call-update
  14.5 0.0 reduce-scatter.2.cloned.1.call-start
  14.6 0.0 copy-done
  14.6 0.0 copy-done.7
  14.6 0.6 fusion.24
  15.3 1.1 copy.11
  16.3 0.0 reduce-scatter.2.cloned.1.call-update
  16.4 0.0 all-reduce.9.cloned.1.call-start
  17.1 27.1 %all-reduce.7.cloned.1.call-done = bf16[512,512]{1,0:T(8,128)(2,1)} async-done(((bf16[512,512]{1,0:T(8,128)(2,1)}), bf16[512,512]{1,0:T(8,128)(2,1)}) %all-reduce.7.cloned.1.call-update) | async-done | bytes 524304 | tf_op jit(solution)/shard_map/psum | solution.py:11
  44.2 39.1 %all-reduce.5.cloned.1.call-done = bf16[1024,512]{1,0:T(8,128)(2,1)} async-done(((bf16[1024,512]{1,0:T(8,128)(2,1)}), bf16[1024,512]{1,0:T(8,128)(2,1)}) %all-reduce.5.cloned.1.call-update) | async-done | bytes 1048592 | tf_op jit(solution)/shard_map/psum | solution.py:11
  83.3 2.4 %convolution_subtract_fusion = f32[1024,512]{1,0:T(8,128)S(1)} fusion(bf16[1024,512]{1,0:T(8,128)(2,1)} %all-reduce.5.cloned.1.call-done, bf16[512,512]{1,0:T(8,128)(2,1)} %all-reduce.7.cloned.1.call-done, bf16[1,1024,512]{2,1,0:T(8,128)(2,1)} %param.9), kind=kOutput, calls=%fused_computation.2 | convolution fusion | flops 537919488 | bytes 4718592 | tf_op jit(solution)/shard_map/dot_general | solution.py:58
  85.8 0.0 copy-start.6
  85.8 2.8 %fusion.1 = bf16[1024,512]{1,0:T(8,128)(2,1)} fusion(f32[1024,512]{1,0:T(8,128)S(1)} %convolution_subtract_fusion, pred[]{:T(512)S(6)} %eq.16, bf16[1,2,512,512]{3,2,1,0:T(8,128)(2,1)} %param.10), kind=kOutput, calls=%fused_computation.6 | convolution fusion | flops 538443776 | bytes 3670017 | tf_op jit(solution)/shard_map/dot_general | solution.py:40
  88.5 0.0 all-reduce.9.cloned.1.call-update
  88.6 0.0 all-reduce.11.cloned.1.call-start
  88.7 2.4 %fusion.3 = bf16[512,512]{1,0:T(8,128)(2,1)} fusion(f32[1024,512]{1,0:T(8,128)S(1)} %convolution_subtract_fusion, s32[]{:T(128)S(6)} %select_n.92, pred[]{:T(512)S(6)} %eq.17, bf16[1,2,512,512]{3,2,1,0:T(8,128)(2,1)} %param.10), kind=kOutput, calls=%fused_computation.10 | convolution fusion | flops 268959744 | bytes 1572869 | tf_op jit(solution)/shard_map/dot_general | solution.py:51
  91.0 0.0 all-reduce.11.cloned.1.call-update
  91.1 1.0 dynamic-slice_bitcast_fusion.1
  92.0 0.0 reduce-scatter.2.cloned.1.call-done
  92.1 1.9 %copy.12 = f32[1,32,1024]{1,2,0:T(8,128)} copy(f32[1,32,1024]{2,1,0:T(8,128)} %reduce-scatter.2.cloned.1.call-done) | data formatting | bytes 262144 | tf_op jit(solution)/shard_map/reduce_scatter | solution.py:29
  94.0 5.0 %gather_fusion = f32[1024,32]{1,0:T(8,128)} fusion(f32[32,1024]{0,1:T(8,128)} %bitcast.48, s32[1024]{0:T(1024)S(1)} %fusion.23), kind=kCustom, calls=%fused_computation | custom fusion | bytes 266240 | tf_op jit(solution)/shard_map/jit(_take)/gather | solution.py:31
  99.0 1.9 %copy.13 = f32[1024,32]{0,1:T(8,128)} copy(f32[1024,32]{1,0:T(8,128)} %gather_fusion) | data formatting | bytes 262144 | tf_op jit(solution)/shard_map/jit(_take)/gather | solution.py:31
  100.9 0.9 broadcast_select_fusion
  101.8 2.2 %fusion.5 = bf16[32,512]{1,0:T(8,128)(2,1)} fusion(bf16[1,2,512,512]{3,2,1,0:T(8,128)(2,1)} %param.10, f32[1024,32]{0,1:T(8,128)S(1)} %broadcast_select_fusion, s32[]{:T(128)S(6)} %select_n.85, pred[]{:T(512)S(6)} %eq.15), kind=kOutput, calls=%fused_computation.16 | convolution fusion | flops 100696064 | bytes 622597 | tf_op jit(solution)/shard_map/dot_general | solution.py:45
  104.0 9.8 %psum.46 = bf16[32,512]{1,0:T(8,128)(2,1)} all-reduce(bf16[32,512]{1,0:T(8,128)(2,1)} %fusion.5), channel_id=1, replica_groups=mesh['latent'=4,'row'=2,'col'=4] {'row'}, use_global_device_ids=true, to_apply=%region_5.6 | all-reduce | flops 16384 | bytes 65536 | tf_op jit(solution)/shard_map/psum | solution.py:11
  113.8 1.7 %convolution_subtract_fusion.2 = f32[32,1024]{1,0:T(8,128)S(1)} fusion(bf16[32,512]{1,0:T(8,128)(2,1)} %psum.46, bf16[1024,512]{1,0:T(8,128)(2,1)} %all-reduce.5.cloned.1.call-done, f32[1024,32]{0,1:T(8,128)S(1)} %broadcast_select_fusion), kind=kOutput, calls=%fused_computation.13 | convolution fusion | flops 33587200 | bytes 1343488 | tf_op jit(solution)/shard_map/dot_general | solution.py:61
  115.5 0.0 copy-start.4
  115.5 0.6 copy-done.4
  116.2 1.6 fusion.6
  117.8 7.2 %psum.47 = bf16[32,512]{1,0:T(8,128)(2,1)S(1)} all-reduce(bf16[32,512]{1,0:T(8,128)(2,1)S(1)} %fusion.6), channel_id=1, replica_groups=mesh['latent'=4,'row'=2,'col'=4] {'row'}, use_global_device_ids=true, to_apply=%region_6.7 | all-reduce | flops 16384 | bytes 65536 | tf_op jit(solution)/shard_map/psum | solution.py:11
  125.0 0.1 all-reduce.9.cloned.1.call-done
  125.2 1.0 dynamic-slice_bitcast_fusion
  126.1 0.8 maximum_bitcast_fusion
  127.0 29.4 %all-reduce.11.cloned.1.call-done = bf16[512,512]{1,0:T(8,128)(2,1)} async-done(((bf16[512,512]{1,0:T(8,128)(2,1)}), bf16[512,512]{1,0:T(8,128)(2,1)}) %all-reduce.11.cloned.1.call-update) | async-done | bytes 524304 | tf_op jit(solution)/shard_map/psum | solution.py:11
  156.4 3.5 %subtract_bitcast_fusion = f32[1,1024,512]{2,1,0:T(8,128)} fusion(f32[1024,512]{1,0:T(8,128)S(1)} %convolution_subtract_fusion, bf16[1024,512]{1,0:T(8,128)(2,1)} %all-reduce.9.cloned.1.call-done, bf16[512,512]{1,0:T(8,128)(2,1)} %all-reduce.11.cloned.1.call-done), kind=kOutput, calls=%fused_computation.1 | convolution fusion | flops 537395200 | bytes 5767168 | tf_op jit(solution)/shard_map/dot_general | solution.py:58
  159.9 1.1 fusion.4
  (7 shorter events, 0.0 us)
Async XLA Ops:
  8.0 6.6 %copy-start = (bf16[32,16,1024]{2,1,0:T(8,128)(2,1)S(1)}, bf16[32,16,1024]{2,1,0:T(8,128)(2,1)}, u32[]{:S(2)}) copy-start(bf16[32,16,1024]{2,1,0:T(8,128)(2,1)} %param.6) | copy-start | bytes 3145732
  8.0 4.8 %copy-start.2 = (bf16[1,2,512,512]{3,2,1,0:T(8,128)(2,1)S(1)}, bf16[1,2,512,512]{3,2,1,0:T(8,128)(2,1)}, u32[]{:S(2)}) copy-start(bf16[1,2,512,512]{3,2,1,0:T(8,128)(2,1)} %param.10) | copy-start | bytes 3145732
  8.0 4.8 %copy-start.3 = (bf16[1,1024,512]{2,1,0:T(8,128)(2,1)S(1)}, bf16[1,1024,512]{2,1,0:T(8,128)(2,1)}, u32[]{:S(2)}) copy-start(bf16[1,1024,512]{2,1,0:T(8,128)(2,1)} %param.9) | copy-start | bytes 3145732
  8.0 36.1 %all-reduce.7.cloned.1.call-start = ((), (), s32[]{:S(2)}) async-start(), calls=%async_computation.2 | async-start | bytes 1048576 | tf_op jit(solution)/shard_map/psum | solution.py:11
  12.7 70.6 %all-reduce.5.cloned.1.call-start = ((), (), s32[]{:S(2)}) async-start(), calls=%async_computation.1 | async-start | bytes 2097152 | tf_op jit(solution)/shard_map/psum | solution.py:11
  12.8 1.8 %copy-start.7 = (f32[64,4]{0,1:T(4,128)S(1)}, f32[64,4]{0,1:T(4,128)}, u32[]{:S(2)}) copy-start(f32[64,4]{0,1:T(4,128)} %param.7) | copy-start | bytes 3076
  14.5 77.5 %reduce-scatter.2.cloned.1.call-start = ((), (), s32[]{:S(2)}) async-start(), calls=%async_computation.5 | async-start | bytes 655360 | tf_op jit(solution)/shard_map/reduce_scatter | solution.py:29
  16.4 108.8 %all-reduce.9.cloned.1.call-start = ((), (), s32[]{:S(2)}) async-start(), calls=%async_computation.3 | async-start | bytes 2097152 | tf_op jit(solution)/shard_map/psum | solution.py:11
  85.8 2.8 %copy-start.6 = (s32[1024]{0:T(1024)S(1)}, s32[1024]{0:T(1024)}, u32[]{:S(2)}) copy-start(s32[1024]{0:T(1024)} %param.8) | copy-start | bytes 12292
  88.6 67.8 %all-reduce.11.cloned.1.call-start = ((), (), s32[]{:S(2)}) async-start(), calls=%async_computation.4 | async-start | bytes 1048576 | tf_op jit(solution)/shard_map/psum | solution.py:11
  115.5 0.7 copy-start.4
  127.0 32.9 %copy-start.5 = (f32[32,1024]{1,0:T(8,128)S(1)}, f32[32,1024]{1,0:T(8,128)}, u32[]{:S(2)}) copy-start(f32[32,1024]{1,0:T(8,128)} %copy-done.4) | copy-start | bytes 393220
  156.4 3.5 %copy-start.1 = (bf16[1024,512]{1,0:T(8,128)(2,1)S(1)}, bf16[1024,512]{1,0:T(8,128)(2,1)}, u32[]{:S(2)}) copy-start(bf16[1024,512]{1,0:T(8,128)(2,1)} %all-reduce.9.cloned.1.call-done) | copy-start | bytes 3145732
Sparse Core Ops, SparseCore 0:
  12.8 31.3 all-reduce.6
  47.2 36.0 all-reduce.4
  88.7 36.4 all-reduce.8
  127.4 28.9 all-reduce.10
Sparse Core Ops, SparseCore 1:
  17.3 24.3 reduce-scatter.1
where the time goes:
time: 169 us; the launch traced here: 168 us
  waiting for transfers between devices  95.9 us (57%)
  matrix products  22.5 us (13%)
  blocking collectives  17 us (10%)
  between operations  16.8 us (10%)
  local copies, waits for them, and re-layouts  14 us (8%)
  other arithmetic  1.78 us (1%)
    psum x4, waiting for transfers between devices, spread(): return lax.psum(kept, axis)  95.8 us
    psum x2, blocking collectives, spread(): return lax.psum(kept, axis)  17 us
    gather x2, local copies, waits for them, and re-layouts, local(): latent_field = jnp.take(latent_field, local_order, axis=1)  6.92 us
    dot_general x2, matrix products, local(): lax.dot_general(row_panel, col_panel, (((1,), (1,)), ((), ())), preferred...  5.94 us
    dot_general x2, matrix products, local(): lax.dot_general(row_block, inverse, (((0,), (1,)), ((), ())), preferred_e...  4.84 us
    dot_general x2, matrix products, local(): jnp.dot(column_block, inverse.T, preferred_element_type=jnp.float32)  4.47 us
    dot_general x2, matrix products, local(): jnp.dot(rhs_part, inverse.astype(jnp.float32).T, precision=lax.Precision....  3.83 us
  transfers between devices with their start and end apart: 5, of which 4 were waited for; matrix products, arithmetic and copies ran while one was open for 17% of the time, Pallas kernels for 0%

commit v1 on v0

v1 whole, which is shorter than its diff:
```python
import jax
import jax.numpy as jnp
from jax import lax
from jax.experimental import pallas as pl
from jax.experimental.pallas import tpu as pltpu
from jax.sharding import PartitionSpec as P

F32 = jnp.float32
BF16 = jnp.bfloat16
VMEM = pl.BlockSpec(memory_space=pltpu.VMEM)
SMEM = pl.BlockSpec(memory_space=pltpu.SMEM)
ANY = pl.BlockSpec(memory_space=pl.ANY)
PARAMS = pltpu.CompilerParams(vmem_limit_bytes=48 * 1024 * 1024)

OWN, SIB, ROW_OWN, ROW_SIB, COL_OWN, COL_SIB, POOL = 0, 8, 16, 21, 26, 31, 36


def dot(a, b, ca, cb):
    return lax.dot_general(a, b, (((ca,), (cb,)), ((), ())), preferred_element_type=F32)


def pieces(x, count):
    out = []
    for _ in range(count):
        piece = x.astype(BF16)
        out.append(piece)
        x = x - piece.astype(F32)
    return out


def where(cond, a, b):
    return jnp.where(cond, a, b)


class Place:
    def __init__(self, place, index):
        self.row, self.col = place[0], place[1]
        self.k, self.y = lax.rem(self.col, 2), lax.div(self.col, 2)
        self.q = [index[0], index[1]]
        self.half = [lax.div(q, 2) for q in self.q]
        self.low = [lax.rem(q, 2) for q in self.q]
        self.equal = self.q[0] == self.q[1]
        self.apart = self.half[0] != self.half[1]
        self.together = jnp.logical_not(self.equal | self.apart)
        self.in_row = [self.row == h for h in self.half]
        self.in_col = [self.y == h for h in self.half]
        self.kept = where(self.low[0] == self.k, 0, 1)

    def tile(self, panel_low, a, s):
        return 2 * (2 * panel_low + a) + s

    def sends(self, over_row, n):
        low = where(self.apart & (self.half[0] != self.row), self.low[1], self.low[0])
        s, a = (n // 2 if over_row else 1 - n // 2), n % 2
        plain = self.tile(low, a, s) if n < 4 else 0
        mine = where(self.kept == 0, self.low[0], self.low[1])
        other = where(self.kept == 0, self.low[1], self.low[0])
        first = self.kept == 0
        source = [
            where(first, self.tile(other, 0, 0), self.tile(other, 0, 1)),
            where(first, self.tile(other, 0, 1), self.tile(other, 1, 1)),
            self.tile(mine, 0, 0),
            self.tile(mine, 1, 1),
            self.tile(mine, 1, 0),
        ][n]
        if n == 4:
            return source
        if over_row:
            passed = self.tile(other, n % 2, n // 2)
        else:
            passed = 2 * (2 * self.k + n // 2) + n % 2
        both = where(self.in_row[0] & self.in_col[0], source, passed)
        return where(self.together, both, plain)

    def message(self, over_row, k):
        own, sib = (ROW_OWN, ROW_SIB) if over_row else (COL_OWN, COL_SIB)
        return where(k == self.k, own, sib)

    def diagonal(self, over_row, p, i, j):
        base = self.message(over_row, self.low[p])
        return base + (2 + i if i == j else 4), jnp.int32(1 if (i, j) == (0, 1) else 0)

    def mixed(self, over_row, i, j):
        return self.message(over_row, self.low[i]) + j, jnp.int32(i)

    def pick(self, cond, a, b):
        return where(cond, a[0], b[0]), where(cond, a[1], b[1])

    def rows(self, p, t, s, a):
        here = where(self.q[p] == self.col, OWN, SIB) + 2 * (2 * t + s) + a, jnp.int32(0)
        plain = self.message(False, jnp.int32(t)) + (a if s == 1 else 2 + a), jnp.int32(1)
        same = self.diagonal(False, p, s, a)
        if p == 0:
            cross = self.mixed(False, s, a)
        else:
            cross = self.mixed(False, a, s)
            cross = cross[0], 1 - cross[1]
        both = self.pick(self.low[p] == t, same, cross)
        beside = self.pick(self.together, both, plain)
        passed = self.message(True, jnp.int32(t)) + 2 * s + a, jnp.int32(1)
        kept = self.message(False, jnp.int32(t)) + 2 * s + a, jnp.int32(0)
        far = self.pick(self.together & (self.low[p] == t), kept, passed)
        return self.pick(self.in_col[p], here, self.pick(self.in_row[p], beside, far))

    def cols(self, p, a, s):
        here = self.tile(self.low[p], a, s), jnp.int32(0)
        plain = jnp.int32(ROW_OWN + 2 * s + a), jnp.int32(0)
        kept = jnp.int32(COL_OWN + 2 * s + a), jnp.int32(1)
        passed = self.pick(self.low[p] == self.k, kept, plain)
        same = self.diagonal(True, p, a, s)
        if p == 0:
            cross = self.mixed(True, s, a)
            cross = cross[0], 1 - cross[1]
        else:
            cross = self.mixed(True, a, s)
        source = self.pick(self.low[p] == self.k, same, cross)
        both = self.pick(self.in_col[p], source, passed)
        far = self.pick(self.together, both, plain)
        return self.pick(self.in_row[p], here, far)

    def cross(self, i, a):
        mine = self.pick(self.low[1] == 0, self.rows(0, 0, i, a), self.rows(0, 1, i, a))
        turned = self.pick(self.low[0] == 0, self.rows(1, 0, a, i), self.rows(1, 1, a, i))
        turned = turned[0], 1 - turned[1]
        equal_near = self.message(True, self.low[1]) + 2 * i + a, jnp.int32(1)
        near = self.pick(self.equal, equal_near, self.mixed(True, i, a))
        holder = self.low[0] if a == 0 else 1 - self.low[0]
        equal_far = self.message(i == 1, holder) + 4, jnp.int32(1)
        both_far = self.message(a == 1, self.low[i]) + 4, jnp.int32(i)
        far = self.pick(self.equal, equal_far, both_far)
        outside = self.pick(self.in_col[1], near, far)
        return self.pick(self.in_row[1], mine, self.pick(self.in_row[0], turned, outside))


def quarter_of(ref, number, size):
    down = pl.multiple_of(lax.div(number, 2) * size, size)
    along = pl.multiple_of(lax.rem(number, 2) * size, size)
    return ref.at[pl.ds(down, size), pl.ds(along, size)]


def first_kernel(place, index, working, row1, row2, col1, col2, sems):
    here = Place(place, index)
    size = row1.shape[1]
    copies = []
    for over_row, refs in ((True, (row1, row2)), (False, (col1, col2))):
        for n in range(4):
            copies.append(
                pltpu.make_async_copy(
                    quarter_of(working, here.sends(over_row, n), size),
                    refs[n // 2].at[n % 2],
                    sems.at[len(copies)],
                )
            )
    for copy in copies:
        copy.start()
    for copy in copies:
        copy.wait()


def second_kernel(place, index, working, row_own, row_sib, col_own, col_sib, row_out, col_out, sems):
    here = Place(place, index)
    size = row_out.shape[1]
    source = here.in_row[0] & here.in_col[0]
    own = here.low[0] == here.k
    for n, (got, got_sib, out, which) in enumerate(
        ((col_own, col_sib, row_out, 1), (row_own, row_sib, col_out, 0))
    ):
        sem = sems.at[n]

        @pl.when(source)
        def _():
            pltpu.make_async_copy(
                quarter_of(working, here.sends(True, 4), size), out.at[0], sem
            ).start()

        @pl.when(jnp.logical_not(source) & here.together)
        def _():
            pltpu.make_async_copy(got.at[which], out.at[0], sem).start()

        @pl.when(jnp.logical_not(source) & jnp.logical_not(here.together) & own)
        def _():
            pltpu.make_async_copy(got.at[0], out.at[0], sem).start()

        @pl.when(jnp.logical_not(source | here.together | own))
        def _():
            pltpu.make_async_copy(got_sib.at[1], out.at[0], sem).start()

    pltpu.make_async_copy(row_own.at[0], row_out.at[0], sems.at[0]).wait()
    pltpu.make_async_copy(col_own.at[0], col_out.at[0], sems.at[1]).wait()


def rotate_kernel(place, obs, rotation, order, out):
    times, own_vars, stations = obs.shape
    all_vars, latents = rotation.shape
    flat = obs[...].reshape(times * own_vars, stations)
    shape = (latents * times, times * own_vars)
    left = lax.broadcasted_iota(jnp.int32, shape, 0)
    right = lax.broadcasted_iota(jnp.int32, shape, 1)
    keep = lax.rem(left, times) == lax.div(right, own_vars)
    sel_l = lax.broadcasted_iota(jnp.int32, (latents * times, latents), 0)
    sel_l = lax.div(sel_l, times) == lax.broadcasted_iota(jnp.int32, (latents * times, latents), 1)
    pick_v = lax.broadcasted_iota(jnp.int32, (all_vars, times * own_vars), 1)
    pick_v = lax.rem(pick_v, own_vars) + place[2] * own_vars
    pick_v = pick_v == lax.broadcasted_iota(jnp.int32, (all_vars, times * own_vars), 0)
    sel_l = sel_l.astype(F32).astype(BF16)
    pick_v = pick_v.astype(F32).astype(BF16)
    total = None
    for piece in pieces(rotation[...], 3):
        wide = dot(sel_l, piece, 1, 1).astype(BF16)
        wide = dot(wide, pick_v, 1, 0)
        wide = jnp.where(keep, wide, 0.0).astype(BF16)
        part = dot(wide, flat, 1, 0)
        total = part if total is None else total + part
    local = order[...] - place[0] * stations
    spread = lax.broadcasted_iota(jnp.int32, (stations, stations), 0) == local
    spread = spread.astype(F32).astype(BF16)
    moved = dot(total.astype(BF16), spread, 1, 0)
    out[...] = moved.astype(BF16).reshape(out.shape)


def factor_kernel(
    place, index, working, sibling, row1, row1s, row2, row2s, row3, row3s, col1, col1s, col2, col2s, col3, col3s,
    inverse, field, rhs_far, trailing, panels, whitened,
    pool, blocks, factors0, factors1, turned0, turned1, rhs_near, table, flip, sems,
):
    here = Place(place, index)
    size = pool.shape[1]
    tall, wide = trailing.shape
    width = inverse.shape[1]
    share = panels.shape[2]
    steps = tall // size

    copies = []

    def fetch(source, slot):
        copies.append(pltpu.make_async_copy(source, pool.at[slot], sems.at[slot]))

    for n in range(8):
        fetch(quarter_of(working, jnp.int32(n), size), OWN + n)
        fetch(quarter_of(sibling, jnp.int32(n), size), SIB + n)
    for base, refs in (
        (ROW_OWN, (row1, row2, row3)),
        (ROW_SIB, (row1s, row2s, row3s)),
        (COL_OWN, (col1, col2, col3)),
        (COL_SIB, (col1s, col2s, col3s)),
    ):
        for n in range(5):
            fetch(refs[n // 2].at[n % 2], base + n)
    for copy in copies:
        copy.start()

    entries = []
    for p in range(2):
        entries += [here.rows(p, n // 4, n // 2 % 2, n % 2) for n in range(8)]
    for p in range(2):
        entries += [here.cols(p, n // 2, n % 2) for n in range(4)]
    entries += [here.cross(n // 2, n % 2) for n in range(4)]
    for n, (slot, turn) in enumerate(entries):
        table[n] = slot
        flip[n] = turn
    for copy in copies:
        copy.wait()

    def assemble(n, _):
        for side in range(2):
            slot = table[2 * n + side]
            turn = flip[2 * n + side]
            down = pl.ds(pl.multiple_of(n * size, size), size)
            along = pl.ds(side * size, size)

            @pl.when(turn == 0)
            def _():
                blocks[down, along] = pool[slot]

            @pl.when(turn != 0)
            def _():
                blocks[down, along] = pool[slot].T

        return 0

    lax.fori_loop(0, len(entries) // 2, assemble, 0)

    def strip(n):
        return pl.ds(n * size, size)

    rows0, rows1, cols0, cols1, cross = 0, steps, 2 * steps, 2 * steps + 2, 2 * steps + 4
    inv0, inv1 = inverse[0], inverse[1]

    def factor(n, _):
        n = where(n < steps, n, cross + n - steps)
        to = where(n < steps, n, n - cross + steps)
        got = blocks[pl.ds(pl.multiple_of(n * size, size), size)]
        factors0[pl.ds(pl.multiple_of(to * size, size), size)] = dot(got, inv0, 1, 1).astype(BF16)
        return 0

    lax.fori_loop(0, steps + 2, factor, 0)
    mixed = factors0[pl.ds(tall, width)]
    turned0[...] = dot(inv0, blocks[pl.ds(cols0 * size, width)], 1, 0).astype(BF16)

    def later(n, _):
        down = pl.ds(pl.multiple_of(n * size, size), size)
        got = blocks[pl.ds(pl.multiple_of((n + rows1) * size, size), size)]
        got = got.astype(F32) - dot(factors0[down], mixed, 1, 1)
        factors1[down] = dot(got.astype(BF16), inv1, 1, 1).astype(BF16)
        return 0

    lax.fori_loop(0, steps, later, 0)
    got = blocks[pl.ds(cols1 * size, width)].astype(F32) - dot(mixed, turned0[...], 1, 0)
    turned1[...] = dot(inv1, got.astype(BF16), 1, 0).astype(BF16)

    def update(n, _):
        down = pl.ds(pl.multiple_of(n * size, size), size)
        change = dot(factors0[down], turned0[...], 1, 0) + dot(factors1[down], turned1[...], 1, 0)
        for side in range(2):
            along = pl.ds(side * size, size)
            trailing[down, along] = pool[2 * n + side].astype(F32) - change[:, side * size : (side + 1) * size]
        return 0

    lax.fori_loop(0, steps, update, 0)
    lanes = pl.ds(pl.multiple_of(here.col * share, share), share)
    panels[0] = factors0[pl.ds(0, tall), lanes]
    panels[1] = factors1[:, lanes]

    for p in range(2):
        inside = pl.ds(pl.multiple_of(here.low[p] * width, width), width)

        @pl.when(here.in_row[p])
        def _():
            rhs_near[p] = field[:, inside]

        @pl.when(jnp.logical_not(here.in_row[p]))
        def _():
            rhs_near[p] = rhs_far[p].astype(F32)

    def solve(rhs, inv):
        return sum(dot(piece, inv, 1, 1) for piece in pieces(rhs, 2)).astype(BF16)

    solved0 = solve(rhs_near[0], inv0)
    solved1 = solve(rhs_near[1] - dot(solved0, mixed, 1, 1), inv1)
    whitened[...] = (
        field[...] - dot(solved0, factors0[pl.ds(0, tall)], 1, 1) - dot(solved1, factors1[...], 1, 1)
    )


def local(observations, rotation, ordering, working, factor_inverse, panel_index):
    latents = rotation.shape[1]
    latent_count = lax.axis_size("latent")
    times, own_vars, stations = observations.shape
    matrix = working[0]
    inverse = factor_inverse[0]
    tall, wide = matrix.shape
    panel_count, width, _ = inverse.shape
    size = width // 2
    share = width // lax.axis_size("col")
    row, col, latent = lax.axis_index("row"), lax.axis_index("col"), lax.axis_index("latent")
    place = jnp.stack([row, col, latent])

    def across_rows(x):
        return lax.ppermute(x, "row", [(0, 1), (1, 0)])

    def across_cols(x):
        return lax.ppermute(x, "col", [(i, i ^ 2) for i in range(lax.axis_size("col"))])

    def siblings(x):
        return lax.ppermute(x, "col", [(i, i ^ 1) for i in range(lax.axis_size("col"))])

    pair = jax.ShapeDtypeStruct((2, size, size), BF16)
    one = jax.ShapeDtypeStruct((1, size, size), BF16)
    row1, row2, col1, col2 = pl.pallas_call(
        first_kernel,
        out_shape=(pair,) * 4,
        in_specs=[SMEM, SMEM, ANY],
        out_specs=(ANY,) * 4,
        scratch_shapes=[pltpu.SemaphoreType.DMA((8,))],
        compiler_params=PARAMS,
    )(place, panel_index, matrix)
    row1, col1 = across_rows(row1), across_cols(col1)
    row2, col2 = across_rows(row2), across_cols(col2)
    sibling = siblings(matrix)

    terms = pl.pallas_call(
        rotate_kernel,
        out_shape=jax.ShapeDtypeStruct((latents, times, stations), BF16),
        in_specs=[SMEM, VMEM, VMEM, VMEM],
        out_specs=VMEM,
        compiler_params=PARAMS,
    )(place, observations, rotation, ordering[None])

    row1s, col1s = siblings(row1), siblings(col1)
    row3, col3 = pl.pallas_call(
        second_kernel,
        out_shape=(one,) * 2,
        in_specs=[SMEM, SMEM] + [ANY] * 5,
        out_specs=(ANY,) * 2,
        scratch_shapes=[pltpu.SemaphoreType.DMA((2,))],
        compiler_params=PARAMS,
    )(place, panel_index, matrix, row1, row1s, col1, col1s)
    row3, col3 = across_rows(row3), across_cols(col3)

    field = lax.dynamic_index_in_dim(terms, latent, 0, keepdims=False).astype(F32)
    for shift in range(1, latent_count):
        target = lax.rem(latent + shift, latent_count)
        sent = lax.dynamic_index_in_dim(terms, target, 0, keepdims=False)
        pairs = [(i, (i + shift) % latent_count) for i in range(latent_count)]
        field = field + lax.ppermute(sent, "latent", pairs).astype(F32)
    rhs = jnp.stack(
        [
            lax.dynamic_slice_in_dim(field, (panel_index[p] % 2) * width, width, 1)
            for p in range(panel_count)
        ]
    ).astype(BF16)
    rhs_far = across_rows(rhs)

    row2s, col2s = siblings(row2), siblings(col2)
    row3s, col3s = siblings(row3), siblings(col3)

    trailing, panels, whitened = pl.pallas_call(
        factor_kernel,
        out_shape=(
            jax.ShapeDtypeStruct((tall, wide), F32),
            jax.ShapeDtypeStruct((panel_count, tall, share), BF16),
            jax.ShapeDtypeStruct((times, stations), F32),
        ),
        in_specs=[SMEM, SMEM] + [ANY] * 14 + [VMEM] * 3,
        out_specs=(VMEM, VMEM, VMEM),
        scratch_shapes=[
            pltpu.VMEM((POOL, size, size), BF16),
            pltpu.VMEM((14 * size, width), BF16),
            pltpu.VMEM((tall + width, width), BF16),
            pltpu.VMEM((tall, width), BF16),
            pltpu.VMEM((width, wide), BF16),
            pltpu.VMEM((width, wide), BF16),
            pltpu.VMEM((panel_count, times, width), F32),
            pltpu.SMEM((28,), jnp.int32),
            pltpu.SMEM((28,), jnp.int32),
            pltpu.SemaphoreType.DMA((POOL,)),
        ],
        compiler_params=PARAMS,
    )(
        place, panel_index, matrix, sibling, row1, row1s, row2, row2s, row3, row3s,
        col1, col1s, col2, col2s, col3, col3s, inverse, field, rhs_far,
    )
    return trailing[None], panels[None], whitened[None]


def solution(mesh):
    return jax.shard_map(
        local,
        mesh=mesh,
        in_specs=(
            P("col", "latent", "row"),
            P(),
            P("row"),
            P("latent", "row", "col"),
            P("latent", None, None, None),
            P(),
        ),
        out_specs=(
            P("latent", "row", "col"),
            P("latent", None, "row", "col"),
            P("latent", "col", "row"),
        ),
        check_vma=False,
    )
```

time: 169 us -> 57.8 us (0.34)
  waiting for transfers between devices: 95.9 us -> 11 us
  matrix products: 22.5 us -> 0 us
  Pallas kernels: 0 us -> 20.5 us
  blocking collectives: 17 us -> 0 us
  starting transfers between devices: 0.21 us -> 14 us
  between operations: 16.8 us -> 4.72 us
  local copies, waits for them, and re-layouts: 14 us -> 6.09 us
    psum x4 -> x0, waiting for transfers between devices: 95.8 us -> none  [spread(): return lax.psum(kept, axis)]
    dot_general x11 -> x0, matrix products: 22.5 us -> none  [the longest x2 5.94 us: local(): lax.dot_general(row_panel, col_panel, (((1,), (1,)), ((), ())), preferred...]
    pallas_call x0 -> x4, Pallas kernels: none -> 20.5 us  [the longest x1 15.4 us: local(): pl.pallas_call(factor_kernel, out_shape=(jax.ShapeDtypeStruct((tall, wide...]
    psum x2 -> x0, blocking collectives: 17 us -> none  [spread(): return lax.psum(kept, axis)]
    ppermute x0 -> x17, starting transfers between devices: none -> 14 us  [the longest x3 5.71 us: local(): field = field + lax.ppermute(sent, 'latent', pairs).astype(F32)]
    ppermute x0 -> x17, waiting for transfers between devices: none -> 11 us  [the longest x4 8.38 us: across_rows(): return lax.ppermute(x, 'row', [(0, 1), (1, 0)])]
    gather x2 -> x0, local copies, waits for them, and re-layouts: 6.92 us -> none  [local(): latent_field = jnp.take(latent_field, local_order, axis=1)]
    unnamed x16 -> x17, local copies, waits for them, and re-layouts: 0.7 us -> 4.77 us
  transfers between devices with their start and end apart: 5 -> 17, of which waited for: 4 -> 6; matrix products, arithmetic and copies ran while one was open for 17% -> 5% of each run, Pallas kernels for 0% -> 9%
where the time goes in v1:
time: 57.8 us; the launch traced here: 57.3 us
  Pallas kernels  20.5 us (35%)
  starting transfers between devices  14 us (24%)
  waiting for transfers between devices  11 us (19%)
  local copies, waits for them, and re-layouts  6.09 us (11%)
  between operations  4.72 us (8%)
  other arithmetic  0.96 us (2%)
    pallas_call x1, Pallas kernels, local(): pl.pallas_call(factor_kernel, out_shape=(jax.ShapeDtypeStruct((tall, wide...  15.4 us
    ppermute x4, waiting for transfers between devices, across_rows(): return lax.ppermute(x, 'row', [(0, 1), (1, 0)])  8.38 us
    ppermute x3, starting transfers between devices, local(): field = field + lax.ppermute(sent, 'latent', pairs).astype(F32)  5.71 us
    unnamed x17, local copies, waits for them, and re-layouts  4.77 us
    ppermute x4, starting transfers between devices, across_rows(): return lax.ppermute(x, 'row', [(0, 1), (1, 0)])  4.18 us
    ppermute x3, starting transfers between devices, across_cols(): lax.ppermute(x, 'col', [(i, i ^ 2) for i in range(lax.axis_size('col'))])  2.53 us
    pallas_call x1, Pallas kernels, local(): pl.pallas_call(rotate_kernel, out_shape=jax.ShapeDtypeStruct((latents, ti...  2.12 us
    ppermute x7, starting transfers between devices, siblings(): lax.ppermute(x, 'col', [(i, i ^ 1) for i in range(lax.axis_size('col'))])  1.59 us
  transfers between devices with their start and end apart: 17, of which 6 were waited for; matrix products, arithmetic and copies ran while one was open for 5% of the time, Pallas kernels for 9%

profile of v1, /device:TPU:0, one launch (start us, length us, event | category | flops | bytes accessed | tf_op | source)
XLA Modules:
  0.0 57.3 jit_solution(16947273740114131202)
XLA Ops:
  0.6 0.5 collective-permute-start
  1.2 0.8 %copy.9.rotation = f32[64,4]{1,0:T(8,128)S(1)} copy(f32[64,4]{0,1:T(4,128)} %param.7) | data formatting | bytes 2048 | tf_op args[1]
  1.9 0.1 pad_add_fusion.place
  2.0 1.2 %copy-done.2 = bf16[32,16,1024]{2,1,0:T(8,128)(2,1)S(1)} copy-done((bf16[32,16,1024]{2,1,0:T(8,128)(2,1)S(1)}, bf16[32,16,1024]{2,1,0:T(8,128)(2,1)}, u32[]{:S(2)}) %copy-start.2) | copy-done | bytes 1048600
  3.2 0.7 %copy-done.5 = s32[1024]{0:T(1024)S(1)} copy-done((s32[1024]{0:T(1024)S(1)}, s32[1024]{0:T(1024)}, u32[]{:S(2)}) %copy-start.5) | copy-done | bytes 4120
  3.9 2.1 %shard_map.87 = bf16[4,32,1024]{2,1,0:T(8,128)(2,1)S(1)} custom-call(s32[3]{0:T(128)S(1)} %pad_add_fusion.place, bf16[32,16,1024]{2,1,0:T(8,128)(2,1)S(1)} %copy-done.2, f32[64,4]{1,0:T(8,128)S(1)} %copy.9.rotation, s32[1,1024]{1,0:T(1,128)S(1)} %bitcast.29), custom_call_target="tpu_custom_call" | custom-call | tf_op jit(solution)/shard_map/pallas_call | solution.py:381
  6.0 0.0 copy-start.1
  6.1 0.7 %dynamic-slice_bitcast_fusion.2 = (bf16[32,1024]{1,0:T(8,128)(2,1)S(1)}, bf16[32,1024]{1,0:T(8,128)(2,1)}, bf16[32,1024]{1,0:T(8,128)(2,1)}) fusion(bf16[4,32,1024]{2,1,0:T(8,128)(2,1)S(1)} %shard_map.87, s32[]{:T(128)S(6)} %select_n.31, s32[]{:T(128)S(6)} %select_n.33, s32[]{:T(128)S(6)} %select_n.32), kind=kLoop, calls=%fused_computation.8 | loop fusion | bytes 393228 | tf_op jit(solution)/shard_map/jit(dynamic_index_in_dim)/squeeze | solution.py:403
  6.7 2.7 %collective-permute-start.13 = (bf16[32,1024]{1,0:T(8,128)(2,1)S(1)}, bf16[32,1024]{1,0:T(8,128)(2,1)S(1)}, u32[]{:S(2)}, u32[]{:S(2)}) collective-permute-start(bf16[32,1024]{1,0:T(8,128)(2,1)S(1)} %get-tuple-element.21), channel_id=1, source_target_pairs={{0,8},{8,16},{16,24},{24,0},{1,9},{9,17},{17,25},{25,1},{2,10},{10... | collective-permute-start | bytes 196616 | tf_op jit(solution)/shard_map/ppermute | solution.py:405
  9.4 2.0 %collective-permute-start.15 = (bf16[32,1024]{1,0:T(8,128)(2,1)}, bf16[32,1024]{1,0:T(8,128)(2,1)S(1)}, u32[]{:S(2)}, u32[]{:S(2)}) collective-permute-start(bf16[32,1024]{1,0:T(8,128)(2,1)} %get-tuple-element.22), channel_id=1, source_target_pairs={{0,24},{8,0},{16,8},{24,16},{1,25},{9,1},{17,9},{25,17},{2,26},{10... | collective-permute-start | bytes 196616 | tf_op jit(solution)/shard_map/ppermute | solution.py:405
  11.4 1.0 %collective-permute-start.14 = (bf16[32,1024]{1,0:T(8,128)(2,1)}, bf16[32,1024]{1,0:T(8,128)(2,1)}, u32[]{:S(2)}, u32[]{:S(2)}) collective-permute-start(bf16[32,1024]{1,0:T(8,128)(2,1)} %get-tuple-element.23), channel_id=1, source_target_pairs={{0,16},{8,24},{16,0},{24,8},{1,17},{9,25},{17,1},{25,9},{2,18},{10... | collective-permute-start | bytes 196616 | tf_op jit(solution)/shard_map/ppermute | solution.py:405
  12.4 0.7 %copy-done.3 = s32[2]{0:T(128)S(1)} copy-done((s32[2]{0:T(128)S(1)}, s32[2]{0:T(128)}, u32[]{:S(2)}) %copy-start.3) | copy-done | bytes 32
  13.1 1.4 %shard_map.85 = (bf16[2,256,256]{2,1,0:T(8,128)(2,1)}, bf16[2,256,256]{2,1,0:T(8,128)(2,1)S(1)}, bf16[2,256,256]{2,1,0:T(8,128)(2,1)}, bf16[2,256,256]{2,1,0:T(8,128)(2,1)S(1)}) custom-call(s32[3]{0:T(128)S(1)} %pad_add_fusion.place, s32[2]{0:T(128)S(1)} %copy-done.3, bf16[1024,512]{1,0:T(8,128)(2,1)S(1)} %bitcast.25), custom_call_target="tpu_custom_call" | custom-call | tf_op jit(solution)/shard_map/pallas_call | solution.py:369
  14.5 0.7 %copy-done.6 = bf16[2,256,256]{2,1,0:T(8,128)(2,1)} copy-done((bf16[2,256,256]{2,1,0:T(8,128)(2,1)}, bf16[2,256,256]{2,1,0:T(8,128)(2,1)S(1)}, u32[]{:S(2)}) %copy-start.6) | copy-done | bytes 262168
  15.2 0.7 %copy-done.7 = bf16[2,256,256]{2,1,0:T(8,128)(2,1)} copy-done((bf16[2,256,256]{2,1,0:T(8,128)(2,1)}, bf16[2,256,256]{2,1,0:T(8,128)(2,1)S(1)}, u32[]{:S(2)}) %copy-start.7) | copy-done | bytes 262168
  16.0 1.5 %collective-permute-start.1 = (bf16[2,256,256]{2,1,0:T(8,128)(2,1)}, bf16[2,256,256]{2,1,0:T(8,128)(2,1)}, u32[]{:S(2)}, u32[]{:S(2)}) collective-permute-start(bf16[2,256,256]{2,1,0:T(8,128)(2,1)} %get-tuple-element.12), channel_id=1, source_target_pairs={{0,4},{4,0},{1,5},{5,1},{2,6},{6,2},{3,7},{7,3},{8,12},{12,8},{9,1... | collective-permute-start | bytes 786440 | tf_op jit(solution)/shard_map/ppermute | solution.py:359
  17.5 0.0 collective-permute-done.13
  17.5 1.5 %collective-permute-start.5 = (bf16[2,256,256]{2,1,0:T(8,128)(2,1)}, bf16[2,256,256]{2,1,0:T(8,128)(2,1)}, u32[]{:S(2)}, u32[]{:S(2)}) collective-permute-start(bf16[2,256,256]{2,1,0:T(8,128)(2,1)} %get-tuple-element.14), channel_id=1, source_target_pairs={{0,2},{1,3},{2,0},{3,1},{4,6},{5,7},{6,4},{7,5},{8,10},{9,11},{10,... | collective-permute-start | bytes 786440 | tf_op jit(solution)/shard_map/ppermute | solution.py:362
  19.0 0.6 %fusion.4 = (s32[1]{0:T(128)}, s32[1]{0:T(128)}) fusion(s32[2]{0:T(128)S(1)} %copy-done.3), kind=kLoop, calls=%fused_computation.12 | loop fusion | bytes 16 | tf_op jit(solution)/shard_map/slice | solution.py:408
  23.6 0.0 collective-permute-done.15
  23.6 0.6 %collective-permute-start.3 = (bf16[2,256,256]{2,1,0:T(8,128)(2,1)}, bf16[2,256,256]{2,1,0:T(8,128)(2,1)S(1)}, u32[]{:S(2)}, u32[]{:S(2)}) collective-permute-start(bf16[2,256,256]{2,1,0:T(8,128)(2,1)} %copy-done.7), channel_id=1, source_target_pairs={{0,4},{4,0},{1,5},{5,1},{2,6},{6,2},{3,7},{7,3},{8,12},{12,8},{9,1... | collective-permute-start | bytes 786440 | tf_op jit(solution)/shard_map/ppermute | solution.py:359
  24.2 0.0 collective-permute-done.14
  24.2 0.5 collective-permute-start.9
  24.7 0.9 %fusion.1.field = f32[32,1024]{1,0:T(8,128)S(1)} fusion(bf16[32,1024]{1,0:T(8,128)(2,1)S(1)} %collective-permute-done.15, bf16[32,1024]{1,0:T(8,128)(2,1)} %collective-permute-done.14, bf16[32,1024]{1,0:T(8,128)(2,1)S(1)} %collective-permute-done.13, bf16[4,32,1024]{2,1,0:T(8,128)(2,1)S(1)} %shard_map.87, s32[]{:T(128)S(6)} %select_n.30), kind=kLoop, calls=%fused_computation.2 | loop fusion | flops 229376 | bytes 393220 | tf_op jit(solution)/shard_map/add | solution.py:405
  25.6 0.0 collective-permute-done.1.row_own.row1
  25.6 0.1 collective-permute-start.2
  25.7 0.0 collective-permute-done.5.col_own.col1
  25.7 0.5 collective-permute-start.6
  26.2 4.9 %collective-permute-done.3.row2 = bf16[2,256,256]{2,1,0:T(8,128)(2,1)S(1)} collective-permute-done((bf16[2,256,256]{2,1,0:T(8,128)(2,1)}, bf16[2,256,256]{2,1,0:T(8,128)(2,1)S(1)}, u32[]{:S(2)}, u32[]{:S(2)}) %collective-permute-start.3) | collective-permute-done | bytes 262176 | tf_op jit(solution)/shard_map/ppermute | solution.py:359
  31.1 0.5 collective-permute-start.16
  31.7 0.0 collective-permute-done.9.col2
  31.7 0.0 collective-permute-start.4
  31.7 0.0 collective-permute-done.2.row_sib.row1s
  31.7 0.5 collective-permute-start.10
  32.2 0.0 collective-permute-done.6.col_sib.col1s
  32.2 1.5 %shard_map.86 = (bf16[1,256,256]{2,1,0:T(8,128)(2,1)S(1)}, bf16[1,256,256]{2,1,0:T(8,128)(2,1)S(1)}) custom-call(s32[3]{0:T(128)S(1)} %pad_add_fusion.place, s32[2]{0:T(128)S(1)} %copy-done.4, bf16[1024,512]{1,0:T(8,128)(2,1)S(1)} %bitcast.26, bf16[2,256,256]{2,1,0:T(8,128)(2,1)} %collective-permute-done.1.row_own.row1, ...), custom_call_target="tpu_custom_call" | custom-call | tf_op jit(solution)/shard_map/pallas_call | solution.py:390
  33.7 1.6 %collective-permute-start.7 = (bf16[1,256,256]{2,1,0:T(8,128)(2,1)S(1)}, bf16[1,256,256]{2,1,0:T(8,128)(2,1)S(1)}, u32[]{:S(2)}, u32[]{:S(2)}) collective-permute-start(bf16[1,256,256]{2,1,0:T(8,128)(2,1)S(1)} %get-tuple-element.15), channel_id=1, source_target_pairs={{0,4},{4,0},{1,5},{5,1},{2,6},{6,2},{3,7},{7,3},{8,12},{12,8},{9,1... | collective-permute-start | bytes 393224 | tf_op jit(solution)/shard_map/ppermute | solution.py:359
  35.3 0.1 collective-permute-done.16.rhs_far
  35.4 0.5 collective-permute-start.11
  35.9 3.4 %collective-permute-done.7.row3 = bf16[1,256,256]{2,1,0:T(8,128)(2,1)S(1)} collective-permute-done((bf16[1,256,256]{2,1,0:T(8,128)(2,1)S(1)}, bf16[1,256,256]{2,1,0:T(8,128)(2,1)S(1)}, u32[]{:S(2)}, u32[]{:S(2)}) %collective-permute-start.7) | collective-permute-done | bytes 131104 | tf_op jit(solution)/shard_map/ppermute | solution.py:359
  39.3 0.0 collective-permute-start.8
  39.3 1.2 %collective-permute-done.11.col3 = bf16[1,256,256]{2,1,0:T(8,128)(2,1)S(1)} collective-permute-done((bf16[1,256,256]{2,1,0:T(8,128)(2,1)S(1)}, bf16[1,256,256]{2,1,0:T(8,128)(2,1)S(1)}, u32[]{:S(2)}, u32[]{:S(2)}) %collective-permute-start.11) | collective-permute-done | bytes 131104 | tf_op jit(solution)/shard_map/ppermute | solution.py:362
  40.5 0.0 collective-permute-start.12
  40.5 0.0 collective-permute-done.4.row2s
  40.5 0.1 collective-permute-done.8.row3s
  40.6 1.2 %collective-permute-done.12.col3s = bf16[1,256,256]{2,1,0:T(8,128)(2,1)S(1)} collective-permute-done((bf16[1,256,256]{2,1,0:T(8,128)(2,1)S(1)}, bf16[1,256,256]{2,1,0:T(8,128)(2,1)S(1)}, u32[]{:S(2)}, u32[]{:S(2)}) %collective-permute-start.12) | collective-permute-done | bytes 131104 | tf_op jit(solution)/shard_map/ppermute | solution.py:365
  41.8 0.0 collective-permute-done.sibling
  41.9 15.4 %shard_map.88 = (f32[1024,512]{1,0:T(8,128)}, bf16[2,1024,128]{2,1,0:T(8,128)(2,1)}, f32[32,1024]{1,0:T(8,128)}) custom-call(s32[3]{0:T(128)S(1)} %pad_add_fusion.place, s32[2]{0:T(128)S(1)} %copy-done.4, bf16[1024,512]{1,0:T(8,128)(2,1)S(1)} %bitcast.27, bf16[1024,512]{1,0:T(8,128)(2,1)S(1)} %collective-permute-done.sibling, ...), custom_call_target="tpu_custom_call" | custom-call | tf_op jit(solution)/shard_map/pallas_call | solution.py:417
  (13 shorter events, 0.0 us)
Async XLA Ops:
  0.6 11.8 %copy-start = (bf16[1,1024,512]{2,1,0:T(8,128)(2,1)S(1)}, bf16[1,1024,512]{2,1,0:T(8,128)(2,1)}, u32[]{:S(2)}) copy-start(bf16[1,1024,512]{2,1,0:T(8,128)(2,1)} %param.9) | copy-start | bytes 3145732
  0.6 41.2 %collective-permute-start = (bf16[1024,512]{1,0:T(8,128)(2,1)}, bf16[1024,512]{1,0:T(8,128)(2,1)S(1)}, u32[]{:S(2)}, u32[]{:S(2)}) collective-permute-start(bf16[1024,512]{1,0:T(8,128)(2,1)} %bitcast.24), channel_id=1, source_target_pairs={{0,1},{1,0},{2,3},{3,2},{4,5},{5,4},{6,7},{7,6},{8,9},{9,8},{10,11... | collective-permute-start | bytes 3145736 | tf_op jit(solution)/shard_map/ppermute | solution.py:365
  2.0 1.2 %copy-start.2 = (bf16[32,16,1024]{2,1,0:T(8,128)(2,1)S(1)}, bf16[32,16,1024]{2,1,0:T(8,128)(2,1)}, u32[]{:S(2)}) copy-start(bf16[32,16,1024]{2,1,0:T(8,128)(2,1)} %obs.1) | copy-start | bytes 3145732
  3.2 0.7 %copy-start.5 = (s32[1024]{0:T(1024)S(1)}, s32[1024]{0:T(1024)}, u32[]{:S(2)}) copy-start(s32[1024]{0:T(1024)} %param.8) | copy-start | bytes 12292
  3.9 28.3 %copy-start.4 = (s32[2]{0:T(128)S(1)}, s32[2]{0:T(128)}, u32[]{:S(2)}) copy-start(s32[2]{0:T(128)} %index.5) | copy-start | bytes 28
  6.0 35.8 %copy-start.1 = (bf16[1,2,512,512]{3,2,1,0:T(8,128)(2,1)S(1)}, bf16[1,2,512,512]{3,2,1,0:T(8,128)(2,1)}, u32[]{:S(2)}) copy-start(bf16[1,2,512,512]{3,2,1,0:T(8,128)(2,1)} %param.10) | copy-start | bytes 3145732
  6.7 10.7 %collective-permute-start.13 = (bf16[32,1024]{1,0:T(8,128)(2,1)S(1)}, bf16[32,1024]{1,0:T(8,128)(2,1)S(1)}, u32[]{:S(2)}, u32[]{:S(2)}) collective-permute-start(bf16[32,1024]{1,0:T(8,128)(2,1)S(1)} %get-tuple-element.21), channel_id=1, source_target_pairs={{0,8},{8,16},{16,24},{24,0},{1,9},{9,17},{17,25},{25,1},{2,10},{10... | collective-permute-start | bytes 196616 | tf_op jit(solution)/shard_map/ppermute | solution.py:405
  9.4 14.2 %collective-permute-start.15 = (bf16[32,1024]{1,0:T(8,128)(2,1)}, bf16[32,1024]{1,0:T(8,128)(2,1)S(1)}, u32[]{:S(2)}, u32[]{:S(2)}) collective-permute-start(bf16[32,1024]{1,0:T(8,128)(2,1)} %get-tuple-element.22), channel_id=1, source_target_pairs={{0,24},{8,0},{16,8},{24,16},{1,25},{9,1},{17,9},{25,17},{2,26},{10... | collective-permute-start | bytes 196616 | tf_op jit(solution)/shard_map/ppermute | solution.py:405
  11.4 12.8 %collective-permute-start.14 = (bf16[32,1024]{1,0:T(8,128)(2,1)}, bf16[32,1024]{1,0:T(8,128)(2,1)}, u32[]{:S(2)}, u32[]{:S(2)}) collective-permute-start(bf16[32,1024]{1,0:T(8,128)(2,1)} %get-tuple-element.23), channel_id=1, source_target_pairs={{0,16},{8,24},{16,0},{24,8},{1,17},{9,25},{17,1},{25,9},{2,18},{10... | collective-permute-start | bytes 196616 | tf_op jit(solution)/shard_map/ppermute | solution.py:405
  12.4 0.7 %copy-start.3 = (s32[2]{0:T(128)S(1)}, s32[2]{0:T(128)}, u32[]{:S(2)}) copy-start(s32[2]{0:T(128)} %index.5) | copy-start | bytes 28
  14.5 0.7 %copy-start.6 = (bf16[2,256,256]{2,1,0:T(8,128)(2,1)}, bf16[2,256,256]{2,1,0:T(8,128)(2,1)S(1)}, u32[]{:S(2)}) copy-start(bf16[2,256,256]{2,1,0:T(8,128)(2,1)S(1)} %get-tuple-element.16) | copy-start | bytes 786436
  15.2 0.7 %copy-start.7 = (bf16[2,256,256]{2,1,0:T(8,128)(2,1)}, bf16[2,256,256]{2,1,0:T(8,128)(2,1)S(1)}, u32[]{:S(2)}) copy-start(bf16[2,256,256]{2,1,0:T(8,128)(2,1)S(1)} %get-tuple-element.13) | copy-start | bytes 786436
  16.0 9.6 %collective-permute-start.1 = (bf16[2,256,256]{2,1,0:T(8,128)(2,1)}, bf16[2,256,256]{2,1,0:T(8,128)(2,1)}, u32[]{:S(2)}, u32[]{:S(2)}) collective-permute-start(bf16[2,256,256]{2,1,0:T(8,128)(2,1)} %get-tuple-element.12), channel_id=1, source_target_pairs={{0,4},{4,0},{1,5},{5,1},{2,6},{6,2},{3,7},{7,3},{8,12},{12,8},{9,1... | collective-permute-start | bytes 786440 | tf_op jit(solution)/shard_map/ppermute | solution.py:359
  17.5 8.2 %collective-permute-start.5 = (bf16[2,256,256]{2,1,0:T(8,128)(2,1)}, bf16[2,256,256]{2,1,0:T(8,128)(2,1)}, u32[]{:S(2)}, u32[]{:S(2)}) collective-permute-start(bf16[2,256,256]{2,1,0:T(8,128)(2,1)} %get-tuple-element.14), channel_id=1, source_target_pairs={{0,2},{1,3},{2,0},{3,1},{4,6},{5,7},{6,4},{7,5},{8,10},{9,11},{10,... | collective-permute-start | bytes 786440 | tf_op jit(solution)/shard_map/ppermute | solution.py:362
  23.6 7.5 %collective-permute-start.3 = (bf16[2,256,256]{2,1,0:T(8,128)(2,1)}, bf16[2,256,256]{2,1,0:T(8,128)(2,1)S(1)}, u32[]{:S(2)}, u32[]{:S(2)}) collective-permute-start(bf16[2,256,256]{2,1,0:T(8,128)(2,1)} %copy-done.7), channel_id=1, source_target_pairs={{0,4},{4,0},{1,5},{5,1},{2,6},{6,2},{3,7},{7,3},{8,12},{12,8},{9,1... | collective-permute-start | bytes 786440 | tf_op jit(solution)/shard_map/ppermute | solution.py:359
  24.2 7.5 %collective-permute-start.9 = (bf16[2,256,256]{2,1,0:T(8,128)(2,1)}, bf16[2,256,256]{2,1,0:T(8,128)(2,1)S(1)}, u32[]{:S(2)}, u32[]{:S(2)}) collective-permute-start(bf16[2,256,256]{2,1,0:T(8,128)(2,1)} %copy-done.6), channel_id=1, source_target_pairs={{0,2},{1,3},{2,0},{3,1},{4,6},{5,7},{6,4},{7,5},{8,10},{9,11},{10,... | collective-permute-start | bytes 786440 | tf_op jit(solution)/shard_map/ppermute | solution.py:362
  25.6 6.1 %collective-permute-start.2 = (bf16[2,256,256]{2,1,0:T(8,128)(2,1)}, bf16[2,256,256]{2,1,0:T(8,128)(2,1)S(1)}, u32[]{:S(2)}, u32[]{:S(2)}) collective-permute-start(bf16[2,256,256]{2,1,0:T(8,128)(2,1)} %collective-permute-done.1.row_own.row1), channel_id=1, source_target_pairs={{0,1},{1,0},{2,3},{3,2},{4,5},{5,4},{6,7},{7,6},{8,9},{9,8},{10,11... | collective-permute-start | bytes 786440 | tf_op jit(solution)/shard_map/ppermute | solution.py:365
  25.7 6.5 %collective-permute-start.6 = (bf16[2,256,256]{2,1,0:T(8,128)(2,1)}, bf16[2,256,256]{2,1,0:T(8,128)(2,1)S(1)}, u32[]{:S(2)}, u32[]{:S(2)}) collective-permute-start(bf16[2,256,256]{2,1,0:T(8,128)(2,1)} %collective-permute-done.5.col_own.col1), channel_id=1, source_target_pairs={{0,1},{1,0},{2,3},{3,2},{4,5},{5,4},{6,7},{7,6},{8,9},{9,8},{10,11... | collective-permute-start | bytes 786440 | tf_op jit(solution)/shard_map/ppermute | solution.py:365
  31.1 4.3 %collective-permute-start.16 = (bf16[2,32,512]{2,1,0:T(8,128)(2,1)S(1)}, bf16[2,32,512]{2,1,0:T(8,128)(2,1)S(1)}, u32[]{:S(2)}, u32[]{:S(2)}) collective-permute-start(bf16[2,32,512]{2,1,0:T(8,128)(2,1)S(1)} %pad_maximum_fusion), channel_id=1, source_target_pairs={{0,4},{4,0},{1,5},{5,1},{2,6},{6,2},{3,7},{7,3},{8,12},{12,8},{9,1... | collective-permute-start | bytes 196616 | tf_op jit(solution)/shard_map/ppermute | solution.py:359
  31.7 8.8 %collective-permute-start.4 = (bf16[2,256,256]{2,1,0:T(8,128)(2,1)S(1)}, bf16[2,256,256]{2,1,0:T(8,128)(2,1)S(1)}, u32[]{:S(2)}, u32[]{:S(2)}) collective-permute-start(bf16[2,256,256]{2,1,0:T(8,128)(2,1)S(1)} %collective-permute-done.3.row2), channel_id=1, source_target_pairs={{0,1},{1,0},{2,3},{3,2},{4,5},{5,4},{6,7},{7,6},{8,9},{9,8},{10,11... | collective-permute-start | bytes 786440 | tf_op jit(solution)/shard_map/ppermute | solution.py:365
  31.7 8.8 %collective-permute-start.10 = (bf16[2,256,256]{2,1,0:T(8,128)(2,1)S(1)}, bf16[2,256,256]{2,1,0:T(8,128)(2,1)S(1)}, u32[]{:S(2)}, u32[]{:S(2)}) collective-permute-start(bf16[2,256,256]{2,1,0:T(8,128)(2,1)S(1)} %collective-permute-done.9.col2), channel_id=1, source_target_pairs={{0,1},{1,0},{2,3},{3,2},{4,5},{5,4},{6,7},{7,6},{8,9},{9,8},{10,11... | collective-permute-start | bytes 786440 | tf_op jit(solution)/shard_map/ppermute | solution.py:365
  33.7 5.5 %collective-permute-start.7 = (bf16[1,256,256]{2,1,0:T(8,128)(2,1)S(1)}, bf16[1,256,256]{2,1,0:T(8,128)(2,1)S(1)}, u32[]{:S(2)}, u32[]{:S(2)}) collective-permute-start(bf16[1,256,256]{2,1,0:T(8,128)(2,1)S(1)} %get-tuple-element.15), channel_id=1, source_target_pairs={{0,4},{4,0},{1,5},{5,1},{2,6},{6,2},{3,7},{7,3},{8,12},{12,8},{9,1... | collective-permute-start | bytes 393224 | tf_op jit(solution)/shard_map/ppermute | solution.py:359
  35.4 5.1 %collective-permute-start.11 = (bf16[1,256,256]{2,1,0:T(8,128)(2,1)S(1)}, bf16[1,256,256]{2,1,0:T(8,128)(2,1)S(1)}, u32[]{:S(2)}, u32[]{:S(2)}) collective-permute-start(bf16[1,256,256]{2,1,0:T(8,128)(2,1)S(1)} %get-tuple-element.17), channel_id=1, source_target_pairs={{0,2},{1,3},{2,0},{3,1},{4,6},{5,7},{6,4},{7,5},{8,10},{9,11},{10,... | collective-permute-start | bytes 393224 | tf_op jit(solution)/shard_map/ppermute | solution.py:362
  39.3 1.3 %collective-permute-start.8 = (bf16[1,256,256]{2,1,0:T(8,128)(2,1)S(1)}, bf16[1,256,256]{2,1,0:T(8,128)(2,1)S(1)}, u32[]{:S(2)}, u32[]{:S(2)}) collective-permute-start(bf16[1,256,256]{2,1,0:T(8,128)(2,1)S(1)} %collective-permute-done.7.row3), channel_id=1, source_target_pairs={{0,1},{1,0},{2,3},{3,2},{4,5},{5,4},{6,7},{7,6},{8,9},{9,8},{10,11... | collective-permute-start | bytes 393224 | tf_op jit(solution)/shard_map/ppermute | solution.py:365
  40.5 1.3 %collective-permute-start.12 = (bf16[1,256,256]{2,1,0:T(8,128)(2,1)S(1)}, bf16[1,256,256]{2,1,0:T(8,128)(2,1)S(1)}, u32[]{:S(2)}, u32[]{:S(2)}) collective-permute-start(bf16[1,256,256]{2,1,0:T(8,128)(2,1)S(1)} %collective-permute-done.11.col3), channel_id=1, source_target_pairs={{0,1},{1,0},{2,3},{3,2},{4,5},{5,4},{6,7},{7,6},{8,9},{9,8},{10,11... | collective-permute-start | bytes 393224 | tf_op jit(solution)/shard_map/ppermute | solution.py:365

commit v2 on v0

v2 whole, which is shorter than its diff:
```python
import jax
import jax.numpy as jnp
from jax import lax
from jax.experimental import pallas as pl
from jax.experimental.pallas import tpu as pltpu
from jax.sharding import PartitionSpec as P

F32 = jnp.float32
BF16 = jnp.bfloat16
VMEM = pl.BlockSpec(memory_space=pltpu.VMEM)
SMEM = pl.BlockSpec(memory_space=pltpu.SMEM)
ANY = pl.BlockSpec(memory_space=pl.ANY)
HBM = pl.BlockSpec(memory_space=pltpu.HBM)
PARAMS = pltpu.CompilerParams(vmem_limit_bytes=24 * 1024 * 1024)
WIDE = pltpu.CompilerParams(vmem_limit_bytes=60 * 1024 * 1024)

OWN, SIB, FIRST, FIRST_SIB, SECOND, SECOND_SIB, THIRD, THIRD_SIB, POOL = 0, 8, 16, 20, 24, 28, 32, 35, 38


def dot(a, b, ca, cb):
    return lax.dot_general(a, b, (((ca,), (cb,)), ((), ())), preferred_element_type=F32)


def pieces(x, count):
    out = []
    for _ in range(count):
        piece = x.astype(BF16)
        out.append(piece)
        x = x - piece.astype(F32)
    return out


def where(cond, a, b):
    return jnp.where(cond, a, b)


class Place:
    def __init__(self, index):
        self.row, self.col = lax.axis_index("row"), lax.axis_index("col")
        self.k, self.y = lax.rem(self.col, 2), lax.div(self.col, 2)
        self.q = [index[0], index[1]]
        self.half = [lax.div(q, 2) for q in self.q]
        self.low = [lax.rem(q, 2) for q in self.q]
        self.equal = self.q[0] == self.q[1]
        self.apart = self.half[0] != self.half[1]
        self.together = jnp.logical_not(self.equal | self.apart)
        self.in_row = [self.row == h for h in self.half]
        self.in_col = [self.y == h for h in self.half]

    def tile(self, panel_low, a, s):
        return 2 * (2 * panel_low + a) + s

    def sends(self, n):
        k = self.k
        s, a = n // 2, n % 2
        low = where(self.apart & (self.half[0] != self.row), self.low[1], self.low[0])
        first = self.low[0] == k
        source = [
            where(first, self.tile(1 - k, 0, 0), self.tile(1 - k, 0, 1)),
            where(first, self.tile(1 - k, 0, 1), self.tile(1 - k, 1, 1)),
            self.tile(k, 0, 0),
            self.tile(k, 1, 1),
        ][n]
        both = where(self.in_row[0], self.tile(1 - k, a, s), 2 * (2 * k + s) + a)
        both = where(self.in_row[0] & self.in_col[0], source, both)
        return where(self.together, both, self.tile(low, a, s))

    def message(self, over_row, k):
        first = k == 0 if over_row else k != 0
        return where(k == self.k, where(first, FIRST, SECOND), where(first, FIRST_SIB, SECOND_SIB))

    def third(self, k):
        return where(k == self.k, THIRD, THIRD_SIB)

    def diagonal(self, over_row, p, i, j):
        if i == j:
            return self.message(over_row, self.low[p]) + 2 + i, jnp.int32(0)
        return self.third(1 if over_row else 0) + self.low[p], jnp.int32(1 if i == 0 else 0)

    def mixed(self, over_row, i, j):
        return self.message(over_row, self.low[i]) + j, jnp.int32(i)

    def pick(self, cond, a, b):
        return where(cond, a[0], b[0]), where(cond, a[1], b[1])

    def rows(self, p, t, s, a):
        here = where(self.q[p] == self.col, OWN, SIB) + 2 * (2 * t + s) + a, jnp.int32(0)
        plain = self.message(False, jnp.int32(t)) + 2 * s + a, jnp.int32(1)
        same = self.diagonal(False, p, s, a)
        if p == 0:
            cross = self.mixed(False, s, a)
        else:
            cross = self.mixed(False, a, s)
            cross = cross[0], 1 - cross[1]
        both = self.pick(self.low[p] == t, same, cross)
        beside = self.pick(self.together, both, plain)
        passed = self.message(True, jnp.int32(t)) + 2 * s + a, jnp.int32(1)
        kept = self.message(False, jnp.int32(t)) + 2 * s + a, jnp.int32(0)
        far = self.pick(self.together & (self.low[p] == t), kept, passed)
        return self.pick(self.in_col[p], here, self.pick(self.in_row[p], beside, far))

    def cols(self, p, a, s):
        here = self.tile(self.low[p], a, s), jnp.int32(0)
        plain = self.message(True, self.k) + 2 * s + a, jnp.int32(0)
        kept = self.message(False, self.k) + 2 * s + a, jnp.int32(1)
        passed = self.pick(self.low[p] == self.k, kept, plain)
        same = self.diagonal(True, p, a, s)
        if p == 0:
            cross = self.mixed(True, s, a)
            cross = cross[0], 1 - cross[1]
        else:
            cross = self.mixed(True, a, s)
        source = self.pick(self.low[p] == self.k, same, cross)
        both = self.pick(self.in_col[p], source, passed)
        far = self.pick(self.together, both, plain)
        return self.pick(self.in_row[p], here, far)

    def cross(self, i, a):
        mine = self.pick(self.low[1] == 0, self.rows(0, 0, i, a), self.rows(0, 1, i, a))
        turned = self.pick(self.low[0] == 0, self.rows(1, 0, a, i), self.rows(1, 1, a, i))
        turned = turned[0], 1 - turned[1]
        equal_near = self.message(True, self.low[1]) + 2 * i + a, jnp.int32(1)
        near = self.pick(self.equal, equal_near, self.mixed(True, i, a))
        equal_far = self.third(self.low[0]) + i + a, jnp.int32(1 if i < a else 0)
        both_far = self.third(self.low[i]) + a, jnp.int32(i)
        far = self.pick(self.equal, equal_far, both_far)
        outside = self.pick(self.in_col[1], near, far)
        return self.pick(self.in_row[1], mine, self.pick(self.in_row[0], turned, outside))


def quarter_of(tile, number, size):
    down = pl.multiple_of(lax.div(number, 2) * size, size)
    along = pl.multiple_of(lax.rem(number, 2) * size, size)
    return tile[pl.ds(down, size), pl.ds(along, size)]


def first_kernel(index_far, working, sent, index, tile, sems):
    copies = [
        pltpu.make_async_copy(index_far, index, sems.at[0]),
        pltpu.make_async_copy(working, tile, sems.at[1]),
    ]
    for copy in copies:
        copy.start()
    copies[0].wait()
    here = Place(index)
    copies[1].wait()
    for n in range(sent.shape[0]):
        sent[n] = quarter_of(tile, here.sends(n), sent.shape[1])


def third_kernel(index, working, sibling, got, _, sent, token, sems):
    here = Place(index)
    size = sent.shape[1]
    source = here.together & here.in_row[0] & here.in_col[0]
    token[...] = jnp.zeros_like(token)

    def far(tile, k, n):
        number = here.tile(k, 1, 0)
        down = pl.ds(pl.multiple_of(lax.div(number, 2) * size, size), size)
        return pltpu.make_async_copy(tile.at[down, pl.ds(0, size)], sent.at[k], sems.at[n])

    @pl.when(source)
    def _():
        far(working, here.k, 0).start()
        far(sibling, 1 - here.k, 1).start()
        far(working, here.k, 0).wait()
        far(sibling, 1 - here.k, 1).wait()

    @pl.when(jnp.logical_not(source))
    def _():
        sent[0] = got[0]
        sent[1] = got[1]

    sent[2] = got[3]


def tie_kernel(_, __, ___):
    pass


TOKEN = jax.ShapeDtypeStruct((8, 128), F32)


def tie(x, *after, params=PARAMS):
    for other in after:
        x = pl.pallas_call(
            tie_kernel,
            out_shape=jax.ShapeDtypeStruct(x.shape, x.dtype),
            in_specs=[ANY, ANY],
            out_specs=ANY,
            input_output_aliases={0: 0},
            compiler_params=params,
        )(x, other)
    return x


def rotate_kernel(obs_far, rotation_far, order_far, _, token, own, *rest):
    sent, (obs, rotation, order, moved, sems) = rest[:-5], rest[-5:]
    pairs = ((order_far, order), (rotation_far, rotation), (obs_far, obs))
    copies = [pltpu.make_async_copy(far, near, sems.at[n]) for n, (far, near) in enumerate(pairs)]
    for copy in copies:
        copy.start()
    row, latent = lax.axis_index("row"), lax.axis_index("latent")
    times, own_vars, stations = obs.shape
    latents, all_vars = rotation.shape
    token[...] = jnp.zeros_like(token)
    copies[0].wait()
    local = order[...] - row * stations
    spread = lax.broadcasted_iota(jnp.int32, (stations, stations), 0) == local
    spread = spread.astype(F32).astype(BF16)
    copies[1].wait()
    shape = (latents * times, times * own_vars)
    left = lax.broadcasted_iota(jnp.int32, shape, 0)
    right = lax.broadcasted_iota(jnp.int32, shape, 1)
    keep = lax.rem(left, times) == lax.div(right, own_vars)
    sel_l = lax.broadcasted_iota(jnp.int32, (latents * times, latents), 0)
    sel_l = lax.div(sel_l, times) == lax.broadcasted_iota(jnp.int32, (latents * times, latents), 1)
    pick_v = lax.broadcasted_iota(jnp.int32, (all_vars, times * own_vars), 1)
    pick_v = lax.rem(pick_v, own_vars) + latent * own_vars
    pick_v = pick_v == lax.broadcasted_iota(jnp.int32, (all_vars, times * own_vars), 0)
    sel_l = sel_l.astype(F32).astype(BF16)
    pick_v = pick_v.astype(F32).astype(BF16)
    lefts = []
    for piece in pieces(rotation[...], 3):
        wide = dot(sel_l, piece, 1, 0).astype(BF16)
        wide = dot(wide, pick_v, 1, 0)
        lefts.append(jnp.where(keep, wide, 0.0).astype(BF16))
    copies[2].wait()
    flat = obs[...].reshape(times * own_vars, stations)
    total = sum(dot(wide, flat, 1, 0) for wide in lefts)
    moved[...] = dot(total.astype(BF16), spread, 1, 0).reshape(moved.shape)
    own[...] = moved[latent]
    for shift, out in enumerate(sent, 1):
        out[...] = moved[lax.rem(latent + shift, latents)].astype(BF16)


def field_kernel(index, _, own, *rest):
    got, (field, rhs) = rest[:-2], rest[-2:]
    total = own[...]
    for part in got:
        total = total + part[...].astype(F32)
    field[...] = total
    width = rhs.shape[2]
    for p in range(rhs.shape[0]):
        inside = pl.ds(pl.multiple_of(lax.rem(index[p], 2) * width, width), width)
        rhs[p] = field[:, inside].astype(BF16)


def entries_of(here):
    entries = []
    for p in range(2):
        entries += [here.rows(p, n // 4, n // 2 % 2, n % 2) for n in range(8)]
    for p in range(2):
        entries += [here.cols(p, n // 2, n % 2) for n in range(4)]
    return entries + [here.cross(n // 2, n % 2) for n in range(4)]


def is_late(slot):
    return slot >= SECOND


def assemble(blocks, size, table, flip, wanted, load, earlier=None):
    def step(n, _):
        for side in range(2):
            slot = table[2 * n + side]
            turn = flip[2 * n + side]
            down = pl.ds(pl.multiple_of(n * size, size), size)
            along = pl.ds(side * size, size)

            if earlier is not None:

                @pl.when(jnp.logical_not(wanted(slot)))
                def _():
                    blocks[down, along] = earlier[down, along]

            @pl.when(wanted(slot) & (turn == 0))
            def _():
                blocks[down, along] = load(slot)

            @pl.when(wanted(slot) & (turn != 0))
            def _():
                blocks[down, along] = load(slot).T

        return 0

    lax.fori_loop(0, blocks.shape[0] // size, step, 0)


def early_kernel(index, working, sibling, first, first_sib, _, blocks, table, flip, pool):
    here = Place(index)
    size = pool.shape[1]
    for n, (slot, turn) in enumerate(entries_of(here)):
        table[n] = slot
        flip[n] = turn

    def tiles(n, _):
        down = pl.ds(pl.multiple_of(n * size, size), size)
        for side in range(2):
            along = pl.ds(side * size, size)
            pool[OWN + 2 * n + side] = working[down, along]
            pool[SIB + 2 * n + side] = sibling[down, along]
        return 0

    lax.fori_loop(0, working.shape[0] // size, tiles, 0)
    pool[pl.ds(FIRST, 4)] = first[...]
    pool[pl.ds(FIRST_SIB, 4)] = first_sib[...]
    assemble(blocks, size, table, flip, lambda slot: jnp.logical_not(is_late(slot)), lambda slot: pool[slot])


def factor_kernel(
    index, table, flip, working, earlier, second, second_sib, third, third_sib,
    inverse, field, rhs_far, trailing, panels, whitened,
    blocks, pool, factors0, factors1, turned0, turned1, rhs_near, result, sems,
):
    here = Place(index)
    size = pool.shape[1]
    tall, wide = working.shape
    width = inverse.shape[1]
    share = panels.shape[2]

    base = 0
    for ref in (second, second_sib, third, third_sib):
        pool[pl.ds(base, ref.shape[0])] = ref[...]
        base += ref.shape[0]

    def load(slot):
        return pool[slot - SECOND]

    assemble(blocks, size, table, flip, is_late, load, earlier)

    rows0, rows1 = pl.ds(0, tall), pl.ds(tall, tall)
    cols0, cols1 = pl.ds(2 * tall, width), pl.ds(2 * tall + width, width)
    cross = pl.ds(2 * tall + 2 * width, width)
    inv0, inv1 = inverse[0], inverse[1]

    factors0[pl.ds(tall, width)] = dot(blocks[cross], inv0, 1, 1).astype(BF16)
    turned0[...] = dot(inv0, blocks[cols0], 1, 0).astype(BF16)
    factors0[rows0] = dot(blocks[rows0], inv0, 1, 1).astype(BF16)
    mixed = factors0[pl.ds(tall, width)]

    got = blocks[cols1].astype(F32) - dot(mixed, turned0[...], 1, 0)
    turned1[...] = dot(inv1, got.astype(BF16), 1, 0).astype(BF16)
    got = blocks[rows1].astype(F32) - dot(factors0[rows0], mixed, 1, 1)
    factors1[...] = dot(got.astype(BF16), inv1, 1, 1).astype(BF16)

    lanes = pl.ds(pl.multiple_of(here.col * share, share), share)
    copies = [
        pltpu.make_async_copy(factors0.at[rows0, lanes], panels.at[0], sems.at[0]),
        pltpu.make_async_copy(factors1.at[:, lanes], panels.at[1], sems.at[1]),
    ]
    copies[0].start()
    copies[1].start()
    parts = sems.shape[0] - 2
    for n in range(parts):
        down = pl.ds(n * tall // parts, tall // parts)
        change = dot(factors0[down], turned0[...], 1, 0) + dot(factors1[down], turned1[...], 1, 0)
        result[down] = working[down].astype(F32) - change
        copies.append(pltpu.make_async_copy(result.at[down], trailing.at[down], sems.at[2 + n]))
        copies[-1].start()

    for p in range(2):
        inside = pl.ds(pl.multiple_of(here.low[p] * width, width), width)

        @pl.when(here.in_row[p])
        def _():
            rhs_near[p] = field[:, inside]

        @pl.when(jnp.logical_not(here.in_row[p]))
        def _():
            rhs_near[p] = rhs_far[p].astype(F32)

    def solve(rhs, inv):
        return sum(dot(piece, inv, 1, 1) for piece in pieces(rhs, 2)).astype(BF16)

    solved0 = solve(rhs_near[0], inv0)
    solved1 = solve(rhs_near[1] - dot(solved0, mixed, 1, 1), inv1)
    whitened[...] = field[...] - dot(solved0, factors0[rows0], 1, 1) - dot(solved1, factors1[...], 1, 1)
    for copy in copies:
        copy.wait()


def local(observations, rotation, ordering, working, factor_inverse, panel_index):
    latents = rotation.shape[1]
    latent_count = lax.axis_size("latent")
    times, own_vars, stations = observations.shape
    matrix = working[0]
    inverse = factor_inverse[0]
    tall, wide = matrix.shape
    panel_count, width, _ = inverse.shape
    size = width // 2
    share = width // lax.axis_size("col")

    cols = lax.axis_size("col")

    def across_rows(x):
        return lax.ppermute(x, "row", [(0, 1), (1, 0)])

    def siblings(x):
        return lax.ppermute(x, "col", [(i, i ^ 1) for i in range(cols)])

    def neighbours(x, row_first):
        pairs = []
        for i in range(2):
            for j in range(cols):
                over_row = (j % 2 == 0) == row_first
                to = (1 - i, j) if over_row else (i, j ^ 2)
                pairs.append((i * cols + j, to[0] * cols + to[1]))
        return lax.ppermute(x, ("row", "col"), pairs)

    message = jax.ShapeDtypeStruct((4, size, size), BF16)
    extra = jax.ShapeDtypeStruct((3, size, size), BF16)
    sibling = siblings(matrix)
    sent_message = pl.pallas_call(
        first_kernel,
        out_shape=message,
        in_specs=[ANY] * 2,
        out_specs=VMEM,
        scratch_shapes=[
            pltpu.SMEM((2,), jnp.int32),
            pltpu.VMEM(matrix.shape, BF16),
            pltpu.SemaphoreType.DMA((2,)),
        ],
        compiler_params=WIDE,
    )(panel_index, matrix)
    first = neighbours(sent_message, True)

    token, own, *sent = pl.pallas_call(
        rotate_kernel,
        out_shape=[TOKEN, jax.ShapeDtypeStruct((times, stations), F32)]
        + [jax.ShapeDtypeStruct((times, stations), BF16)] * (latent_count - 1),
        in_specs=[ANY] * 4,
        out_specs=[VMEM] * (1 + latent_count),
        scratch_shapes=[
            pltpu.VMEM(observations.shape, BF16),
            pltpu.VMEM(rotation.shape[::-1], F32),
            pltpu.VMEM((1, stations), jnp.int32),
            pltpu.VMEM((latents, times, stations), F32),
            pltpu.SemaphoreType.DMA((3,)),
        ],
        compiler_params=WIDE,
    )(observations, rotation.T, ordering[None], sent_message)
    second = neighbours(tie(sent_message, token, params=WIDE), False)
    got = []
    for shift, part in enumerate(sent, 1):
        pairs = [(i, (i + shift) % latent_count) for i in range(latent_count)]
        got.append(lax.ppermute(part, "latent", pairs))

    first_sib = siblings(first)
    sent_third, third_token = pl.pallas_call(
        third_kernel,
        out_shape=(extra, TOKEN),
        in_specs=[SMEM, ANY, ANY, VMEM, ANY],
        out_specs=(VMEM, VMEM),
        scratch_shapes=[pltpu.SemaphoreType.DMA((2,))],
        compiler_params=PARAMS,
    )(panel_index, matrix, sibling, first, token)
    third = neighbours(sent_third, False)

    field, rhs = pl.pallas_call(
        field_kernel,
        out_shape=(
            jax.ShapeDtypeStruct((times, stations), F32),
            jax.ShapeDtypeStruct((panel_count, times, width), BF16),
        ),
        in_specs=[SMEM, ANY] + [VMEM] * latent_count,
        out_specs=(VMEM, VMEM),
        compiler_params=PARAMS,
    )(panel_index, token, own, *got)
    rhs_far = across_rows(rhs)

    second = tie(second, third_token, rhs)
    second_sib, third_sib = siblings(second), siblings(third)

    block_shape = jax.ShapeDtypeStruct((14 * size, width), BF16)
    table_shape = jax.ShapeDtypeStruct((28,), jnp.int32)
    blocks, table, flip = pl.pallas_call(
        early_kernel,
        out_shape=(block_shape, table_shape, table_shape),
        in_specs=[SMEM] + [VMEM] * 4 + [ANY],
        out_specs=(VMEM, SMEM, SMEM),
        scratch_shapes=[pltpu.VMEM((POOL, size, size), BF16)],
        compiler_params=PARAMS,
    )(panel_index, matrix, sibling, first, first_sib, third_token)

    trailing, panels, whitened = pl.pallas_call(
        factor_kernel,
        out_shape=(
            jax.ShapeDtypeStruct((tall, wide), F32),
            jax.ShapeDtypeStruct((panel_count, tall, share), BF16),
            jax.ShapeDtypeStruct((times, stations), F32),
        ),
        in_specs=[SMEM] * 3 + [VMEM] * 9,
        out_specs=(HBM, HBM, VMEM),
        scratch_shapes=[
            pltpu.VMEM(block_shape.shape, BF16),
            pltpu.VMEM((POOL - SECOND, size, size), BF16),
            pltpu.VMEM((tall + width, width), BF16),
            pltpu.VMEM((tall, width), BF16),
            pltpu.VMEM((width, wide), BF16),
            pltpu.VMEM((width, wide), BF16),
            pltpu.VMEM((panel_count, times, width), F32),
            pltpu.VMEM((tall, wide), F32),
            pltpu.SemaphoreType.DMA((4,)),
        ],
        compiler_params=PARAMS,
    )(
        panel_index, table, flip, matrix, blocks, second, second_sib, third, third_sib,
        inverse, field, rhs_far,
    )
    return trailing[None], panels[None], whitened[None]


def solution(mesh):
    return jax.shard_map(
        local,
        mesh=mesh,
        in_specs=(
            P("col", "latent", "row"),
            P(),
            P("row"),
            P("latent", "row", "col"),
            P("latent", None, None, None),
            P(),
        ),
        out_specs=(
            P("latent", "row", "col"),
            P("latent", None, "row", "col"),
            P("latent", "col", "row"),
        ),
        check_vma=False,
    )
```

time: 169 us -> 40.1 us (0.24)
  waiting for transfers between devices: 95.9 us -> 7.28 us
  matrix products: 22.5 us -> 0 us
  Pallas kernels: 0 us -> 17.4 us
  blocking collectives: 17 us -> 0 us
  between operations: 16.8 us -> 0.77 us
  starting transfers between devices: 0.21 us -> 13.6 us
  local copies, waits for them, and re-layouts: 14 us -> 0.71 us
  other arithmetic: 1.78 us -> 0 us
    psum x4 -> x0, waiting for transfers between devices: 95.8 us -> none  [spread(): return lax.psum(kept, axis)]
    dot_general x11 -> x0, matrix products: 22.5 us -> none  [the longest x2 5.94 us: local(): lax.dot_general(row_panel, col_panel, (((1,), (1,)), ((), ())), preferred...]
    pallas_call x0 -> x9, Pallas kernels: none -> 17.4 us  [the longest x1 8.14 us: local(): pl.pallas_call(factor_kernel, out_shape=(jax.ShapeDtypeStruct((tall, wide...]
    psum x2 -> x0, blocking collectives: 17 us -> none  [spread(): return lax.psum(kept, axis)]
    ppermute x0 -> x11, starting transfers between devices: none -> 13.6 us  [the longest x3 5.92 us: local(): got.append(lax.ppermute(part, 'latent', pairs))]
    ppermute x0 -> x11, waiting for transfers between devices: none -> 7.28 us  [the longest x3 3.84 us: neighbours(): return lax.ppermute(x, ('row', 'col'), pairs)]
    gather x2 -> x0, local copies, waits for them, and re-layouts: 6.92 us -> none  [local(): latent_field = jnp.take(latent_field, local_order, axis=1)]
    another operation x2 -> x0, local copies, waits for them, and re-layouts: 1.94 us -> none  [local(): return (matrix[None], jnp.stack(shares)[None], latent_field[None])]
  transfers between devices with their start and end apart: 5 -> 11, of which waited for: 4 -> 5; matrix products, arithmetic and copies ran while one was open for 17% -> 0% of each run, Pallas kernels for 0% -> 23%
where the time goes in v2:
time: 40.1 us; the launch traced here: 39.8 us
  Pallas kernels  17.4 us (43%)
  starting transfers between devices  13.6 us (34%)
  waiting for transfers between devices  7.28 us (18%)
  between operations  0.77 us (2%)
  local copies, waits for them, and re-layouts  0.71 us (2%)
    pallas_call x1, Pallas kernels, local(): pl.pallas_call(factor_kernel, out_shape=(jax.ShapeDtypeStruct((tall, wide...  8.14 us
    ppermute x3, starting transfers between devices, local(): got.append(lax.ppermute(part, 'latent', pairs))  5.92 us
    ppermute x3, starting transfers between devices, neighbours(): return lax.ppermute(x, ('row', 'col'), pairs)  4.85 us
    ppermute x3, waiting for transfers between devices, neighbours(): return lax.ppermute(x, ('row', 'col'), pairs)  3.84 us
    pallas_call x1, Pallas kernels, local(): pl.pallas_call(rotate_kernel, out_shape=[TOKEN, jax.ShapeDtypeStruct((tim...  3.48 us
    ppermute x3, waiting for transfers between devices, local(): got.append(lax.ppermute(part, 'latent', pairs))  3.22 us
    pallas_call x1, Pallas kernels, local(): pl.pallas_call(early_kernel, out_shape=(block_shape, table_shape, table_s...  2.54 us
    pallas_call x1, Pallas kernels, local(): pl.pallas_call(first_kernel, out_shape=message, in_specs=[ANY] * 2, out_s...  2.07 us
  transfers between devices with their start and end apart: 11, of which 5 were waited for; matrix products, arithmetic and copies ran while one was open for 0% of the time, Pallas kernels for 23%

profile of v2, /device:TPU:0, one launch (start us, length us, event | category | flops | bytes accessed | tf_op | source)
XLA Modules:
  0.0 39.8 jit_solution(10459769859395274248)
XLA Ops:
  0.6 0.0 copy-start
  0.6 0.0 copy-start.4
  0.7 0.5 %collective-permute-start = (bf16[1024,512]{1,0:T(8,128)(2,1)}, bf16[1024,512]{1,0:T(8,128)(2,1)S(1)}, u32[]{:S(2)}, u32[]{:S(2)}) collective-permute-start(bf16[1024,512]{1,0:T(8,128)(2,1)} %bitcast.7), channel_id=1, source_target_pairs={{0,1},{1,0},{2,3},{3,2},{4,5},{5,4},{6,7},{7,6},{8,9},{9,8},{10,11... | collective-permute-start | bytes 3145736 | tf_op jit(solution)/shard_map/ppermute | solution.py:399
  1.2 2.1 %shard_map.85._ = bf16[4,256,256]{2,1,0:T(8,128)(2,1)} custom-call(s32[2]{0:T(128)} %index.7, bf16[1024,512]{1,0:T(8,128)(2,1)} %bitcast.8), custom_call_target="tpu_custom_call" | custom-call | tf_op jit(solution)/shard_map/pallas_call | solution.py:413
  3.2 2.6 %collective-permute-start.1 = (bf16[4,256,256]{2,1,0:T(8,128)(2,1)}, bf16[4,256,256]{2,1,0:T(8,128)(2,1)S(1)}, u32[]{:S(2)}, u32[]{:S(2)}) collective-permute-start(bf16[4,256,256]{2,1,0:T(8,128)(2,1)} %shard_map.85._), channel_id=1, source_target_pairs={{0,4},{1,3},{2,6},{3,1},{4,0},{5,7},{6,2},{7,5},{8,12},{9,11},{10,... | collective-permute-start | bytes 1572872 | tf_op jit(solution)/shard_map/ppermute | solution.py:408
  5.9 3.5 %shard_map.86 = (f32[8,128]{1,0:T(8,128)}, f32[32,1024]{1,0:T(8,128)}, bf16[32,1024]{1,0:T(8,128)(2,1)}, bf16[32,1024]{1,0:T(8,128)(2,1)}, bf16[32,1024]{1,0:T(8,128)(2,1)}) custom-call(bf16[32,16,1024]{2,1,0:T(8,128)(2,1)} %obs_far.1, f32[4,64]{1,0:T(4,128)} %bitcast.14, s32[1,1024]{1,0:T(1,128)} %bitcast.13, bf16[4,256,256]{2,1,0:T(8,128)(2,1)} %shard_map.85._), custom_call_target="tpu_custom_call" | custom-call | tf_op jit(solution)/shard_map/pallas_call | solution.py:427
  9.4 0.0 copy-start.7
  9.4 0.0 copy-start.6
  9.4 0.0 copy-start.5
  9.4 0.0 copy-start.2
  9.4 3.8 %collective-permute-done.1.got.first = bf16[4,256,256]{2,1,0:T(8,128)(2,1)S(1)} collective-permute-done((bf16[4,256,256]{2,1,0:T(8,128)(2,1)}, bf16[4,256,256]{2,1,0:T(8,128)(2,1)S(1)}, u32[]{:S(2)}, u32[]{:S(2)}) %collective-permute-start.1) | collective-permute-done | bytes 524320 | tf_op jit(solution)/shard_map/ppermute | solution.py:408
  13.3 0.0 copy-start.1
  13.3 2.0 %collective-permute-start.3 = (bf16[4,256,256]{2,1,0:T(8,128)(2,1)}, bf16[4,256,256]{2,1,0:T(8,128)(2,1)S(1)}, u32[]{:S(2)}, u32[]{:S(2)}) collective-permute-start(bf16[4,256,256]{2,1,0:T(8,128)(2,1)} %shard_map.89), channel_id=1, source_target_pairs={{0,2},{1,5},{2,0},{3,7},{4,6},{5,1},{6,4},{7,3},{8,10},{9,13},{10,... | collective-permute-start | bytes 1572872 | tf_op jit(solution)/shard_map/ppermute | solution.py:408
  15.3 0.0 collective-permute-done.sibling
  15.3 0.0 copy-done
  15.3 0.0 copy-done.4
  15.3 0.0 copy-start.3
  15.3 0.7 %copy-done.3 = f32[8,128]{1,0:T(8,128)S(1)} copy-done((f32[8,128]{1,0:T(8,128)S(1)}, f32[8,128]{1,0:T(8,128)}, u32[]{:S(2)}) %copy-start.3) | copy-done | bytes 4120
  16.0 0.6 %shard_map.87 = (bf16[3,256,256]{2,1,0:T(8,128)(2,1)S(1)}, f32[8,128]{1,0:T(8,128)S(1)}) custom-call(s32[2]{0:T(128)S(1)} %copy-done.4, bf16[1024,512]{1,0:T(8,128)(2,1)S(1)} %bitcast.9, bf16[1024,512]{1,0:T(8,128)(2,1)S(1)} %collective-permute-done.sibling, bf16[4,256,256]{2,1,0:T(8,128)(2,1)S(1)} %collective-permute-done.1.got.first, f32[8,128]{1,0:T(8,128)S(1)} %copy-done.3), custom_call_target="tpu_custom_call" | custom-call | tf_op jit(solution)/shard_map/pallas_call | solution.py:449
  16.6 0.2 collective-permute-start.8
  16.8 0.0 copy-done.7
  16.8 2.0 %collective-permute-start.4 = (bf16[32,1024]{1,0:T(8,128)(2,1)S(1)}, bf16[32,1024]{1,0:T(8,128)(2,1)S(1)}, u32[]{:S(2)}, u32[]{:S(2)}) collective-permute-start(bf16[32,1024]{1,0:T(8,128)(2,1)S(1)} %copy-done.7), channel_id=1, source_target_pairs={{0,8},{8,16},{16,24},{24,0},{1,9},{9,17},{17,25},{25,1},{2,10},{10... | collective-permute-start | bytes 196616 | tf_op jit(solution)/shard_map/ppermute | solution.py:446
  18.8 0.0 copy-done.6
  18.8 2.6 %collective-permute-start.5 = (bf16[32,1024]{1,0:T(8,128)(2,1)S(1)}, bf16[32,1024]{1,0:T(8,128)(2,1)S(1)}, u32[]{:S(2)}, u32[]{:S(2)}) collective-permute-start(bf16[32,1024]{1,0:T(8,128)(2,1)S(1)} %copy-done.6), channel_id=1, source_target_pairs={{0,16},{8,24},{16,0},{24,8},{1,17},{9,25},{17,1},{25,9},{2,18},{10... | collective-permute-start | bytes 196616 | tf_op jit(solution)/shard_map/ppermute | solution.py:446
  21.4 0.0 copy-done.5
  21.4 1.3 %collective-permute-start.6 = (bf16[32,1024]{1,0:T(8,128)(2,1)S(1)}, bf16[32,1024]{1,0:T(8,128)(2,1)S(1)}, u32[]{:S(2)}, u32[]{:S(2)}) collective-permute-start(bf16[32,1024]{1,0:T(8,128)(2,1)S(1)} %copy-done.5), channel_id=1, source_target_pairs={{0,24},{8,0},{16,8},{24,16},{1,25},{9,1},{17,9},{25,17},{2,26},{10... | collective-permute-start | bytes 196616 | tf_op jit(solution)/shard_map/ppermute | solution.py:446
  22.7 1.1 %collective-permute-done.4.rest_0_ = bf16[32,1024]{1,0:T(8,128)(2,1)S(1)} collective-permute-done((bf16[32,1024]{1,0:T(8,128)(2,1)S(1)}, bf16[32,1024]{1,0:T(8,128)(2,1)S(1)}, u32[]{:S(2)}, u32[]{:S(2)}) %collective-permute-start.4) | collective-permute-done | bytes 65568 | tf_op jit(solution)/shard_map/ppermute | solution.py:446
  23.8 1.9 %collective-permute-done.5.rest_1_ = bf16[32,1024]{1,0:T(8,128)(2,1)S(1)} collective-permute-done((bf16[32,1024]{1,0:T(8,128)(2,1)S(1)}, bf16[32,1024]{1,0:T(8,128)(2,1)S(1)}, u32[]{:S(2)}, u32[]{:S(2)}) %collective-permute-start.5) | collective-permute-done | bytes 65568 | tf_op jit(solution)/shard_map/ppermute | solution.py:446
  25.7 0.2 collective-permute-done.6.rest_2_
  25.9 0.0 copy-done.2
  25.9 0.6 %shard_map.91 = (f32[32,1024]{1,0:T(8,128)S(1)}, bf16[2,32,512]{2,1,0:T(8,128)(2,1)S(1)}) custom-call(s32[2]{0:T(128)S(1)} %copy-done.4, f32[8,128]{1,0:T(8,128)S(1)} %copy-done.3, f32[32,1024]{1,0:T(8,128)S(1)} %copy-done.2, bf16[32,1024]{1,0:T(8,128)(2,1)S(1)} %collective-permute-done.4.rest_0_, bf16[32,1024]{1,0:T(8,128)(2,1)S(1)} %collective-permute-done.5.rest_1_, ...), custom_call_target="tpu_custom_call" | custom-call | tf_op jit(solution)/shard_map/pallas_call | solution.py:459
  26.5 0.1 collective-permute-start.2
  26.6 0.0 collective-permute-done.3._
  26.6 0.5 %collective-permute-start.7 = (bf16[4,256,256]{2,1,0:T(8,128)(2,1)S(1)}, bf16[4,256,256]{2,1,0:T(8,128)(2,1)S(1)}, u32[]{:S(2)}, u32[]{:S(2)}) collective-permute-start(bf16[4,256,256]{2,1,0:T(8,128)(2,1)S(1)} %shard_map.92.second), channel_id=1, source_target_pairs={{0,1},{1,0},{2,3},{3,2},{4,5},{5,4},{6,7},{7,6},{8,9},{9,8},{10,11... | collective-permute-start | bytes 1572872 | tf_op jit(solution)/shard_map/ppermute | solution.py:399
  27.1 0.0 collective-permute-done.8.third
  27.1 0.1 collective-permute-start.9
  27.2 1.7 %collective-permute-start.10 = (bf16[2,32,512]{2,1,0:T(8,128)(2,1)S(1)}, bf16[2,32,512]{2,1,0:T(8,128)(2,1)S(1)}, u32[]{:S(2)}, u32[]{:S(2)}) collective-permute-start(bf16[2,32,512]{2,1,0:T(8,128)(2,1)S(1)} %get-tuple-element.27.__), channel_id=1, source_target_pairs={{0,4},{4,0},{1,5},{5,1},{2,6},{6,2},{3,7},{7,3},{8,12},{12,8},{9,1... | collective-permute-start | bytes 196616 | tf_op jit(solution)/shard_map/ppermute | solution.py:396
  28.9 0.0 collective-permute-done.2.first_sib
  28.9 2.5 %shard_map.88 = (bf16[3584,512]{1,0:T(8,128)(2,1)S(1)}, s32[28]{0:T(128)S(1)}, s32[28]{0:T(128)S(1)}) custom-call(s32[2]{0:T(128)S(1)} %copy-done.4, bf16[1024,512]{1,0:T(8,128)(2,1)S(1)} %bitcast.10, bf16[1024,512]{1,0:T(8,128)(2,1)S(1)} %collective-permute-done.sibling, bf16[4,256,256]{2,1,0:T(8,128)(2,1)S(1)} %collective-permute-done.1.got.first, ...), custom_call_target="tpu_custom_call" | custom-call | tf_op jit(solution)/shard_map/pallas_call | solution.py:476
  31.4 0.2 collective-permute-done.10.rhs_far
  31.6 0.0 collective-permute-done.7.second_sib
  31.6 0.0 collective-permute-done.9.third_sib
  31.7 0.0 copy-done.1
  31.7 8.1 %shard_map.93 = (f32[1024,512]{1,0:T(8,128)}, bf16[2,1024,128]{2,1,0:T(8,128)(2,1)}, f32[32,1024]{1,0:T(8,128)}) custom-call(s32[2]{0:T(128)S(1)} %copy-done.4, s32[28]{0:T(128)S(1)} %get-tuple-element.20.table, s32[28]{0:T(128)S(1)} %get-tuple-element.21.flip, bf16[1024,512]{1,0:T(8,128)(2,1)S(1)} %bitcast.11, ...), custom_call_target="tpu_custom_call" | custom-call | tf_op jit(solution)/shard_map/pallas_call | solution.py:485
  (3 shorter events, 0.0 us)
Async XLA Ops:
  0.6 14.7 %copy-start = (bf16[1,1024,512]{2,1,0:T(8,128)(2,1)S(1)}, bf16[1,1024,512]{2,1,0:T(8,128)(2,1)}, u32[]{:S(2)}) copy-start(bf16[1,1024,512]{2,1,0:T(8,128)(2,1)} %param.9) | copy-start | bytes 3145732
  0.6 14.7 %copy-start.4 = (s32[2]{0:T(128)S(1)}, s32[2]{0:T(128)}, u32[]{:S(2)}) copy-start(s32[2]{0:T(128)} %index.7) | copy-start | bytes 28
  0.7 14.7 %collective-permute-start = (bf16[1024,512]{1,0:T(8,128)(2,1)}, bf16[1024,512]{1,0:T(8,128)(2,1)S(1)}, u32[]{:S(2)}, u32[]{:S(2)}) collective-permute-start(bf16[1024,512]{1,0:T(8,128)(2,1)} %bitcast.7), channel_id=1, source_target_pairs={{0,1},{1,0},{2,3},{3,2},{4,5},{5,4},{6,7},{7,6},{8,9},{9,8},{10,11... | collective-permute-start | bytes 3145736 | tf_op jit(solution)/shard_map/ppermute | solution.py:399
  3.2 10.0 %collective-permute-start.1 = (bf16[4,256,256]{2,1,0:T(8,128)(2,1)}, bf16[4,256,256]{2,1,0:T(8,128)(2,1)S(1)}, u32[]{:S(2)}, u32[]{:S(2)}) collective-permute-start(bf16[4,256,256]{2,1,0:T(8,128)(2,1)} %shard_map.85._), channel_id=1, source_target_pairs={{0,4},{1,3},{2,6},{3,1},{4,0},{5,7},{6,2},{7,5},{8,12},{9,11},{10,... | collective-permute-start | bytes 1572872 | tf_op jit(solution)/shard_map/ppermute | solution.py:408
  9.4 7.4 %copy-start.7 = (bf16[32,1024]{1,0:T(8,128)(2,1)S(1)}, bf16[32,1024]{1,0:T(8,128)(2,1)}, u32[]{:S(2)}) copy-start(bf16[32,1024]{1,0:T(8,128)(2,1)} %get-tuple-element.24) | copy-start | bytes 196612
  9.4 9.4 %copy-start.6 = (bf16[32,1024]{1,0:T(8,128)(2,1)S(1)}, bf16[32,1024]{1,0:T(8,128)(2,1)}, u32[]{:S(2)}) copy-start(bf16[32,1024]{1,0:T(8,128)(2,1)} %get-tuple-element.25) | copy-start | bytes 196612
  9.4 12.0 %copy-start.5 = (bf16[32,1024]{1,0:T(8,128)(2,1)S(1)}, bf16[32,1024]{1,0:T(8,128)(2,1)}, u32[]{:S(2)}) copy-start(bf16[32,1024]{1,0:T(8,128)(2,1)} %get-tuple-element.26) | copy-start | bytes 196612
  9.4 16.5 %copy-start.2 = (f32[32,1024]{1,0:T(8,128)S(1)}, f32[32,1024]{1,0:T(8,128)}, u32[]{:S(2)}) copy-start(f32[32,1024]{1,0:T(8,128)} %get-tuple-element.23.own) | copy-start | bytes 393220
  13.3 18.4 %copy-start.1 = (bf16[1,2,512,512]{3,2,1,0:T(8,128)(2,1)S(1)}, bf16[1,2,512,512]{3,2,1,0:T(8,128)(2,1)}, u32[]{:S(2)}) copy-start(bf16[1,2,512,512]{3,2,1,0:T(8,128)(2,1)} %param.10) | copy-start | bytes 3145732
  13.3 13.4 %collective-permute-start.3 = (bf16[4,256,256]{2,1,0:T(8,128)(2,1)}, bf16[4,256,256]{2,1,0:T(8,128)(2,1)S(1)}, u32[]{:S(2)}, u32[]{:S(2)}) collective-permute-start(bf16[4,256,256]{2,1,0:T(8,128)(2,1)} %shard_map.89), channel_id=1, source_target_pairs={{0,2},{1,5},{2,0},{3,7},{4,6},{5,1},{6,4},{7,3},{8,10},{9,13},{10,... | collective-permute-start | bytes 1572872 | tf_op jit(solution)/shard_map/ppermute | solution.py:408
  15.3 0.7 %copy-start.3 = (f32[8,128]{1,0:T(8,128)S(1)}, f32[8,128]{1,0:T(8,128)}, u32[]{:S(2)}) copy-start(f32[8,128]{1,0:T(8,128)} %get-tuple-element.18._.__) | copy-start | bytes 12292
  16.6 10.5 %collective-permute-start.8 = (bf16[3,256,256]{2,1,0:T(8,128)(2,1)S(1)}, bf16[3,256,256]{2,1,0:T(8,128)(2,1)S(1)}, u32[]{:S(2)}, u32[]{:S(2)}) collective-permute-start(bf16[3,256,256]{2,1,0:T(8,128)(2,1)S(1)} %get-tuple-element.28), channel_id=1, source_target_pairs={{0,2},{1,5},{2,0},{3,7},{4,6},{5,1},{6,4},{7,3},{8,10},{9,13},{10,... | collective-permute-start | bytes 1179656 | tf_op jit(solution)/shard_map/ppermute | solution.py:408
  16.8 7.0 %collective-permute-start.4 = (bf16[32,1024]{1,0:T(8,128)(2,1)S(1)}, bf16[32,1024]{1,0:T(8,128)(2,1)S(1)}, u32[]{:S(2)}, u32[]{:S(2)}) collective-permute-start(bf16[32,1024]{1,0:T(8,128)(2,1)S(1)} %copy-done.7), channel_id=1, source_target_pairs={{0,8},{8,16},{16,24},{24,0},{1,9},{9,17},{17,25},{25,1},{2,10},{10... | collective-permute-start | bytes 196616 | tf_op jit(solution)/shard_map/ppermute | solution.py:446
  18.8 6.9 %collective-permute-start.5 = (bf16[32,1024]{1,0:T(8,128)(2,1)S(1)}, bf16[32,1024]{1,0:T(8,128)(2,1)S(1)}, u32[]{:S(2)}, u32[]{:S(2)}) collective-permute-start(bf16[32,1024]{1,0:T(8,128)(2,1)S(1)} %copy-done.6), channel_id=1, source_target_pairs={{0,16},{8,24},{16,0},{24,8},{1,17},{9,25},{17,1},{25,9},{2,18},{10... | collective-permute-start | bytes 196616 | tf_op jit(solution)/shard_map/ppermute | solution.py:446
  21.4 4.6 %collective-permute-start.6 = (bf16[32,1024]{1,0:T(8,128)(2,1)S(1)}, bf16[32,1024]{1,0:T(8,128)(2,1)S(1)}, u32[]{:S(2)}, u32[]{:S(2)}) collective-permute-start(bf16[32,1024]{1,0:T(8,128)(2,1)S(1)} %copy-done.5), channel_id=1, source_target_pairs={{0,24},{8,0},{16,8},{24,16},{1,25},{9,1},{17,9},{25,17},{2,26},{10... | collective-permute-start | bytes 196616 | tf_op jit(solution)/shard_map/ppermute | solution.py:446
  26.5 2.4 %collective-permute-start.2 = (bf16[4,256,256]{2,1,0:T(8,128)(2,1)S(1)}, bf16[4,256,256]{2,1,0:T(8,128)(2,1)S(1)}, u32[]{:S(2)}, u32[]{:S(2)}) collective-permute-start(bf16[4,256,256]{2,1,0:T(8,128)(2,1)S(1)} %collective-permute-done.1.got.first), channel_id=1, source_target_pairs={{0,1},{1,0},{2,3},{3,2},{4,5},{5,4},{6,7},{7,6},{8,9},{9,8},{10,11... | collective-permute-start | bytes 1572872 | tf_op jit(solution)/shard_map/ppermute | solution.py:399
  26.6 5.0 %collective-permute-start.7 = (bf16[4,256,256]{2,1,0:T(8,128)(2,1)S(1)}, bf16[4,256,256]{2,1,0:T(8,128)(2,1)S(1)}, u32[]{:S(2)}, u32[]{:S(2)}) collective-permute-start(bf16[4,256,256]{2,1,0:T(8,128)(2,1)S(1)} %shard_map.92.second), channel_id=1, source_target_pairs={{0,1},{1,0},{2,3},{3,2},{4,5},{5,4},{6,7},{7,6},{8,9},{9,8},{10,11... | collective-permute-start | bytes 1572872 | tf_op jit(solution)/shard_map/ppermute | solution.py:399
  27.1 4.5 %collective-permute-start.9 = (bf16[3,256,256]{2,1,0:T(8,128)(2,1)S(1)}, bf16[3,256,256]{2,1,0:T(8,128)(2,1)S(1)}, u32[]{:S(2)}, u32[]{:S(2)}) collective-permute-start(bf16[3,256,256]{2,1,0:T(8,128)(2,1)S(1)} %collective-permute-done.8.third), channel_id=1, source_target_pairs={{0,1},{1,0},{2,3},{3,2},{4,5},{5,4},{6,7},{7,6},{8,9},{9,8},{10,11... | collective-permute-start | bytes 1179656 | tf_op jit(solution)/shard_map/ppermute | solution.py:399
  27.2 4.4 %collective-permute-start.10 = (bf16[2,32,512]{2,1,0:T(8,128)(2,1)S(1)}, bf16[2,32,512]{2,1,0:T(8,128)(2,1)S(1)}, u32[]{:S(2)}, u32[]{:S(2)}) collective-permute-start(bf16[2,32,512]{2,1,0:T(8,128)(2,1)S(1)} %get-tuple-element.27.__), channel_id=1, source_target_pairs={{0,4},{4,0},{1,5},{5,1},{2,6},{6,2},{3,7},{7,3},{8,12},{12,8},{9,1... | collective-permute-start | bytes 196616 | tf_op jit(solution)/shard_map/ppermute | solution.py:396

commit v3 on v2

--- a/solution.py
+++ b/solution.py
@@ -14,7 +14,9 @@
 PARAMS = pltpu.CompilerParams(vmem_limit_bytes=24 * 1024 * 1024)
 WIDE = pltpu.CompilerParams(vmem_limit_bytes=60 * 1024 * 1024)
 
-OWN, SIB, FIRST, FIRST_SIB, SECOND, SECOND_SIB, THIRD, THIRD_SIB, POOL = 0, 8, 16, 20, 24, 28, 32, 35, 38
+OWN, SIB, FIRST, FIRST_SIB, SECOND, SECOND_SIB, PASSED, PASSED_SIB, POOL = 0, 8, 16, 20, 24, 28, 32, 36, 40
+PLAIN, TURNED, LOWER, UPPER = range(4)
+ROWS = 16
 
 
 def dot(a, b, ca, cb):
@@ -59,7 +61,7 @@
             where(first, self.tile(1 - k, 0, 0), self.tile(1 - k, 0, 1)),
             where(first, self.tile(1 - k, 0, 1), self.tile(1 - k, 1, 1)),
             self.tile(k, 0, 0),
-            self.tile(k, 1, 1),
+            self.tile(k, 1, 0),
         ][n]
         both = where(self.in_row[0], self.tile(1 - k, a, s), 2 * (2 * k + s) + a)
         both = where(self.in_row[0] & self.in_col[0], source, both)
@@ -69,13 +71,16 @@
         first = k == 0 if over_row else k != 0
         return where(k == self.k, where(first, FIRST, SECOND), where(first, FIRST_SIB, SECOND_SIB))
 
-    def third(self, k):
-        return where(k == self.k, THIRD, THIRD_SIB)
+    def passed(self, k):
+        return where(k == self.k, PASSED, PASSED_SIB)
+
+    def square(self, base, i, j):
+        if i == j:
+            return base, jnp.int32(UPPER if i else LOWER)
+        return base + 1, jnp.int32(PLAIN if i else TURNED)
 
     def diagonal(self, over_row, p, i, j):
-        if i == j:
-            return self.message(over_row, self.low[p]) + 2 + i, jnp.int32(0)
-        return self.third(1 if over_row else 0) + self.low[p], jnp.int32(1 if i == 0 else 0)
+        return self.square(self.message(over_row, self.low[p]) + 2, i, j)
 
     def mixed(self, over_row, i, j):
         return self.message(over_row, self.low[i]) + j, jnp.int32(i)
@@ -86,6 +91,8 @@
     def rows(self, p, t, s, a):
         here = where(self.q[p] == self.col, OWN, SIB) + 2 * (2 * t + s) + a, jnp.int32(0)
         plain = self.message(False, jnp.int32(t)) + 2 * s + a, jnp.int32(1)
+        own = self.square(self.message(False, jnp.int32(t)), s, a)
+        plain = self.pick(self.equal & (self.low[p] == t), own, plain)
         same = self.diagonal(False, p, s, a)
         if p == 0:
             cross = self.mixed(False, s, a)
@@ -102,6 +109,8 @@
     def cols(self, p, a, s):
         here = self.tile(self.low[p], a, s), jnp.int32(0)
         plain = self.message(True, self.k) + 2 * s + a, jnp.int32(0)
+        own = self.square(self.message(True, self.k), a, s)
+        plain = self.pick(self.equal & self.in_col[p] & (self.low[p] == self.k), own, plain)
         kept = self.message(False, self.k) + 2 * s + a, jnp.int32(1)
         passed = self.pick(self.low[p] == self.k, kept, plain)
         same = self.diagonal(True, p, a, s)
@@ -119,10 +128,10 @@
         mine = self.pick(self.low[1] == 0, self.rows(0, 0, i, a), self.rows(0, 1, i, a))
         turned = self.pick(self.low[0] == 0, self.rows(1, 0, a, i), self.rows(1, 1, a, i))
         turned = turned[0], 1 - turned[1]
-        equal_near = self.message(True, self.low[1]) + 2 * i + a, jnp.int32(1)
+        equal_near = self.square(self.message(True, self.low[1]), i, a)
         near = self.pick(self.equal, equal_near, self.mixed(True, i, a))
-        equal_far = self.third(self.low[0]) + i + a, jnp.int32(1 if i < a else 0)
-        both_far = self.third(self.low[i]) + a, jnp.int32(i)
+        equal_far = self.square(self.passed(self.low[0]), i, a)
+        both_far = self.passed(self.low[i]) + a, jnp.int32(i)
         far = self.pick(self.equal, equal_far, both_far)
         outside = self.pick(self.in_col[1], near, far)
         return self.pick(self.in_row[1], mine, self.pick(self.in_row[0], turned, outside))
@@ -132,46 +141,6 @@
     down = pl.multiple_of(lax.div(number, 2) * size, size)
     along = pl.multiple_of(lax.rem(number, 2) * size, size)
     return tile[pl.ds(down, size), pl.ds(along, size)]
-
-
-def first_kernel(index_far, working, sent, index, tile, sems):
-    copies = [
-        pltpu.make_async_copy(index_far, index, sems.at[0]),
-        pltpu.make_async_copy(working, tile, sems.at[1]),
-    ]
-    for copy in copies:
-        copy.start()
-    copies[0].wait()
-    here = Place(index)
-    copies[1].wait()
-    for n in range(sent.shape[0]):
-        sent[n] = quarter_of(tile, here.sends(n), sent.shape[1])
-
-
-def third_kernel(index, working, sibling, got, _, sent, token, sems):
-    here = Place(index)
-    size = sent.shape[1]
-    source = here.together & here.in_row[0] & here.in_col[0]
-    token[...] = jnp.zeros_like(token)
-
-    def far(tile, k, n):
-        number = here.tile(k, 1, 0)
-        down = pl.ds(pl.multiple_of(lax.div(number, 2) * size, size), size)
-        return pltpu.make_async_copy(tile.at[down, pl.ds(0, size)], sent.at[k], sems.at[n])
-
-    @pl.when(source)
-    def _():
-        far(working, here.k, 0).start()
-        far(sibling, 1 - here.k, 1).start()
-        far(working, here.k, 0).wait()
-        far(sibling, 1 - here.k, 1).wait()
-
-    @pl.when(jnp.logical_not(source))
-    def _():
-        sent[0] = got[0]
-        sent[1] = got[1]
-
-    sent[2] = got[3]
 
 
 def tie_kernel(_, __, ___):
@@ -194,16 +163,21 @@
     return x
 
 
-def rotate_kernel(obs_far, rotation_far, order_far, _, token, own, *rest):
-    sent, (obs, rotation, order, moved, sems) = rest[:-5], rest[-5:]
-    pairs = ((order_far, order), (rotation_far, rotation), (obs_far, obs))
+def first_kernel(index_far, working, obs_far, rotation_far, order_far, message, own, *rest):
+    sent, (index, tile, obs, rotation, order, moved, sems) = rest[:-7], rest[-7:]
+    pairs = (
+        (order_far, order),
+        (rotation_far, rotation),
+        (obs_far, obs),
+        (index_far, index),
+        (working, tile),
+    )
     copies = [pltpu.make_async_copy(far, near, sems.at[n]) for n, (far, near) in enumerate(pairs)]
     for copy in copies:
         copy.start()
     row, latent = lax.axis_index("row"), lax.axis_index("latent")
     times, own_vars, stations = obs.shape
     latents, all_vars = rotation.shape
-    token[...] = jnp.zeros_like(token)
     copies[0].wait()
     local = order[...] - row * stations
     spread = lax.broadcasted_iota(jnp.int32, (stations, stations), 0) == local
@@ -232,9 +206,31 @@
     own[...] = moved[latent]
     for shift, out in enumerate(sent, 1):
         out[...] = moved[lax.rem(latent + shift, latents)].astype(BF16)
-
-
-def field_kernel(index, _, own, *rest):
+    copies[3].wait()
+    here = Place(index)
+    copies[4].wait()
+    size = message.shape[1]
+    starts = [0, size, 2 * size + ROWS, 3 * size + ROWS]
+    for n, start in enumerate(starts):
+        message[pl.ds(start, size)] = quarter_of(tile, here.sends(n), size)
+    upper = quarter_of(tile, here.tile(here.k, 1, 1), size).astype(F32)
+    down = lax.broadcasted_iota(jnp.int32, (size, size), 0)
+    along = lax.broadcasted_iota(jnp.int32, (size, size), 1)
+    triangles = jnp.where(down >= along, quarter_of(tile, here.tile(here.k, 0, 0), size).astype(F32), upper).astype(BF16)
+    middle = jnp.sum(jnp.where(down == along, upper, 0.0), axis=0, keepdims=True)
+    message[pl.ds(2 * size, ROWS)] = jnp.broadcast_to(middle, (ROWS, size)).astype(BF16)
+    source = here.in_row[0] & here.in_col[0]
+
+    @pl.when(source & here.equal & (here.low[0] == here.k))
+    def _():
+        message[pl.ds(starts[0], size)] = triangles
+
+    @pl.when(source & here.together)
+    def _():
+        message[pl.ds(starts[2], size)] = triangles
+
+
+def field_kernel(index, own, *rest):
     got, (field, rhs) = rest[:-2], rest[-2:]
     total = own[...]
     for part in got:
@@ -259,34 +255,57 @@
     return slot >= SECOND
 
 
-def assemble(blocks, size, table, flip, wanted, load, earlier=None):
+def assemble(blocks, pool, middles, table, flip, base, wanted, earlier=None):
+    size = pool.shape[1]
+
     def step(n, _):
+        down = pl.ds(pl.multiple_of(n * size, size), size)
         for side in range(2):
             slot = table[2 * n + side]
             turn = flip[2 * n + side]
-            down = pl.ds(pl.multiple_of(n * size, size), size)
             along = pl.ds(side * size, size)
+            here = wanted(slot)
 
             if earlier is not None:
 
-                @pl.when(jnp.logical_not(wanted(slot)))
+                @pl.when(jnp.logical_not(here))
                 def _():
                     blocks[down, along] = earlier[down, along]
 
-            @pl.when(wanted(slot) & (turn == 0))
+            @pl.when(here & (turn == PLAIN))
             def _():
-                blocks[down, along] = load(slot)
-
-            @pl.when(wanted(slot) & (turn != 0))
+                blocks[down, along] = pool[slot - base]
+
+            @pl.when(here & (turn == TURNED))
             def _():
-                blocks[down, along] = load(slot).T
+                blocks[down, along] = pool[slot - base].T
+
+            @pl.when(here & (turn >= LOWER))
+            def _():
+                both = pool[slot - base].astype(F32)
+                i = lax.broadcasted_iota(jnp.int32, (size, size), 0)
+                j = lax.broadcasted_iota(jnp.int32, (size, size), 1)
+                lower = jnp.where(i >= j, both, both.T)
+                middle = middles[lax.div(slot - base, 4)].astype(F32)[0:1]
+                upper = jnp.where(i == j, middle, jnp.where(i < j, both, both.T))
+                blocks[down, along] = jnp.where(turn == LOWER, lower, upper).astype(BF16)
 
         return 0
 
     lax.fori_loop(0, blocks.shape[0] // size, step, 0)
 
 
-def early_kernel(index, working, sibling, first, first_sib, _, blocks, table, flip, pool):
+def unpack(ref, pool, middles, slot, number):
+    size = pool.shape[1]
+    pool[slot] = ref[pl.ds(0, size)]
+    pool[slot + 1] = ref[pl.ds(size, size)]
+    middles[number] = ref[pl.ds(2 * size, ROWS)]
+    if ref.shape[0] > 3 * size:
+        pool[slot + 2] = ref[pl.ds(2 * size + ROWS, size)]
+        pool[slot + 3] = ref[pl.ds(3 * size + ROWS, size)]
+
+
+def early_kernel(index, working, sibling, first, first_sib, blocks, table, flip, pool, middles):
     here = Place(index)
     size = pool.shape[1]
     for n, (slot, turn) in enumerate(entries_of(here)):
@@ -302,15 +321,15 @@
         return 0
 
     lax.fori_loop(0, working.shape[0] // size, tiles, 0)
-    pool[pl.ds(FIRST, 4)] = first[...]
-    pool[pl.ds(FIRST_SIB, 4)] = first_sib[...]
-    assemble(blocks, size, table, flip, lambda slot: jnp.logical_not(is_late(slot)), lambda slot: pool[slot])
+    unpack(first, pool, middles, FIRST, FIRST // 4)
+    unpack(first_sib, pool, middles, FIRST_SIB, FIRST_SIB // 4)
+    assemble(blocks, pool, middles, table, flip, 0, lambda slot: jnp.logical_not(is_late(slot)))
 
 
 def factor_kernel(
-    index, table, flip, working, earlier, second, second_sib, third, third_sib,
+    index, table, flip, working, earlier, second, second_sib, passed, passed_sib,
     inverse, field, rhs_far, trailing, panels, whitened,
-    blocks, pool, factors0, factors1, turned0, turned1, rhs_near, result, sems,
+    blocks, pool, middles, factors0, factors1, turned0, turned1, rhs_near, result, sems,
 ):
     here = Place(index)
     size = pool.shape[1]
@@ -318,15 +337,9 @@
     width = inverse.shape[1]
     share = panels.shape[2]
 
-    base = 0
-    for ref in (second, second_sib, third, third_sib):
-        pool[pl.ds(base, ref.shape[0])] = ref[...]
-        base += ref.shape[0]
-
-    def load(slot):
-        return pool[slot - SECOND]
-
-    assemble(blocks, size, table, flip, is_late, load, earlier)
+    for n, ref in enumerate((second, second_sib, passed, passed_sib)):
+        unpack(ref, pool, middles, 4 * n, n)
+    assemble(blocks, pool, middles, table, flip, SECOND, is_late, earlier)
 
     rows0, rows1 = pl.ds(0, tall), pl.ds(tall, tall)
     cols0, cols1 = pl.ds(2 * tall, width), pl.ds(2 * tall + width, width)
@@ -407,80 +420,62 @@
                 pairs.append((i * cols + j, to[0] * cols + to[1]))
         return lax.ppermute(x, ("row", "col"), pairs)
 
-    message = jax.ShapeDtypeStruct((4, size, size), BF16)
-    extra = jax.ShapeDtypeStruct((3, size, size), BF16)
+    message = jax.ShapeDtypeStruct((4 * size + ROWS, size), BF16)
     sibling = siblings(matrix)
-    sent_message = pl.pallas_call(
+    sent_message, own, *sent = pl.pallas_call(
         first_kernel,
-        out_shape=message,
-        in_specs=[ANY] * 2,
-        out_specs=VMEM,
-        scratch_shapes=[
-            pltpu.SMEM((2,), jnp.int32),
-            pltpu.VMEM(matrix.shape, BF16),
-            pltpu.SemaphoreType.DMA((2,)),
-        ],
-        compiler_params=WIDE,
-    )(panel_index, matrix)
-    first = neighbours(sent_message, True)
-
-    token, own, *sent = pl.pallas_call(
-        rotate_kernel,
-        out_shape=[TOKEN, jax.ShapeDtypeStruct((times, stations), F32)]
+        out_shape=[message, jax.ShapeDtypeStruct((times, stations), F32)]
         + [jax.ShapeDtypeStruct((times, stations), BF16)] * (latent_count - 1),
-        in_specs=[ANY] * 4,
+        in_specs=[ANY] * 5,
         out_specs=[VMEM] * (1 + latent_count),
         scratch_shapes=[
+            pltpu.SMEM(panel_index.shape, jnp.int32),
+            pltpu.VMEM(matrix.shape, BF16),
             pltpu.VMEM(observations.shape, BF16),
             pltpu.VMEM(rotation.shape[::-1], F32),
             pltpu.VMEM((1, stations), jnp.int32),
             pltpu.VMEM((latents, times, stations), F32),
-            pltpu.SemaphoreType.DMA((3,)),
+            pltpu.SemaphoreType.DMA((5,)),
         ],
         compiler_params=WIDE,
-    )(observations, rotation.T, ordering[None], sent_message)
-    second = neighbours(tie(sent_message, token, params=WIDE), False)
+    )(panel_index, matrix, observations, rotation.T, ordering[None])
+    first = neighbours(sent_message, True)
     got = []
     for shift, part in enumerate(sent, 1):
         pairs = [(i, (i + shift) % latent_count) for i in range(latent_count)]
         got.append(lax.ppermute(part, "latent", pairs))
 
-    first_sib = siblings(first)
-    sent_third, third_token = pl.pallas_call(
-        third_kernel,
-        out_shape=(extra, TOKEN),
-        in_specs=[SMEM, ANY, ANY, VMEM, ANY],
-        out_specs=(VMEM, VMEM),
-        scratch_shapes=[pltpu.SemaphoreType.DMA((2,))],
-        compiler_params=PARAMS,
-    )(panel_index, matrix, sibling, first, token)
-    third = neighbours(sent_third, False)
-
+    second = neighbours(sent_message, False)
+    first = tie(first, *got)
     field, rhs = pl.pallas_call(
         field_kernel,
         out_shape=(
             jax.ShapeDtypeStruct((times, stations), F32),
             jax.ShapeDtypeStruct((panel_count, times, width), BF16),
         ),
-        in_specs=[SMEM, ANY] + [VMEM] * latent_count,
+        in_specs=[SMEM] + [VMEM] * latent_count,
         out_specs=(VMEM, VMEM),
         compiler_params=PARAMS,
-    )(panel_index, token, own, *got)
+    )(panel_index, own, *got)
     rhs_far = across_rows(rhs)
-
-    second = tie(second, third_token, rhs)
-    second_sib, third_sib = siblings(second), siblings(third)
-
+    first_sib = siblings(first)
+    passed = neighbours(first[: 2 * size + ROWS], False)
     block_shape = jax.ShapeDtypeStruct((14 * size, width), BF16)
     table_shape = jax.ShapeDtypeStruct((28,), jnp.int32)
     blocks, table, flip = pl.pallas_call(
         early_kernel,
         out_shape=(block_shape, table_shape, table_shape),
-        in_specs=[SMEM] + [VMEM] * 4 + [ANY],
+        in_specs=[SMEM] + [VMEM] * 4,
         out_specs=(VMEM, SMEM, SMEM),
-        scratch_shapes=[pltpu.VMEM((POOL, size, size), BF16)],
+        scratch_shapes=[
+            pltpu.VMEM((SECOND, size, size), BF16),
+            pltpu.VMEM((SECOND // 4, ROWS, size), BF16),
+        ],
         compiler_params=PARAMS,
-    )(panel_index, matrix, sibling, first, first_sib, third_token)
+    )(panel_index, matrix, sibling, first, first_sib)
+
+    second = tie(second, rhs_far)
+    second_sib, passed_sib = siblings(second), siblings(passed)
 
     trailing, panels, whitened = pl.pallas_call(
         factor_kernel,
@@ -494,6 +489,7 @@
         scratch_shapes=[
             pltpu.VMEM(block_shape.shape, BF16),
             pltpu.VMEM((POOL - SECOND, size, size), BF16),
+            pltpu.VMEM(((POOL - SECOND) // 4, ROWS, size), BF16),
             pltpu.VMEM((tall + width, width), BF16),
             pltpu.VMEM((tall, width), BF16),
             pltpu.VMEM((width, wide), BF16),
@@ -504,7 +500,7 @@
         ],
         compiler_params=PARAMS,
     )(
-        panel_index, table, flip, matrix, blocks, second, second_sib, third, third_sib,
+        panel_index, table, flip, matrix, blocks, second, second_sib, passed, passed_sib,
         inverse, field, rhs_far,
     )
     return trailing[None], panels[None], whitened[None]

time: 40.1 us -> 41.3 us (1.030); the launches traced: 39.8 us -> 41.7 us
  waiting for transfers between devices: 7.28 us -> 10.7 us
  starting transfers between devices: 13.6 us -> 12.3 us
  Pallas kernels: 17.4 us -> 16.3 us
  local copies, waits for them, and re-layouts: 0.71 us -> 1.59 us
    ppermute x1, waiting for transfers between devices: 0.21 us -> 3.87 us  [across_rows(): return lax.ppermute(x, 'row', [(0, 1), (1, 0)])]
    pallas_call x3 -> x1, Pallas kernels: 6.16 us -> 3.91 us  [local(): pl.pallas_call(first_kernel, out_shape=[message, jax.ShapeDtypeStruct((ti...]
    ppermute x3, waiting for transfers between devices: 3.84 us -> 2.07 us  [neighbours(): return lax.ppermute(x, ('row', 'col'), pairs)]
    ppermute x3, waiting for transfers between devices: 3.22 us -> 4.79 us  [local(): got.append(lax.ppermute(part, 'latent', pairs))]
    ppermute x4, starting transfers between devices: 1.16 us -> 0.01 us  [siblings(): return lax.ppermute(x, 'col', [(i, i ^ 1) for i in range(cols)])]
    ppermute x1, starting transfers between devices: 1.67 us -> 0.61 us  [across_rows(): return lax.ppermute(x, 'row', [(0, 1), (1, 0)])]
    unnamed x16 -> x8, local copies, waits for them, and re-layouts: 0.71 us -> 1.57 us
    pallas_call x1, Pallas kernels: 8.14 us -> 8.86 us  [local(): pl.pallas_call(factor_kernel, out_shape=(jax.ShapeDtypeStruct((tall, wide...]
  transfers between devices with their start and end apart: 11 -> 11, of which waited for: 5 -> 5; matrix products, arithmetic and copies ran while one was open for 0% -> 0% of each run, Pallas kernels for 23% -> 9%
where the time goes in v3:
time: 41.3 us; the launch traced here: 41.7 us
  Pallas kernels  16.3 us (39%)
  starting transfers between devices  12.3 us (30%)
  waiting for transfers between devices  10.7 us (26%)
  local copies, waits for them, and re-layouts  1.59 us (4%)
  between operations  0.72 us (2%)
    pallas_call x1, Pallas kernels, local(): pl.pallas_call(factor_kernel, out_shape=(jax.ShapeDtypeStruct((tall, wide...  8.86 us
    ppermute x3, starting transfers between devices, local(): got.append(lax.ppermute(part, 'latent', pairs))  6.64 us
    ppermute x3, starting transfers between devices, neighbours(): return lax.ppermute(x, ('row', 'col'), pairs)  5.09 us
    ppermute x3, waiting for transfers between devices, local(): got.append(lax.ppermute(part, 'latent', pairs))  4.79 us
    pallas_call x1, Pallas kernels, local(): pl.pallas_call(first_kernel, out_shape=[message, jax.ShapeDtypeStruct((ti...  3.91 us
    ppermute x1, waiting for transfers between devices, across_rows(): return lax.ppermute(x, 'row', [(0, 1), (1, 0)])  3.87 us
    pallas_call x1, Pallas kernels, local(): pl.pallas_call(early_kernel, out_shape=(block_shape, table_shape, table_s...  2.97 us
    ppermute x3, waiting for transfers between devices, neighbours(): return lax.ppermute(x, ('row', 'col'), pairs)  2.07 us
  transfers between devices with their start and end apart: 11, of which 5 were waited for; matrix products, arithmetic and copies ran while one was open for 0% of the time, Pallas kernels for 9%

profile of v3, /device:TPU:0, one launch (start us, length us, event | category | flops | bytes accessed | tf_op | source)
XLA Modules:
  0.0 41.7 jit_solution(15392107006372120702)
XLA Ops:
  0.6 0.0 copy-start
  0.6 3.9 %shard_map.85 = (bf16[1040,256]{1,0:T(8,128)(2,1)}, f32[32,1024]{1,0:T(8,128)}, bf16[32,1024]{1,0:T(8,128)(2,1)}, bf16[32,1024]{1,0:T(8,128)(2,1)}, bf16[32,1024]{1,0:T(8,128)(2,1)}) custom-call(s32[2]{0:T(128)} %index.5, bf16[1024,512]{1,0:T(8,128)(2,1)} %bitcast.7, bf16[32,16,1024]{2,1,0:T(8,128)(2,1)} %obs_far.1, f32[4,64]{1,0:T(4,128)} %bitcast.13, ...), custom_call_target="tpu_custom_call" | custom-call | tf_op jit(solution)/shard_map/pallas_call | solution.py:425
  4.6 3.0 %collective-permute-start.1 = (bf16[1040,256]{1,0:T(8,128)(2,1)}, bf16[1040,256]{1,0:T(8,128)(2,1)S(1)}, u32[]{:S(2)}, u32[]{:S(2)}) collective-permute-start(bf16[1040,256]{1,0:T(8,128)(2,1)} %get-tuple-element.16), channel_id=1, source_target_pairs={{0,4},{1,3},{2,6},{3,1},{4,0},{5,7},{6,2},{7,5},{8,12},{9,11},{10,... | collective-permute-start | bytes 1597448 | tf_op jit(solution)/shard_map/ppermute | solution.py:421
  7.6 1.5 %collective-permute-start.6 = (bf16[1040,256]{1,0:T(8,128)(2,1)}, bf16[1040,256]{1,0:T(8,128)(2,1)S(1)}, u32[]{:S(2)}, u32[]{:S(2)}) collective-permute-start(bf16[1040,256]{1,0:T(8,128)(2,1)} %get-tuple-element.16), channel_id=1, source_target_pairs={{0,2},{1,5},{2,0},{3,7},{4,6},{5,1},{6,4},{7,3},{8,10},{9,13},{10,... | collective-permute-start | bytes 1597448 | tf_op jit(solution)/shard_map/ppermute | solution.py:421
  9.1 0.0 collective-permute-start
  9.1 1.6 %collective-permute-start.2 = (bf16[32,1024]{1,0:T(8,128)(2,1)}, bf16[32,1024]{1,0:T(8,128)(2,1)S(1)}, u32[]{:S(2)}, u32[]{:S(2)}) collective-permute-start(bf16[32,1024]{1,0:T(8,128)(2,1)} %get-tuple-element.17), channel_id=1, source_target_pairs={{0,8},{8,16},{16,24},{24,0},{1,9},{9,17},{17,25},{25,1},{2,10},{10... | collective-permute-start | bytes 196616 | tf_op jit(solution)/shard_map/ppermute | solution.py:446
  10.7 2.6 %collective-permute-start.3 = (bf16[32,1024]{1,0:T(8,128)(2,1)}, bf16[32,1024]{1,0:T(8,128)(2,1)S(1)}, u32[]{:S(2)}, u32[]{:S(2)}) collective-permute-start(bf16[32,1024]{1,0:T(8,128)(2,1)} %get-tuple-element.18), channel_id=1, source_target_pairs={{0,16},{8,24},{16,0},{24,8},{1,17},{9,25},{17,1},{25,9},{2,18},{10... | collective-permute-start | bytes 196616 | tf_op jit(solution)/shard_map/ppermute | solution.py:446
  13.2 2.6 %collective-permute-done.2.__.rest_0_ = bf16[32,1024]{1,0:T(8,128)(2,1)S(1)} collective-permute-done((bf16[32,1024]{1,0:T(8,128)(2,1)}, bf16[32,1024]{1,0:T(8,128)(2,1)S(1)}, u32[]{:S(2)}, u32[]{:S(2)}) %collective-permute-start.2) | collective-permute-done | bytes 65568 | tf_op jit(solution)/shard_map/ppermute | solution.py:446
  15.8 2.5 %collective-permute-start.4 = (bf16[32,1024]{1,0:T(8,128)(2,1)}, bf16[32,1024]{1,0:T(8,128)(2,1)S(1)}, u32[]{:S(2)}, u32[]{:S(2)}) collective-permute-start(bf16[32,1024]{1,0:T(8,128)(2,1)} %get-tuple-element.19), channel_id=1, source_target_pairs={{0,24},{8,0},{16,8},{24,16},{1,25},{9,1},{17,9},{25,17},{2,26},{10... | collective-permute-start | bytes 196616 | tf_op jit(solution)/shard_map/ppermute | solution.py:446
  18.3 0.2 collective-permute-done.3.__.rest_1_
  18.5 2.0 %collective-permute-done.4.__.rest_2_ = bf16[32,1024]{1,0:T(8,128)(2,1)S(1)} collective-permute-done((bf16[32,1024]{1,0:T(8,128)(2,1)}, bf16[32,1024]{1,0:T(8,128)(2,1)S(1)}, u32[]{:S(2)}, u32[]{:S(2)}) %collective-permute-start.4) | collective-permute-done | bytes 65568 | tf_op jit(solution)/shard_map/ppermute | solution.py:446
  20.5 0.0 copy-start.2
  20.5 0.9 %copy-done.2 = f32[32,1024]{1,0:T(8,128)S(1)} copy-done((f32[32,1024]{1,0:T(8,128)S(1)}, f32[32,1024]{1,0:T(8,128)}, u32[]{:S(2)}) %copy-start.2) | copy-done | bytes 131096
  21.4 0.0 copy-start.3
  21.4 0.7 %copy-done.3 = s32[2]{0:T(128)S(1)} copy-done((s32[2]{0:T(128)S(1)}, s32[2]{0:T(128)}, u32[]{:S(2)}) %copy-start.3) | copy-done | bytes 32
  22.1 0.6 %shard_map.90 = (f32[32,1024]{1,0:T(8,128)S(1)}, bf16[2,32,512]{2,1,0:T(8,128)(2,1)S(1)}) custom-call(s32[2]{0:T(128)S(1)} %copy-done.3, f32[32,1024]{1,0:T(8,128)S(1)} %copy-done.2, bf16[32,1024]{1,0:T(8,128)(2,1)S(1)} %collective-permute-done.2.__.rest_0_, bf16[32,1024]{1,0:T(8,128)(2,1)S(1)} %collective-permute-done.3.__.rest_1_, ...), custom_call_target="tpu_custom_call" | custom-call | tf_op jit(solution)/shard_map/pallas_call | solution.py:450
  22.7 0.6 %collective-permute-start.7 = (bf16[2,32,512]{2,1,0:T(8,128)(2,1)S(1)}, bf16[2,32,512]{2,1,0:T(8,128)(2,1)S(1)}, u32[]{:S(2)}, u32[]{:S(2)}) collective-permute-start(bf16[2,32,512]{2,1,0:T(8,128)(2,1)S(1)} %get-tuple-element.24), channel_id=1, source_target_pairs={{0,4},{4,0},{1,5},{5,1},{2,6},{6,2},{3,7},{7,3},{8,12},{12,8},{9,1... | collective-permute-start | bytes 196616 | tf_op jit(solution)/shard_map/ppermute | solution.py:409
  23.3 0.0 collective-permute-done.1._
  23.3 0.0 copy-start.1
  23.3 0.6 %collective-permute-start.9 = (bf16[528,256]{1,0:T(8,128)(2,1)S(1)}, bf16[528,256]{1,0:T(8,128)(2,1)S(1)}, u32[]{:S(2)}, u32[]{:S(2)}) collective-permute-start(bf16[528,256]{1,0:T(8,128)(2,1)S(1)} %slice.4), channel_id=1, source_target_pairs={{0,2},{1,5},{2,0},{3,7},{4,6},{5,1},{6,4},{7,3},{8,10},{9,13},{10,... | collective-permute-start | bytes 811016 | tf_op jit(solution)/shard_map/ppermute | solution.py:421
  23.9 0.0 collective-permute-start.5
  23.9 3.9 %collective-permute-done.7.__.rhs_far = bf16[2,32,512]{2,1,0:T(8,128)(2,1)S(1)} collective-permute-done((bf16[2,32,512]{2,1,0:T(8,128)(2,1)S(1)}, bf16[2,32,512]{2,1,0:T(8,128)(2,1)S(1)}, u32[]{:S(2)}, u32[]{:S(2)}) %collective-permute-start.7) | collective-permute-done | bytes 65568 | tf_op jit(solution)/shard_map/ppermute | solution.py:409
  27.8 0.0 collective-permute-done.6._
  27.8 0.0 collective-permute-start.8
  27.8 2.1 %collective-permute-done.9.passed = bf16[528,256]{1,0:T(8,128)(2,1)S(1)} collective-permute-done((bf16[528,256]{1,0:T(8,128)(2,1)S(1)}, bf16[528,256]{1,0:T(8,128)(2,1)S(1)}, u32[]{:S(2)}, u32[]{:S(2)}) %collective-permute-start.9) | collective-permute-done | bytes 270368 | tf_op jit(solution)/shard_map/ppermute | solution.py:421
  29.8 0.0 collective-permute-start.10
  29.8 0.0 collective-permute-done.sibling
  29.8 0.0 collective-permute-done.5.first_sib
  29.8 0.0 copy-done
  29.9 3.0 %shard_map.89 = (bf16[3584,512]{1,0:T(8,128)(2,1)S(1)}, s32[28]{0:T(128)S(1)}, s32[28]{0:T(128)S(1)}) custom-call(s32[2]{0:T(128)S(1)} %copy-done.3, bf16[1024,512]{1,0:T(8,128)(2,1)S(1)} %bitcast.9, bf16[1024,512]{1,0:T(8,128)(2,1)S(1)} %collective-permute-done.sibling, bf16[1040,256]{1,0:T(8,128)(2,1)S(1)} %shard_map.88.first, ...), custom_call_target="tpu_custom_call" | custom-call | tf_op jit(solution)/shard_map/pallas_call | solution.py:465
  32.8 0.0 collective-permute-done.8.second_sib
  32.8 0.0 collective-permute-done.10.passed_sib
  32.9 0.0 copy-done.1
  32.9 8.9 %shard_map.92 = (f32[1024,512]{1,0:T(8,128)}, bf16[2,1024,128]{2,1,0:T(8,128)(2,1)}, f32[32,1024]{1,0:T(8,128)}) custom-call(s32[2]{0:T(128)S(1)} %copy-done.3, s32[28]{0:T(128)S(1)} %get-tuple-element.20.table, s32[28]{0:T(128)S(1)} %get-tuple-element.21.flip, bf16[1024,512]{1,0:T(8,128)(2,1)S(1)} %bitcast.10, ...), custom_call_target="tpu_custom_call" | custom-call | tf_op jit(solution)/shard_map/pallas_call | solution.py:480
  (5 shorter events, 0.0 us)
Async XLA Ops:
  0.6 29.2 %copy-start = (bf16[1,1024,512]{2,1,0:T(8,128)(2,1)S(1)}, bf16[1,1024,512]{2,1,0:T(8,128)(2,1)}, u32[]{:S(2)}) copy-start(bf16[1,1024,512]{2,1,0:T(8,128)(2,1)} %param.9) | copy-start | bytes 3145732
  4.6 18.7 %collective-permute-start.1 = (bf16[1040,256]{1,0:T(8,128)(2,1)}, bf16[1040,256]{1,0:T(8,128)(2,1)S(1)}, u32[]{:S(2)}, u32[]{:S(2)}) collective-permute-start(bf16[1040,256]{1,0:T(8,128)(2,1)} %get-tuple-element.16), channel_id=1, source_target_pairs={{0,4},{1,3},{2,6},{3,1},{4,0},{5,7},{6,2},{7,5},{8,12},{9,11},{10,... | collective-permute-start | bytes 1597448 | tf_op jit(solution)/shard_map/ppermute | solution.py:421
  7.6 20.2 %collective-permute-start.6 = (bf16[1040,256]{1,0:T(8,128)(2,1)}, bf16[1040,256]{1,0:T(8,128)(2,1)S(1)}, u32[]{:S(2)}, u32[]{:S(2)}) collective-permute-start(bf16[1040,256]{1,0:T(8,128)(2,1)} %get-tuple-element.16), channel_id=1, source_target_pairs={{0,2},{1,5},{2,0},{3,7},{4,6},{5,1},{6,4},{7,3},{8,10},{9,13},{10,... | collective-permute-start | bytes 1597448 | tf_op jit(solution)/shard_map/ppermute | solution.py:421
  9.1 20.8 %collective-permute-start = (bf16[1024,512]{1,0:T(8,128)(2,1)}, bf16[1024,512]{1,0:T(8,128)(2,1)S(1)}, u32[]{:S(2)}, u32[]{:S(2)}) collective-permute-start(bf16[1024,512]{1,0:T(8,128)(2,1)} %bitcast.8), channel_id=1, source_target_pairs={{0,1},{1,0},{2,3},{3,2},{4,5},{5,4},{6,7},{7,6},{8,9},{9,8},{10,11... | collective-permute-start | bytes 3145736 | tf_op jit(solution)/shard_map/ppermute | solution.py:412
  9.1 6.7 %collective-permute-start.2 = (bf16[32,1024]{1,0:T(8,128)(2,1)}, bf16[32,1024]{1,0:T(8,128)(2,1)S(1)}, u32[]{:S(2)}, u32[]{:S(2)}) collective-permute-start(bf16[32,1024]{1,0:T(8,128)(2,1)} %get-tuple-element.17), channel_id=1, source_target_pairs={{0,8},{8,16},{16,24},{24,0},{1,9},{9,17},{17,25},{25,1},{2,10},{10... | collective-permute-start | bytes 196616 | tf_op jit(solution)/shard_map/ppermute | solution.py:446
  10.7 7.9 %collective-permute-start.3 = (bf16[32,1024]{1,0:T(8,128)(2,1)}, bf16[32,1024]{1,0:T(8,128)(2,1)S(1)}, u32[]{:S(2)}, u32[]{:S(2)}) collective-permute-start(bf16[32,1024]{1,0:T(8,128)(2,1)} %get-tuple-element.18), channel_id=1, source_target_pairs={{0,16},{8,24},{16,0},{24,8},{1,17},{9,25},{17,1},{25,9},{2,18},{10... | collective-permute-start | bytes 196616 | tf_op jit(solution)/shard_map/ppermute | solution.py:446
  15.8 4.7 %collective-permute-start.4 = (bf16[32,1024]{1,0:T(8,128)(2,1)}, bf16[32,1024]{1,0:T(8,128)(2,1)S(1)}, u32[]{:S(2)}, u32[]{:S(2)}) collective-permute-start(bf16[32,1024]{1,0:T(8,128)(2,1)} %get-tuple-element.19), channel_id=1, source_target_pairs={{0,24},{8,0},{16,8},{24,16},{1,25},{9,1},{17,9},{25,17},{2,26},{10... | collective-permute-start | bytes 196616 | tf_op jit(solution)/shard_map/ppermute | solution.py:446
  20.5 0.9 %copy-start.2 = (f32[32,1024]{1,0:T(8,128)S(1)}, f32[32,1024]{1,0:T(8,128)}, u32[]{:S(2)}) copy-start(f32[32,1024]{1,0:T(8,128)} %get-tuple-element.23.own) | copy-start | bytes 393220
  21.4 0.7 %copy-start.3 = (s32[2]{0:T(128)S(1)}, s32[2]{0:T(128)}, u32[]{:S(2)}) copy-start(s32[2]{0:T(128)} %index.5) | copy-start | bytes 28
  22.7 5.1 %collective-permute-start.7 = (bf16[2,32,512]{2,1,0:T(8,128)(2,1)S(1)}, bf16[2,32,512]{2,1,0:T(8,128)(2,1)S(1)}, u32[]{:S(2)}, u32[]{:S(2)}) collective-permute-start(bf16[2,32,512]{2,1,0:T(8,128)(2,1)S(1)} %get-tuple-element.24), channel_id=1, source_target_pairs={{0,4},{4,0},{1,5},{5,1},{2,6},{6,2},{3,7},{7,3},{8,12},{12,8},{9,1... | collective-permute-start | bytes 196616 | tf_op jit(solution)/shard_map/ppermute | solution.py:409
  23.3 9.6 %copy-start.1 = (bf16[1,2,512,512]{3,2,1,0:T(8,128)(2,1)S(1)}, bf16[1,2,512,512]{3,2,1,0:T(8,128)(2,1)}, u32[]{:S(2)}) copy-start(bf16[1,2,512,512]{3,2,1,0:T(8,128)(2,1)} %param.10) | copy-start | bytes 3145732
  23.3 6.5 %collective-permute-start.9 = (bf16[528,256]{1,0:T(8,128)(2,1)S(1)}, bf16[528,256]{1,0:T(8,128)(2,1)S(1)}, u32[]{:S(2)}, u32[]{:S(2)}) collective-permute-start(bf16[528,256]{1,0:T(8,128)(2,1)S(1)} %slice.4), channel_id=1, source_target_pairs={{0,2},{1,5},{2,0},{3,7},{4,6},{5,1},{6,4},{7,3},{8,10},{9,13},{10,... | collective-permute-start | bytes 811016 | tf_op jit(solution)/shard_map/ppermute | solution.py:421
  23.9 6.0 %collective-permute-start.5 = (bf16[1040,256]{1,0:T(8,128)(2,1)S(1)}, bf16[1040,256]{1,0:T(8,128)(2,1)S(1)}, u32[]{:S(2)}, u32[]{:S(2)}) collective-permute-start(bf16[1040,256]{1,0:T(8,128)(2,1)S(1)} %shard_map.88.first), channel_id=1, source_target_pairs={{0,1},{1,0},{2,3},{3,2},{4,5},{5,4},{6,7},{7,6},{8,9},{9,8},{10,11... | collective-permute-start | bytes 1597448 | tf_op jit(solution)/shard_map/ppermute | solution.py:412
  27.8 5.1 %collective-permute-start.8 = (bf16[1040,256]{1,0:T(8,128)(2,1)S(1)}, bf16[1040,256]{1,0:T(8,128)(2,1)S(1)}, u32[]{:S(2)}, u32[]{:S(2)}) collective-permute-start(bf16[1040,256]{1,0:T(8,128)(2,1)S(1)} %shard_map.91.second), channel_id=1, source_target_pairs={{0,1},{1,0},{2,3},{3,2},{4,5},{5,4},{6,7},{7,6},{8,9},{9,8},{10,11... | collective-permute-start | bytes 1597448 | tf_op jit(solution)/shard_map/ppermute | solution.py:412
  29.8 3.0 %collective-permute-start.10 = (bf16[528,256]{1,0:T(8,128)(2,1)S(1)}, bf16[528,256]{1,0:T(8,128)(2,1)S(1)}, u32[]{:S(2)}, u32[]{:S(2)}) collective-permute-start(bf16[528,256]{1,0:T(8,128)(2,1)S(1)} %collective-permute-done.9.passed), channel_id=1, source_target_pairs={{0,1},{1,0},{2,3},{3,2},{4,5},{5,4},{6,7},{7,6},{8,9},{9,8},{10,11... | collective-permute-start | bytes 811016 | tf_op jit(solution)/shard_map/ppermute | solution.py:412

commit v4 on v3

--- a/solution.py
+++ b/solution.py
@@ -21,6 +21,18 @@
 
 def dot(a, b, ca, cb):
     return lax.dot_general(a, b, (((ca,), (cb,)), ((), ())), preferred_element_type=F32)
+
+
+def by_lower(x, inverse, out, rows):
+    half = inverse.shape[0] // 2
+    out[rows, :half] = dot(x[:, :half], inverse[:half, :half], 1, 1).astype(BF16)
+    out[rows, half:] = dot(x, inverse[half:], 1, 1).astype(BF16)
+
+
+def lower_by(inverse, x, out):
+    half = inverse.shape[0] // 2
+    out[:half] = dot(inverse[:half, :half], x[:half], 1, 0).astype(BF16)
+    out[half:] = dot(inverse[half:], x, 1, 0).astype(BF16)
 
 
 def pieces(x, count):
@@ -346,15 +358,15 @@
     cross = pl.ds(2 * tall + 2 * width, width)
     inv0, inv1 = inverse[0], inverse[1]
 
-    factors0[pl.ds(tall, width)] = dot(blocks[cross], inv0, 1, 1).astype(BF16)
-    turned0[...] = dot(inv0, blocks[cols0], 1, 0).astype(BF16)
-    factors0[rows0] = dot(blocks[rows0], inv0, 1, 1).astype(BF16)
+    by_lower(blocks[cross], inv0, factors0, slice(tall, tall + width))
+    lower_by(inv0, blocks[cols0], turned0)
+    by_lower(blocks[rows0], inv0, factors0, slice(0, tall))
     mixed = factors0[pl.ds(tall, width)]
 
     got = blocks[cols1].astype(F32) - dot(mixed, turned0[...], 1, 0)
-    turned1[...] = dot(inv1, got.astype(BF16), 1, 0).astype(BF16)
+    lower_by(inv1, got.astype(BF16), turned1)
     got = blocks[rows1].astype(F32) - dot(factors0[rows0], mixed, 1, 1)
-    factors1[...] = dot(got.astype(BF16), inv1, 1, 1).astype(BF16)
+    by_lower(got.astype(BF16), inv1, factors1, slice(0, tall))
 
     lanes = pl.ds(pl.multiple_of(here.col * share, share), share)
     copies = [
@@ -474,7 +486,7 @@
         compiler_params=PARAMS,
     )(panel_index, matrix, sibling, first, first_sib)
 
-    second = tie(second, rhs_far)
+    second = tie(second, rhs_far, table)
     second_sib, passed_sib = siblings(second), siblings(passed)
 
     trailing, panels, whitened = pl.pallas_call(
@@ -496,7 +508,7 @@
             pltpu.VMEM((width, wide), BF16),
             pltpu.VMEM((panel_count, times, width), F32),
             pltpu.VMEM((tall, wide), F32),
-            pltpu.SemaphoreType.DMA((4,)),
+            pltpu.SemaphoreType.DMA((6,)),
         ],
         compiler_params=PARAMS,
     )(

time: 41.3 us -> 37.8 us (0.915); the launches traced: 41.7 us -> 37.6 us
  waiting for transfers between devices: 10.7 us -> 7.39 us
  Pallas kernels: 16.3 us -> 15.7 us
  local copies, waits for them, and re-layouts: 1.59 us -> 0.99 us
  starting transfers between devices: 12.3 us -> 12.8 us
    ppermute x3, waiting for transfers between devices: 4.79 us -> 2.69 us  [local(): got.append(lax.ppermute(part, 'latent', pairs))]
    ppermute x3, waiting for transfers between devices: 2.07 us -> 0.01 us  [neighbours(): return lax.ppermute(x, ('row', 'col'), pairs)]
    ppermute x4, waiting for transfers between devices: 0.01 us -> 1.8 us  [siblings(): return lax.ppermute(x, 'col', [(i, i ^ 1) for i in range(cols)])]
    ppermute x3, starting transfers between devices: 6.64 us -> 5.51 us  [local(): got.append(lax.ppermute(part, 'latent', pairs))]
    ppermute x3, starting transfers between devices: 5.09 us -> 6.09 us  [neighbours(): return lax.ppermute(x, ('row', 'col'), pairs)]
    ppermute x1, waiting for transfers between devices: 3.87 us -> 2.89 us  [across_rows(): return lax.ppermute(x, 'row', [(0, 1), (1, 0)])]
    unnamed x8, local copies, waits for them, and re-layouts: 1.57 us -> 0.98 us
    ppermute x4, starting transfers between devices: 0.01 us -> 0.58 us  [siblings(): return lax.ppermute(x, 'col', [(i, i ^ 1) for i in range(cols)])]
where the time goes in v4:
time: 37.8 us; the launch traced here: 37.6 us
  Pallas kernels  15.7 us (42%)
  starting transfers between devices  12.8 us (34%)
  waiting for transfers between devices  7.39 us (20%)
  local copies, waits for them, and re-layouts  0.99 us (3%)
  between operations  0.71 us (2%)
    pallas_call x1, Pallas kernels, local(): pl.pallas_call(factor_kernel, out_shape=(jax.ShapeDtypeStruct((tall, wide...  8.59 us
    ppermute x3, starting transfers between devices, neighbours(): return lax.ppermute(x, ('row', 'col'), pairs)  6.09 us
    ppermute x3, starting transfers between devices, local(): got.append(lax.ppermute(part, 'latent', pairs))  5.51 us
    pallas_call x1, Pallas kernels, local(): pl.pallas_call(first_kernel, out_shape=[message, jax.ShapeDtypeStruct((ti...  3.9 us
    ppermute x1, waiting for transfers between devices, across_rows(): return lax.ppermute(x, 'row', [(0, 1), (1, 0)])  2.89 us
    ppermute x3, waiting for transfers between devices, local(): got.append(lax.ppermute(part, 'latent', pairs))  2.69 us
    pallas_call x1, Pallas kernels, local(): pl.pallas_call(early_kernel, out_shape=(block_shape, table_shape, table_s...  2.66 us
    ppermute x4, waiting for transfers between devices, siblings(): return lax.ppermute(x, 'col', [(i, i ^ 1) for i in range(cols)])  1.8 us
  transfers between devices with their start and end apart: 11, of which 5 were waited for; matrix products, arithmetic and copies ran while one was open for 0% of the time, Pallas kernels for 9%

profile of v4, /device:TPU:0, one launch (start us, length us, event | category | flops | bytes accessed | tf_op | source)
XLA Modules:
  0.0 37.6 jit_solution(18091543817616080239)
XLA Ops:
  0.6 0.0 copy-start.3
  0.6 0.0 copy-start
  0.7 3.9 %shard_map.85 = (bf16[1040,256]{1,0:T(8,128)(2,1)}, f32[32,1024]{1,0:T(8,128)}, bf16[32,1024]{1,0:T(8,128)(2,1)}, bf16[32,1024]{1,0:T(8,128)(2,1)}, bf16[32,1024]{1,0:T(8,128)(2,1)}) custom-call(s32[2]{0:T(128)} %index.5, bf16[1024,512]{1,0:T(8,128)(2,1)} %bitcast.7, bf16[32,16,1024]{2,1,0:T(8,128)(2,1)} %obs_far.1, f32[4,64]{1,0:T(4,128)} %bitcast.13, ...), custom_call_target="tpu_custom_call" | custom-call | tf_op jit(solution)/shard_map/pallas_call | solution.py:437
  4.6 3.0 %collective-permute-start.1 = (bf16[1040,256]{1,0:T(8,128)(2,1)}, bf16[1040,256]{1,0:T(8,128)(2,1)S(1)}, u32[]{:S(2)}, u32[]{:S(2)}) collective-permute-start(bf16[1040,256]{1,0:T(8,128)(2,1)} %get-tuple-element.16), channel_id=1, source_target_pairs={{0,4},{1,3},{2,6},{3,1},{4,0},{5,7},{6,2},{7,5},{8,12},{9,11},{10,... | collective-permute-start | bytes 1597448 | tf_op jit(solution)/shard_map/ppermute | solution.py:433
  7.6 0.0 collective-permute-start
  7.6 1.6 %collective-permute-start.2 = (bf16[32,1024]{1,0:T(8,128)(2,1)}, bf16[32,1024]{1,0:T(8,128)(2,1)S(1)}, u32[]{:S(2)}, u32[]{:S(2)}) collective-permute-start(bf16[32,1024]{1,0:T(8,128)(2,1)} %get-tuple-element.17), channel_id=1, source_target_pairs={{0,8},{8,16},{16,24},{24,0},{1,9},{9,17},{17,25},{25,1},{2,10},{10... | collective-permute-start | bytes 196616 | tf_op jit(solution)/shard_map/ppermute | solution.py:458
  9.1 2.6 %collective-permute-start.3 = (bf16[32,1024]{1,0:T(8,128)(2,1)}, bf16[32,1024]{1,0:T(8,128)(2,1)S(1)}, u32[]{:S(2)}, u32[]{:S(2)}) collective-permute-start(bf16[32,1024]{1,0:T(8,128)(2,1)} %get-tuple-element.18), channel_id=1, source_target_pairs={{0,16},{8,24},{16,0},{24,8},{1,17},{9,25},{17,1},{25,9},{2,18},{10... | collective-permute-start | bytes 196616 | tf_op jit(solution)/shard_map/ppermute | solution.py:458
  11.7 1.3 %collective-permute-start.4 = (bf16[32,1024]{1,0:T(8,128)(2,1)}, bf16[32,1024]{1,0:T(8,128)(2,1)S(1)}, u32[]{:S(2)}, u32[]{:S(2)}) collective-permute-start(bf16[32,1024]{1,0:T(8,128)(2,1)} %get-tuple-element.19), channel_id=1, source_target_pairs={{0,24},{8,0},{16,8},{24,16},{1,25},{9,1},{17,9},{25,17},{2,26},{10... | collective-permute-start | bytes 196616 | tf_op jit(solution)/shard_map/ppermute | solution.py:458
  13.1 1.2 %collective-permute-done.2.__.rest_0_ = bf16[32,1024]{1,0:T(8,128)(2,1)S(1)} collective-permute-done((bf16[32,1024]{1,0:T(8,128)(2,1)}, bf16[32,1024]{1,0:T(8,128)(2,1)S(1)}, u32[]{:S(2)}, u32[]{:S(2)}) %collective-permute-start.2) | collective-permute-done | bytes 65568 | tf_op jit(solution)/shard_map/ppermute | solution.py:458
  14.3 1.5 %collective-permute-start.6 = (bf16[1040,256]{1,0:T(8,128)(2,1)}, bf16[1040,256]{1,0:T(8,128)(2,1)S(1)}, u32[]{:S(2)}, u32[]{:S(2)}) collective-permute-start(bf16[1040,256]{1,0:T(8,128)(2,1)} %get-tuple-element.16), channel_id=1, source_target_pairs={{0,2},{1,5},{2,0},{3,7},{4,6},{5,1},{6,4},{7,3},{8,10},{9,13},{10,... | collective-permute-start | bytes 1597448 | tf_op jit(solution)/shard_map/ppermute | solution.py:433
  15.8 0.0 collective-permute-done.1._
  15.8 1.2 %collective-permute-done.3.__.rest_1_ = bf16[32,1024]{1,0:T(8,128)(2,1)S(1)} collective-permute-done((bf16[32,1024]{1,0:T(8,128)(2,1)}, bf16[32,1024]{1,0:T(8,128)(2,1)S(1)}, u32[]{:S(2)}, u32[]{:S(2)}) %collective-permute-start.3) | collective-permute-done | bytes 65568 | tf_op jit(solution)/shard_map/ppermute | solution.py:458
  17.1 0.0 copy-start.1
  17.1 0.2 collective-permute-done.4.__.rest_2_
  17.3 0.0 collective-permute-start.5
  17.3 0.0 copy-done.3
  17.3 0.0 copy-start.2
  17.3 1.0 %copy-done.2 = f32[32,1024]{1,0:T(8,128)S(1)} copy-done((f32[32,1024]{1,0:T(8,128)S(1)}, f32[32,1024]{1,0:T(8,128)}, u32[]{:S(2)}) %copy-start.2) | copy-done | bytes 131096
  18.3 0.6 %shard_map.90 = (f32[32,1024]{1,0:T(8,128)S(1)}, bf16[2,32,512]{2,1,0:T(8,128)(2,1)S(1)}) custom-call(s32[2]{0:T(128)S(1)} %copy-done.3, f32[32,1024]{1,0:T(8,128)S(1)} %copy-done.2, bf16[32,1024]{1,0:T(8,128)(2,1)S(1)} %collective-permute-done.2.__.rest_0_, bf16[32,1024]{1,0:T(8,128)(2,1)S(1)} %collective-permute-done.3.__.rest_1_, ...), custom_call_target="tpu_custom_call" | custom-call | tf_op jit(solution)/shard_map/pallas_call | solution.py:462
  18.9 0.6 %collective-permute-start.7 = (bf16[2,32,512]{2,1,0:T(8,128)(2,1)S(1)}, bf16[2,32,512]{2,1,0:T(8,128)(2,1)S(1)}, u32[]{:S(2)}, u32[]{:S(2)}) collective-permute-start(bf16[2,32,512]{2,1,0:T(8,128)(2,1)S(1)} %get-tuple-element.24), channel_id=1, source_target_pairs={{0,4},{4,0},{1,5},{5,1},{2,6},{6,2},{3,7},{7,3},{8,12},{12,8},{9,1... | collective-permute-start | bytes 196616 | tf_op jit(solution)/shard_map/ppermute | solution.py:421
  19.5 1.6 %collective-permute-start.9 = (bf16[528,256]{1,0:T(8,128)(2,1)S(1)}, bf16[528,256]{1,0:T(8,128)(2,1)S(1)}, u32[]{:S(2)}, u32[]{:S(2)}) collective-permute-start(bf16[528,256]{1,0:T(8,128)(2,1)S(1)} %slice.4), channel_id=1, source_target_pairs={{0,2},{1,5},{2,0},{3,7},{4,6},{5,1},{6,4},{7,3},{8,10},{9,13},{10,... | collective-permute-start | bytes 811016 | tf_op jit(solution)/shard_map/ppermute | solution.py:433
  21.1 2.9 %collective-permute-done.7.__.rhs_far = bf16[2,32,512]{2,1,0:T(8,128)(2,1)S(1)} collective-permute-done((bf16[2,32,512]{2,1,0:T(8,128)(2,1)S(1)}, bf16[2,32,512]{2,1,0:T(8,128)(2,1)S(1)}, u32[]{:S(2)}, u32[]{:S(2)}) %collective-permute-start.7) | collective-permute-done | bytes 65568 | tf_op jit(solution)/shard_map/ppermute | solution.py:421
  24.0 0.0 collective-permute-done.6._
  24.0 0.0 collective-permute-done.sibling
  24.0 0.0 collective-permute-done.5.first_sib
  24.0 0.0 copy-done
  24.0 2.7 %shard_map.89 = (bf16[3584,512]{1,0:T(8,128)(2,1)S(1)}, s32[28]{0:T(128)S(1)}, s32[28]{0:T(128)S(1)}) custom-call(s32[2]{0:T(128)S(1)} %copy-done.3, bf16[1024,512]{1,0:T(8,128)(2,1)S(1)} %bitcast.9, bf16[1024,512]{1,0:T(8,128)(2,1)S(1)} %collective-permute-done.sibling, bf16[1040,256]{1,0:T(8,128)(2,1)S(1)} %shard_map.88.first, ...), custom_call_target="tpu_custom_call" | custom-call | tf_op jit(solution)/shard_map/pallas_call | solution.py:477
  26.7 0.2 collective-permute-start.8
  26.9 0.0 collective-permute-done.9.passed
  26.9 0.3 collective-permute-start.10
  27.2 1.8 %collective-permute-done.10.passed_sib = bf16[528,256]{1,0:T(8,128)(2,1)S(1)} collective-permute-done((bf16[528,256]{1,0:T(8,128)(2,1)S(1)}, bf16[528,256]{1,0:T(8,128)(2,1)S(1)}, u32[]{:S(2)}, u32[]{:S(2)}) %collective-permute-start.10) | collective-permute-done | bytes 270368 | tf_op jit(solution)/shard_map/ppermute | solution.py:424
  29.0 0.0 collective-permute-done.8.second_sib
  29.0 0.0 copy-done.1
  29.1 8.6 %shard_map.93 = (f32[1024,512]{1,0:T(8,128)}, bf16[2,1024,128]{2,1,0:T(8,128)(2,1)}, f32[32,1024]{1,0:T(8,128)}) custom-call(s32[2]{0:T(128)S(1)} %copy-done.3, s32[28]{0:T(128)S(1)} %get-tuple-element.20.__.table, s32[28]{0:T(128)S(1)} %get-tuple-element.21.flip, bf16[1024,512]{1,0:T(8,128)(2,1)S(1)} %bitcast.10, ...), custom_call_target="tpu_custom_call" | custom-call | tf_op jit(solution)/shard_map/pallas_call | solution.py:492
  (6 shorter events, 0.0 us)
Async XLA Ops:
  0.6 16.7 %copy-start.3 = (s32[2]{0:T(128)S(1)}, s32[2]{0:T(128)}, u32[]{:S(2)}) copy-start(s32[2]{0:T(128)} %index.5) | copy-start | bytes 28
  0.6 23.3 %copy-start = (bf16[1,1024,512]{2,1,0:T(8,128)(2,1)S(1)}, bf16[1,1024,512]{2,1,0:T(8,128)(2,1)}, u32[]{:S(2)}) copy-start(bf16[1,1024,512]{2,1,0:T(8,128)(2,1)} %param.9) | copy-start | bytes 3145732
  4.6 11.3 %collective-permute-start.1 = (bf16[1040,256]{1,0:T(8,128)(2,1)}, bf16[1040,256]{1,0:T(8,128)(2,1)S(1)}, u32[]{:S(2)}, u32[]{:S(2)}) collective-permute-start(bf16[1040,256]{1,0:T(8,128)(2,1)} %get-tuple-element.16), channel_id=1, source_target_pairs={{0,4},{1,3},{2,6},{3,1},{4,0},{5,7},{6,2},{7,5},{8,12},{9,11},{10,... | collective-permute-start | bytes 1597448 | tf_op jit(solution)/shard_map/ppermute | solution.py:433
  7.6 16.4 %collective-permute-start = (bf16[1024,512]{1,0:T(8,128)(2,1)}, bf16[1024,512]{1,0:T(8,128)(2,1)S(1)}, u32[]{:S(2)}, u32[]{:S(2)}) collective-permute-start(bf16[1024,512]{1,0:T(8,128)(2,1)} %bitcast.8), channel_id=1, source_target_pairs={{0,1},{1,0},{2,3},{3,2},{4,5},{5,4},{6,7},{7,6},{8,9},{9,8},{10,11... | collective-permute-start | bytes 3145736 | tf_op jit(solution)/shard_map/ppermute | solution.py:424
  7.6 6.7 %collective-permute-start.2 = (bf16[32,1024]{1,0:T(8,128)(2,1)}, bf16[32,1024]{1,0:T(8,128)(2,1)S(1)}, u32[]{:S(2)}, u32[]{:S(2)}) collective-permute-start(bf16[32,1024]{1,0:T(8,128)(2,1)} %get-tuple-element.17), channel_id=1, source_target_pairs={{0,8},{8,16},{16,24},{24,0},{1,9},{9,17},{17,25},{25,1},{2,10},{10... | collective-permute-start | bytes 196616 | tf_op jit(solution)/shard_map/ppermute | solution.py:458
  9.1 7.9 %collective-permute-start.3 = (bf16[32,1024]{1,0:T(8,128)(2,1)}, bf16[32,1024]{1,0:T(8,128)(2,1)S(1)}, u32[]{:S(2)}, u32[]{:S(2)}) collective-permute-start(bf16[32,1024]{1,0:T(8,128)(2,1)} %get-tuple-element.18), channel_id=1, source_target_pairs={{0,16},{8,24},{16,0},{24,8},{1,17},{9,25},{17,1},{25,9},{2,18},{10... | collective-permute-start | bytes 196616 | tf_op jit(solution)/shard_map/ppermute | solution.py:458
  11.7 5.6 %collective-permute-start.4 = (bf16[32,1024]{1,0:T(8,128)(2,1)}, bf16[32,1024]{1,0:T(8,128)(2,1)S(1)}, u32[]{:S(2)}, u32[]{:S(2)}) collective-permute-start(bf16[32,1024]{1,0:T(8,128)(2,1)} %get-tuple-element.19), channel_id=1, source_target_pairs={{0,24},{8,0},{16,8},{24,16},{1,25},{9,1},{17,9},{25,17},{2,26},{10... | collective-permute-start | bytes 196616 | tf_op jit(solution)/shard_map/ppermute | solution.py:458
  14.3 9.7 %collective-permute-start.6 = (bf16[1040,256]{1,0:T(8,128)(2,1)}, bf16[1040,256]{1,0:T(8,128)(2,1)S(1)}, u32[]{:S(2)}, u32[]{:S(2)}) collective-permute-start(bf16[1040,256]{1,0:T(8,128)(2,1)} %get-tuple-element.16), channel_id=1, source_target_pairs={{0,2},{1,5},{2,0},{3,7},{4,6},{5,1},{6,4},{7,3},{8,10},{9,13},{10,... | collective-permute-start | bytes 1597448 | tf_op jit(solution)/shard_map/ppermute | solution.py:433
  17.1 12.0 %copy-start.1 = (bf16[1,2,512,512]{3,2,1,0:T(8,128)(2,1)S(1)}, bf16[1,2,512,512]{3,2,1,0:T(8,128)(2,1)}, u32[]{:S(2)}) copy-start(bf16[1,2,512,512]{3,2,1,0:T(8,128)(2,1)} %param.10) | copy-start | bytes 3145732
  17.3 6.7 %collective-permute-start.5 = (bf16[1040,256]{1,0:T(8,128)(2,1)S(1)}, bf16[1040,256]{1,0:T(8,128)(2,1)S(1)}, u32[]{:S(2)}, u32[]{:S(2)}) collective-permute-start(bf16[1040,256]{1,0:T(8,128)(2,1)S(1)} %shard_map.88.first), channel_id=1, source_target_pairs={{0,1},{1,0},{2,3},{3,2},{4,5},{5,4},{6,7},{7,6},{8,9},{9,8},{10,11... | collective-permute-start | bytes 1597448 | tf_op jit(solution)/shard_map/ppermute | solution.py:424
  17.3 1.0 %copy-start.2 = (f32[32,1024]{1,0:T(8,128)S(1)}, f32[32,1024]{1,0:T(8,128)}, u32[]{:S(2)}) copy-start(f32[32,1024]{1,0:T(8,128)} %get-tuple-element.23.own) | copy-start | bytes 393220
  18.9 5.1 %collective-permute-start.7 = (bf16[2,32,512]{2,1,0:T(8,128)(2,1)S(1)}, bf16[2,32,512]{2,1,0:T(8,128)(2,1)S(1)}, u32[]{:S(2)}, u32[]{:S(2)}) collective-permute-start(bf16[2,32,512]{2,1,0:T(8,128)(2,1)S(1)} %get-tuple-element.24), channel_id=1, source_target_pairs={{0,4},{4,0},{1,5},{5,1},{2,6},{6,2},{3,7},{7,3},{8,12},{12,8},{9,1... | collective-permute-start | bytes 196616 | tf_op jit(solution)/shard_map/ppermute | solution.py:421
  19.5 7.4 %collective-permute-start.9 = (bf16[528,256]{1,0:T(8,128)(2,1)S(1)}, bf16[528,256]{1,0:T(8,128)(2,1)S(1)}, u32[]{:S(2)}, u32[]{:S(2)}) collective-permute-start(bf16[528,256]{1,0:T(8,128)(2,1)S(1)} %slice.4), channel_id=1, source_target_pairs={{0,2},{1,5},{2,0},{3,7},{4,6},{5,1},{6,4},{7,3},{8,10},{9,13},{10,... | collective-permute-start | bytes 811016 | tf_op jit(solution)/shard_map/ppermute | solution.py:433
  26.7 2.4 %collective-permute-start.8 = (bf16[1040,256]{1,0:T(8,128)(2,1)S(1)}, bf16[1040,256]{1,0:T(8,128)(2,1)S(1)}, u32[]{:S(2)}, u32[]{:S(2)}) collective-permute-start(bf16[1040,256]{1,0:T(8,128)(2,1)S(1)} %shard_map.92.second), channel_id=1, source_target_pairs={{0,1},{1,0},{2,3},{3,2},{4,5},{5,4},{6,7},{7,6},{8,9},{9,8},{10,11... | collective-permute-start | bytes 1597448 | tf_op jit(solution)/shard_map/ppermute | solution.py:424
  26.9 2.1 %collective-permute-start.10 = (bf16[528,256]{1,0:T(8,128)(2,1)S(1)}, bf16[528,256]{1,0:T(8,128)(2,1)S(1)}, u32[]{:S(2)}, u32[]{:S(2)}) collective-permute-start(bf16[528,256]{1,0:T(8,128)(2,1)S(1)} %collective-permute-done.9.passed), channel_id=1, source_target_pairs={{0,1},{1,0},{2,3},{3,2},{4,5},{5,4},{6,7},{7,6},{8,9},{9,8},{10,11... | collective-permute-start | bytes 811016 | tf_op jit(solution)/shard_map/ppermute | solution.py:424

commit v5 on v4

--- a/solution.py
+++ b/solution.py
@@ -458,7 +458,7 @@
         got.append(lax.ppermute(part, "latent", pairs))
 
     second = neighbours(sent_message, False)
-    first = tie(first, *got)
+    first = tie(first, got[0], own, *got[1:])
     field, rhs = pl.pallas_call(
         field_kernel,
         out_shape=(

time: 37.8 us -> 37.3 us (0.987)
    ppermute x3, waiting for transfers between devices: 2.69 us -> 1.77 us  [local(): got.append(lax.ppermute(part, 'latent', pairs))]
    ppermute x3, waiting for transfers between devices: 0.01 us -> 0.79 us  [neighbours(): return lax.ppermute(x, ('row', 'col'), pairs)]
    pallas_call x1, Pallas kernels: 8.59 us -> 8.18 us  [local(): pl.pallas_call(factor_kernel, out_shape=(jax.ShapeDtypeStruct((tall, wide...]
    pallas_call x1, Pallas kernels: 2.66 us -> 3.04 us  [local(): pl.pallas_call(early_kernel, out_shape=(block_shape, table_shape, table_s...]
  transfers between devices with their start and end apart: 11 -> 11, of which waited for: 5 -> 6; matrix products, arithmetic and copies ran while one was open for 0% -> 0% of each run, Pallas kernels for 9% -> 10%
where the time goes in v5:
time: 37.3 us
  Pallas kernels  15.6 us (42%)
  starting transfers between devices  13 us (35%)
  waiting for transfers between devices  7.03 us (19%)
  local copies, waits for them, and re-layouts  0.94 us (3%)
  between operations  0.7 us (2%)
    pallas_call x1, Pallas kernels, local(): pl.pallas_call(factor_kernel, out_shape=(jax.ShapeDtypeStruct((tall, wide...  8.18 us
    ppermute x3, starting transfers between devices, neighbours(): return lax.ppermute(x, ('row', 'col'), pairs)  6.12 us
    ppermute x3, starting transfers between devices, local(): got.append(lax.ppermute(part, 'latent', pairs))  5.51 us
    pallas_call x1, Pallas kernels, local(): pl.pallas_call(first_kernel, out_shape=[message, jax.ShapeDtypeStruct((ti...  3.82 us
    pallas_call x1, Pallas kernels, local(): pl.pallas_call(early_kernel, out_shape=(block_shape, table_shape, table_s...  3.04 us
    ppermute x1, waiting for transfers between devices, across_rows(): return lax.ppermute(x, 'row', [(0, 1), (1, 0)])  2.66 us
    ppermute x4, waiting for transfers between devices, siblings(): return lax.ppermute(x, 'col', [(i, i ^ 1) for i in range(cols)])  1.8 us
    ppermute x3, waiting for transfers between devices, local(): got.append(lax.ppermute(part, 'latent', pairs))  1.77 us
  transfers between devices with their start and end apart: 11, of which 6 were waited for; matrix products, arithmetic and copies ran while one was open for 0% of the time, Pallas kernels for 10%

profile of v5, /device:TPU:0, one launch (start us, length us, event | category | flops | bytes accessed | tf_op | source)
XLA Modules:
  0.0 37.3 jit_solution(11780941754768008624)
XLA Ops:
  0.6 0.0 copy-start.3
  0.6 3.8 %shard_map.85 = (bf16[1040,256]{1,0:T(8,128)(2,1)}, f32[32,1024]{1,0:T(8,128)}, bf16[32,1024]{1,0:T(8,128)(2,1)}, bf16[32,1024]{1,0:T(8,128)(2,1)}, bf16[32,1024]{1,0:T(8,128)(2,1)}) custom-call(s32[2]{0:T(128)} %index.5, bf16[1024,512]{1,0:T(8,128)(2,1)} %bitcast.7, bf16[32,16,1024]{2,1,0:T(8,128)(2,1)} %obs_far.1, f32[4,64]{1,0:T(4,128)} %bitcast.13, ...), custom_call_target="tpu_custom_call" | custom-call | tf_op jit(solution)/shard_map/pallas_call | solution.py:437
  4.5 0.0 copy-start
  4.5 3.0 %collective-permute-start.1 = (bf16[1040,256]{1,0:T(8,128)(2,1)}, bf16[1040,256]{1,0:T(8,128)(2,1)S(1)}, u32[]{:S(2)}, u32[]{:S(2)}) collective-permute-start(bf16[1040,256]{1,0:T(8,128)(2,1)} %get-tuple-element.16), channel_id=1, source_target_pairs={{0,4},{1,3},{2,6},{3,1},{4,0},{5,7},{6,2},{7,5},{8,12},{9,11},{10,... | collective-permute-start | bytes 1597448 | tf_op jit(solution)/shard_map/ppermute | solution.py:433
  7.5 0.0 collective-permute-start
  7.5 1.6 %collective-permute-start.2 = (bf16[32,1024]{1,0:T(8,128)(2,1)}, bf16[32,1024]{1,0:T(8,128)(2,1)S(1)}, u32[]{:S(2)}, u32[]{:S(2)}) collective-permute-start(bf16[32,1024]{1,0:T(8,128)(2,1)} %get-tuple-element.17), channel_id=1, source_target_pairs={{0,8},{8,16},{16,24},{24,0},{1,9},{9,17},{17,25},{25,1},{2,10},{10... | collective-permute-start | bytes 196616 | tf_op jit(solution)/shard_map/ppermute | solution.py:458
  9.1 2.6 %collective-permute-start.3 = (bf16[32,1024]{1,0:T(8,128)(2,1)}, bf16[32,1024]{1,0:T(8,128)(2,1)S(1)}, u32[]{:S(2)}, u32[]{:S(2)}) collective-permute-start(bf16[32,1024]{1,0:T(8,128)(2,1)} %get-tuple-element.19), channel_id=1, source_target_pairs={{0,16},{8,24},{16,0},{24,8},{1,17},{9,25},{17,1},{25,9},{2,18},{10... | collective-permute-start | bytes 196616 | tf_op jit(solution)/shard_map/ppermute | solution.py:458
  11.7 1.4 %collective-permute-start.4 = (bf16[32,1024]{1,0:T(8,128)(2,1)}, bf16[32,1024]{1,0:T(8,128)(2,1)S(1)}, u32[]{:S(2)}, u32[]{:S(2)}) collective-permute-start(bf16[32,1024]{1,0:T(8,128)(2,1)} %get-tuple-element.20), channel_id=1, source_target_pairs={{0,24},{8,0},{16,8},{24,16},{1,25},{9,1},{17,9},{25,17},{2,26},{10... | collective-permute-start | bytes 196616 | tf_op jit(solution)/shard_map/ppermute | solution.py:458
  13.0 1.2 %collective-permute-done.2.__.rest_0_ = bf16[32,1024]{1,0:T(8,128)(2,1)S(1)} collective-permute-done((bf16[32,1024]{1,0:T(8,128)(2,1)}, bf16[32,1024]{1,0:T(8,128)(2,1)S(1)}, u32[]{:S(2)}, u32[]{:S(2)}) %collective-permute-start.2) | collective-permute-done | bytes 65568 | tf_op jit(solution)/shard_map/ppermute | solution.py:458
  14.2 1.5 %collective-permute-start.6 = (bf16[1040,256]{1,0:T(8,128)(2,1)}, bf16[1040,256]{1,0:T(8,128)(2,1)S(1)}, u32[]{:S(2)}, u32[]{:S(2)}) collective-permute-start(bf16[1040,256]{1,0:T(8,128)(2,1)} %get-tuple-element.16), channel_id=1, source_target_pairs={{0,2},{1,5},{2,0},{3,7},{4,6},{5,1},{6,4},{7,3},{8,10},{9,13},{10,... | collective-permute-start | bytes 1597448 | tf_op jit(solution)/shard_map/ppermute | solution.py:433
  15.7 0.0 collective-permute-done.1._
  15.8 0.0 copy-start.2
  15.8 0.9 %copy-done.2 = f32[32,1024]{1,0:T(8,128)S(1)} copy-done((f32[32,1024]{1,0:T(8,128)S(1)}, f32[32,1024]{1,0:T(8,128)}, u32[]{:S(2)}) %copy-start.2) | copy-done | bytes 131096
  16.7 0.3 collective-permute-done.3.__.rest_1_
  17.0 0.0 copy-start.1
  17.0 0.2 collective-permute-done.4.__.rest_2_
  17.2 0.0 collective-permute-start.5
  17.2 0.0 copy-done.3
  17.2 0.6 %shard_map.91 = (f32[32,1024]{1,0:T(8,128)S(1)}, bf16[2,32,512]{2,1,0:T(8,128)(2,1)S(1)}) custom-call(s32[2]{0:T(128)S(1)} %copy-done.3, f32[32,1024]{1,0:T(8,128)S(1)} %copy-done.2, bf16[32,1024]{1,0:T(8,128)(2,1)S(1)} %collective-permute-done.2.__.rest_0_, bf16[32,1024]{1,0:T(8,128)(2,1)S(1)} %collective-permute-done.3.__.rest_1_, ...), custom_call_target="tpu_custom_call" | custom-call | tf_op jit(solution)/shard_map/pallas_call | solution.py:462
  17.8 0.8 %collective-permute-start.7 = (bf16[2,32,512]{2,1,0:T(8,128)(2,1)S(1)}, bf16[2,32,512]{2,1,0:T(8,128)(2,1)S(1)}, u32[]{:S(2)}, u32[]{:S(2)}) collective-permute-start(bf16[2,32,512]{2,1,0:T(8,128)(2,1)S(1)} %get-tuple-element.24), channel_id=1, source_target_pairs={{0,4},{4,0},{1,5},{5,1},{2,6},{6,2},{3,7},{7,3},{8,12},{12,8},{9,1... | collective-permute-start | bytes 196616 | tf_op jit(solution)/shard_map/ppermute | solution.py:421
  18.7 1.6 %collective-permute-start.9 = (bf16[528,256]{1,0:T(8,128)(2,1)S(1)}, bf16[528,256]{1,0:T(8,128)(2,1)S(1)}, u32[]{:S(2)}, u32[]{:S(2)}) collective-permute-start(bf16[528,256]{1,0:T(8,128)(2,1)S(1)} %slice.4), channel_id=1, source_target_pairs={{0,2},{1,5},{2,0},{3,7},{4,6},{5,1},{6,4},{7,3},{8,10},{9,13},{10,... | collective-permute-start | bytes 811016 | tf_op jit(solution)/shard_map/ppermute | solution.py:433
  20.2 2.7 %collective-permute-done.7.__.rhs_far = bf16[2,32,512]{2,1,0:T(8,128)(2,1)S(1)} collective-permute-done((bf16[2,32,512]{2,1,0:T(8,128)(2,1)S(1)}, bf16[2,32,512]{2,1,0:T(8,128)(2,1)S(1)}, u32[]{:S(2)}, u32[]{:S(2)}) %collective-permute-start.7) | collective-permute-done | bytes 65568 | tf_op jit(solution)/shard_map/ppermute | solution.py:421
  22.9 0.8 %collective-permute-done.6._ = bf16[1040,256]{1,0:T(8,128)(2,1)S(1)} collective-permute-done((bf16[1040,256]{1,0:T(8,128)(2,1)}, bf16[1040,256]{1,0:T(8,128)(2,1)S(1)}, u32[]{:S(2)}, u32[]{:S(2)}) %collective-permute-start.6) | collective-permute-done | bytes 532512 | tf_op jit(solution)/shard_map/ppermute | solution.py:433
  23.7 0.0 collective-permute-done.sibling
  23.7 0.0 collective-permute-done.5.first_sib
  23.7 0.0 copy-done
  23.7 3.0 %shard_map.90 = (bf16[3584,512]{1,0:T(8,128)(2,1)S(1)}, s32[28]{0:T(128)S(1)}, s32[28]{0:T(128)S(1)}) custom-call(s32[2]{0:T(128)S(1)} %copy-done.3, bf16[1024,512]{1,0:T(8,128)(2,1)S(1)} %bitcast.9, bf16[1024,512]{1,0:T(8,128)(2,1)S(1)} %collective-permute-done.sibling, bf16[1040,256]{1,0:T(8,128)(2,1)S(1)} %shard_map.89.first, ...), custom_call_target="tpu_custom_call" | custom-call | tf_op jit(solution)/shard_map/pallas_call | solution.py:477
  26.8 0.2 collective-permute-start.8
  27.0 0.0 collective-permute-done.9.passed
  27.0 0.4 collective-permute-start.10
  27.4 1.8 %collective-permute-done.10.passed_sib = bf16[528,256]{1,0:T(8,128)(2,1)S(1)} collective-permute-done((bf16[528,256]{1,0:T(8,128)(2,1)S(1)}, bf16[528,256]{1,0:T(8,128)(2,1)S(1)}, u32[]{:S(2)}, u32[]{:S(2)}) %collective-permute-start.10) | collective-permute-done | bytes 270368 | tf_op jit(solution)/shard_map/ppermute | solution.py:424
  29.1 0.0 collective-permute-done.8.second_sib
  29.2 0.0 copy-done.1
  29.2 8.2 %shard_map.94 = (f32[1024,512]{1,0:T(8,128)}, bf16[2,1024,128]{2,1,0:T(8,128)(2,1)}, f32[32,1024]{1,0:T(8,128)}) custom-call(s32[2]{0:T(128)S(1)} %copy-done.3, s32[28]{0:T(128)S(1)} %get-tuple-element.21.__.table, s32[28]{0:T(128)S(1)} %get-tuple-element.22.flip, bf16[1024,512]{1,0:T(8,128)(2,1)S(1)} %bitcast.10, ...), custom_call_target="tpu_custom_call" | custom-call | tf_op jit(solution)/shard_map/pallas_call | solution.py:492
  (7 shorter events, 0.0 us)
Async XLA Ops:
  0.6 16.6 %copy-start.3 = (s32[2]{0:T(128)S(1)}, s32[2]{0:T(128)}, u32[]{:S(2)}) copy-start(s32[2]{0:T(128)} %index.5) | copy-start | bytes 28
  4.5 19.2 %copy-start = (bf16[1,1024,512]{2,1,0:T(8,128)(2,1)S(1)}, bf16[1,1024,512]{2,1,0:T(8,128)(2,1)}, u32[]{:S(2)}) copy-start(bf16[1,1024,512]{2,1,0:T(8,128)(2,1)} %param.9) | copy-start | bytes 3145732
  4.5 11.3 %collective-permute-start.1 = (bf16[1040,256]{1,0:T(8,128)(2,1)}, bf16[1040,256]{1,0:T(8,128)(2,1)S(1)}, u32[]{:S(2)}, u32[]{:S(2)}) collective-permute-start(bf16[1040,256]{1,0:T(8,128)(2,1)} %get-tuple-element.16), channel_id=1, source_target_pairs={{0,4},{1,3},{2,6},{3,1},{4,0},{5,7},{6,2},{7,5},{8,12},{9,11},{10,... | collective-permute-start | bytes 1597448 | tf_op jit(solution)/shard_map/ppermute | solution.py:433
  7.5 16.2 %collective-permute-start = (bf16[1024,512]{1,0:T(8,128)(2,1)}, bf16[1024,512]{1,0:T(8,128)(2,1)S(1)}, u32[]{:S(2)}, u32[]{:S(2)}) collective-permute-start(bf16[1024,512]{1,0:T(8,128)(2,1)} %bitcast.8), channel_id=1, source_target_pairs={{0,1},{1,0},{2,3},{3,2},{4,5},{5,4},{6,7},{7,6},{8,9},{9,8},{10,11... | collective-permute-start | bytes 3145736 | tf_op jit(solution)/shard_map/ppermute | solution.py:424
  7.5 6.7 %collective-permute-start.2 = (bf16[32,1024]{1,0:T(8,128)(2,1)}, bf16[32,1024]{1,0:T(8,128)(2,1)S(1)}, u32[]{:S(2)}, u32[]{:S(2)}) collective-permute-start(bf16[32,1024]{1,0:T(8,128)(2,1)} %get-tuple-element.17), channel_id=1, source_target_pairs={{0,8},{8,16},{16,24},{24,0},{1,9},{9,17},{17,25},{25,1},{2,10},{10... | collective-permute-start | bytes 196616 | tf_op jit(solution)/shard_map/ppermute | solution.py:458
  9.1 7.9 %collective-permute-start.3 = (bf16[32,1024]{1,0:T(8,128)(2,1)}, bf16[32,1024]{1,0:T(8,128)(2,1)S(1)}, u32[]{:S(2)}, u32[]{:S(2)}) collective-permute-start(bf16[32,1024]{1,0:T(8,128)(2,1)} %get-tuple-element.19), channel_id=1, source_target_pairs={{0,16},{8,24},{16,0},{24,8},{1,17},{9,25},{17,1},{25,9},{2,18},{10... | collective-permute-start | bytes 196616 | tf_op jit(solution)/shard_map/ppermute | solution.py:458
  11.7 5.6 %collective-permute-start.4 = (bf16[32,1024]{1,0:T(8,128)(2,1)}, bf16[32,1024]{1,0:T(8,128)(2,1)S(1)}, u32[]{:S(2)}, u32[]{:S(2)}) collective-permute-start(bf16[32,1024]{1,0:T(8,128)(2,1)} %get-tuple-element.20), channel_id=1, source_target_pairs={{0,24},{8,0},{16,8},{24,16},{1,25},{9,1},{17,9},{25,17},{2,26},{10... | collective-permute-start | bytes 196616 | tf_op jit(solution)/shard_map/ppermute | solution.py:458
  14.2 9.5 %collective-permute-start.6 = (bf16[1040,256]{1,0:T(8,128)(2,1)}, bf16[1040,256]{1,0:T(8,128)(2,1)S(1)}, u32[]{:S(2)}, u32[]{:S(2)}) collective-permute-start(bf16[1040,256]{1,0:T(8,128)(2,1)} %get-tuple-element.16), channel_id=1, source_target_pairs={{0,2},{1,5},{2,0},{3,7},{4,6},{5,1},{6,4},{7,3},{8,10},{9,13},{10,... | collective-permute-start | bytes 1597448 | tf_op jit(solution)/shard_map/ppermute | solution.py:433
  15.8 0.9 %copy-start.2 = (f32[32,1024]{1,0:T(8,128)S(1)}, f32[32,1024]{1,0:T(8,128)}, u32[]{:S(2)}) copy-start(f32[32,1024]{1,0:T(8,128)} %get-tuple-element.18.__.own) | copy-start | bytes 393220
  17.0 12.2 %copy-start.1 = (bf16[1,2,512,512]{3,2,1,0:T(8,128)(2,1)S(1)}, bf16[1,2,512,512]{3,2,1,0:T(8,128)(2,1)}, u32[]{:S(2)}) copy-start(bf16[1,2,512,512]{3,2,1,0:T(8,128)(2,1)} %param.10) | copy-start | bytes 3145732
  17.2 6.5 %collective-permute-start.5 = (bf16[1040,256]{1,0:T(8,128)(2,1)S(1)}, bf16[1040,256]{1,0:T(8,128)(2,1)S(1)}, u32[]{:S(2)}, u32[]{:S(2)}) collective-permute-start(bf16[1040,256]{1,0:T(8,128)(2,1)S(1)} %shard_map.89.first), channel_id=1, source_target_pairs={{0,1},{1,0},{2,3},{3,2},{4,5},{5,4},{6,7},{7,6},{8,9},{9,8},{10,11... | collective-permute-start | bytes 1597448 | tf_op jit(solution)/shard_map/ppermute | solution.py:424
  17.8 5.1 %collective-permute-start.7 = (bf16[2,32,512]{2,1,0:T(8,128)(2,1)S(1)}, bf16[2,32,512]{2,1,0:T(8,128)(2,1)S(1)}, u32[]{:S(2)}, u32[]{:S(2)}) collective-permute-start(bf16[2,32,512]{2,1,0:T(8,128)(2,1)S(1)} %get-tuple-element.24), channel_id=1, source_target_pairs={{0,4},{4,0},{1,5},{5,1},{2,6},{6,2},{3,7},{7,3},{8,12},{12,8},{9,1... | collective-permute-start | bytes 196616 | tf_op jit(solution)/shard_map/ppermute | solution.py:421
  18.7 8.3 %collective-permute-start.9 = (bf16[528,256]{1,0:T(8,128)(2,1)S(1)}, bf16[528,256]{1,0:T(8,128)(2,1)S(1)}, u32[]{:S(2)}, u32[]{:S(2)}) collective-permute-start(bf16[528,256]{1,0:T(8,128)(2,1)S(1)} %slice.4), channel_id=1, source_target_pairs={{0,2},{1,5},{2,0},{3,7},{4,6},{5,1},{6,4},{7,3},{8,10},{9,13},{10,... | collective-permute-start | bytes 811016 | tf_op jit(solution)/shard_map/ppermute | solution.py:433
  26.8 2.4 %collective-permute-start.8 = (bf16[1040,256]{1,0:T(8,128)(2,1)S(1)}, bf16[1040,256]{1,0:T(8,128)(2,1)S(1)}, u32[]{:S(2)}, u32[]{:S(2)}) collective-permute-start(bf16[1040,256]{1,0:T(8,128)(2,1)S(1)} %shard_map.93.second), channel_id=1, source_target_pairs={{0,1},{1,0},{2,3},{3,2},{4,5},{5,4},{6,7},{7,6},{8,9},{9,8},{10,11... | collective-permute-start | bytes 1597448 | tf_op jit(solution)/shard_map/ppermute | solution.py:424
  27.0 2.1 %collective-permute-start.10 = (bf16[528,256]{1,0:T(8,128)(2,1)S(1)}, bf16[528,256]{1,0:T(8,128)(2,1)S(1)}, u32[]{:S(2)}, u32[]{:S(2)}) collective-permute-start(bf16[528,256]{1,0:T(8,128)(2,1)S(1)} %collective-permute-done.9.passed), channel_id=1, source_target_pairs={{0,1},{1,0},{2,3},{3,2},{4,5},{5,4},{6,7},{7,6},{8,9},{9,8},{10,11... | collective-permute-start | bytes 811016 | tf_op jit(solution)/shard_map/ppermute | solution.py:424
